TPU v7x, 256 devices: a whole 4x4x8 slice. The times are simulated.
256 devices in a mesh: prow: 8 (over z), pcol: 32 (over y, x, core).
Axes of the slice: x: 4, y: 4, z: 8, core: 2. Of those that a mesh axis runs over, the one named last changes fastest.
Arguments:
- matrix: bfloat16 [24576, 32768], P('prow', 'pcol'), may hold values from -6 to 6
- pivots: int32 [2, 128], replicated, may hold values from 0 to 24575, as said below
- col_blocks: int32 [256], replicated, may hold values from 0 to 255, each once
- lower_inv: float32 [2, 128, 128], replicated, as said below
- upper_inv: float32 [2, 128, 128], replicated, as said below
Outputs:
- updated: bfloat16 [24576, 32768], P('prow', 'pcol')
Inputs may be any that keep to these rules, and one draw needn't show every extreme that they name: pivots[k, i] is at least k * 128 + i. `col_blocks`: each column block is stored in exactly one slot. lower_inv[k] is unit lower triangular. upper_inv[k] is upper triangular with a positive diagonal.
All inputs are finite; a program needn't handle non-finite values.
Results may differ from a plain program's by a relative error of at most 0.0077.
Values may be sent and summed in bfloat16 or wider, within the bound.
No kernel may reach another device: no remote copies, remote signals or barrier semaphores. Data moves between devices by JAX's collectives and lax.ppermute only.
A program may use at most 64 MiB of HBM per device.

v0:
```python
import jax
import jax.numpy as jnp
from jax import lax
from jax.sharding import PartitionSpec as P


def broadcast(block, axis, owner):
    block = jnp.where(lax.axis_index(axis) == owner, block, jnp.zeros_like(block))
    return lax.psum(block, axis)


def compose_touched(pivots, block_size):
    panel_count = pivots.shape[0]
    firsts = jnp.arange(panel_count, dtype=jnp.int32)[:, None] * block_size
    top_pos = firsts + jnp.arange(block_size, dtype=jnp.int32)[None, :]
    positions = jnp.concatenate([top_pos, pivots], axis=1)

    def exchange_pair(column, values):
        near_pos = firsts[:, 0] + column
        far_pos = pivots[:, column]
        near_value = lax.dynamic_index_in_dim(values, column, 1, keepdims=True)
        far_value = lax.dynamic_index_in_dim(values, block_size + column, 1, keepdims=True)
        at_near = positions == near_pos[:, None]
        at_far = positions == far_pos[:, None]
        return jnp.where(at_near, far_value, jnp.where(at_far, near_value, values))

    return lax.fori_loop(0, block_size, exchange_pair, positions)


def lower_update(current, lowered, upper_zero):
    product = jnp.dot(lowered, upper_zero, preferred_element_type=jnp.float32)
    return (current.astype(jnp.float32) - product).astype(jnp.bfloat16)


def local(matrix, pivots, col_blocks, lower_inv, upper_inv):
    block_size = lower_inv.shape[-1]
    rows_here, cols_here = matrix.shape
    prow_count = lax.axis_size("prow")
    prow_index = lax.axis_index("prow")
    pcol_index = lax.axis_index("pcol")
    slots_here = cols_here // block_size
    owned = lax.dynamic_slice_in_dim(col_blocks, pcol_index * slots_here, slots_here)
    line_index = jnp.arange(rows_here, dtype=jnp.int32)
    global_rows = (
        line_index // block_size * prow_count + prow_index
    ) * block_size + line_index % block_size
    global_cols = (
        jnp.repeat(owned, block_size) * block_size
        + jnp.arange(cols_here, dtype=jnp.int32) % block_size
    )
    slot_ids = jnp.arange(col_blocks.shape[0], dtype=jnp.int32)
    touched_values = compose_touched(pivots, block_size)

    def holder_of(wanted):
        return wanted // block_size % prow_count == prow_index

    def local_of(wanted):
        return wanted // block_size // prow_count * block_size + wanted % block_size

    current = matrix
    for step_index in range(pivots.shape[0]):
        panel_current = current
        panel_first_row = step_index * block_size
        panel_target_values = touched_values[step_index]
        top_global = panel_first_row + jnp.arange(block_size, dtype=jnp.int32)
        panel_targets = jnp.concatenate([top_global, pivots[step_index]])
        panel_wanted = panel_target_values[:block_size]
        position = jnp.sum(jnp.where(col_blocks == step_index, slot_ids, 0))
        owner_col = position // slots_here
        column_start = position % slots_here * block_size
        trail_rows = (global_rows >= panel_first_row + block_size)[:, None]
        trail_cols = (global_cols >= panel_first_row + block_size)[None, :]
        members = (panel_current,)
        old_first = step_index // prow_count * block_size
        old_root = step_index % prow_count
        fetched = jnp.concatenate(
            [jnp.take(member, local_of(panel_wanted), axis=0, mode="clip") for member in members],
            axis=1,
        )
        fetched = jnp.where(holder_of(panel_wanted)[:, None], fetched, jnp.zeros_like(fetched))
        current_top = jnp.concatenate(
            [
                lax.slice_in_dim(member, old_first, old_first + block_size, axis=0)
                for member in members
            ],
            axis=1,
        )
        root_top = jnp.where(prow_index == old_root, current_top, jnp.zeros_like(current_top))
        summed_new = lax.psum(fetched, "prow").astype(jnp.float32)
        summed_old = lax.psum(root_top, "prow").astype(jnp.float32)
        panel_new_top = summed_new.astype(jnp.bfloat16)
        panel_old_top = summed_old.astype(jnp.bfloat16)
        in_top = panel_targets < panel_first_row + block_size
        source = jnp.where(
            in_top,
            panel_targets - panel_first_row,
            block_size + panel_target_values - panel_first_row,
        )
        values = jnp.take(jnp.concatenate([panel_new_top, panel_old_top], axis=0), source, axis=0)
        where_to = jnp.where(holder_of(panel_targets), local_of(panel_targets), rows_here)
        panel_current = panel_current.at[where_to].set(values, mode="drop")
        panel_cols = lax.dynamic_slice_in_dim(panel_current, column_start, block_size, 1)
        factored = jnp.dot(
            panel_cols.astype(jnp.float32), upper_inv[step_index], precision=lax.Precision.HIGHEST
        ).astype(jnp.bfloat16)
        lowered = broadcast(
            jnp.where(trail_rows, factored, jnp.zeros_like(factored)), "pcol", owner_col
        )
        written = jnp.where(trail_rows, lowered, panel_cols)
        upper_part = jnp.dot(
            lower_inv[step_index],
            panel_new_top.astype(jnp.float32),
            precision=lax.Precision.HIGHEST,
        ).astype(jnp.bfloat16)
        upper_zero = jnp.where(trail_cols, upper_part, jnp.zeros_like(upper_part))
        present = lax.dynamic_slice_in_dim(panel_current, column_start, block_size, 1)
        panel_current = lax.dynamic_update_slice_in_dim(
            panel_current, jnp.where(pcol_index == owner_col, written, present), column_start, 1
        )
        top_local = step_index // prow_count * block_size
        present_top = lax.slice_in_dim(panel_current, top_local, top_local + block_size, axis=0)
        fresh_top = jnp.where(trail_cols, upper_part, panel_new_top)
        chosen_top = jnp.where(prow_index == step_index % prow_count, fresh_top, present_top)
        panel_current = lax.dynamic_update_slice_in_dim(panel_current, chosen_top, top_local, 0)
        current = panel_current
        made_now = (lowered, upper_zero)
        current = lower_update(current, made_now[0], made_now[1])
    return current


def solution(mesh):
    in_specs = (P("prow", "pcol"), P(), P(), P(), P())
    out_specs = P("prow", "pcol")
    return jax.shard_map(local, mesh=mesh, in_specs=in_specs, out_specs=out_specs, check_vma=False)
```

profile of v0, /device:TPU:1, one launch (start us, length us, event | category | flops | bytes accessed | tf_op | source)
XLA Modules:
  0.0 478.1 jit_solution(4760430858723522362)
XLA Ops:
  6.5 6.2 %copy.40 = bf16[3072,1024]{1,0:T(8,128)(2,1)} copy(bf16[3072,1024]{1,0:T(8,128)(2,1)} %param.9) | data formatting | bytes 12582912
  12.8 0.1 iota_add_fusion
  12.8 0.1 copy.16
  12.9 0.1 copy.14
  13.1 14.5 %while.16 = (s32[]{:T(128)}, s32[2,256]{0,1:T(8,128)S(1)}, s32[2,256]{0,1:T(8,128)S(1)}, s32[2,128]{0,1:T(8,128)S(1)}, s32[]{:T(128)}, /*index=5*/s32[]{:T(128)}, s32[]{:T(128)}, s32[]{:T(128)}) while((s32[]{:T(128)}, s32[2,256]{0,1:T(8,128)S(1)}, s32[2,256]{0,1:T(8,128)S(1)}, s32[2,128]{0,1:T(8,128)S(1)}, s32[]{:T(128)}, ...), condition=%wide.region_1.2_spmd.clone, body=%wide.region_0.1_spmd.clone.sunk | while | flops 2058 | bytes 6375 | solution.py:27
  13.2 0.1 select_select_fusion.4
  13.3 0.1 select_select_fusion.4
  14.3 0.1 select_select_fusion.4
  14.4 0.1 select_select_fusion.4
  15.3 0.1 select_select_fusion.4
  15.4 0.1 select_select_fusion.4
  16.4 0.1 select_select_fusion.4
  16.6 0.1 select_select_fusion.4
  17.5 0.1 select_select_fusion.4
  17.6 0.1 select_select_fusion.4
  18.6 0.1 select_select_fusion.4
  18.7 0.1 select_select_fusion.4
  19.6 0.1 select_select_fusion.4
  19.7 0.1 select_select_fusion.4
  20.7 0.1 select_select_fusion.4
  20.9 0.1 select_select_fusion.4
  27.6 0.2 slice_reduce_fusion.1
  27.9 4.6 gather_fusion
  32.5 1.8 slice_select_fusion.3
  34.4 0.7 fusion.62
  36.9 0.2 slice_reduce_fusion
  40.2 0.1 dynamic-slice_multiply_fusion
  40.4 67.0 %all-reduce.13.cloned.1.call-done = (bf16[128,1024]{1,0:T(8,128)(2,1)}, bf16[128,1024]{1,0:T(8,128)(2,1)}) async-done(((bf16[128,1024]{1,0:T(8,128)(2,1)}, bf16[128,1024]{1,0:T(8,128)(2,1)}), (bf16[128,1024]{1,0:T(8,128)(2,1)}, bf16[128,1024]{1,0:T(8,128)(2,1)})) %all-reduce.13.cloned.1.call-update) | async-done | bytes 524304 | tf_op jit(solution)/shard_map/psum | solution.py:90
  107.3 1.1 pad_maximum_fusion
  108.4 10.2 %scatter_custom_fusion = bf16[3072,1024]{1,0:T(8,128)(2,1)} fusion(bf16[3072,1024]{1,0:T(8,128)(2,1)} %copy.40, s32[256]{0:T(256)S(1)} %bitcast.89, pred[256]{0:T(512)(128)(4,1)S(1)} %get-tuple-element.181, bf16[]{:T(256)} %constant.270.clone.2, bf16[256,1024]{1,0:T(8,128)(2,1)S(1)} %pad_maximum_fusion, s32[1024]{0:T(1024)S(1)} %pad_clamp_fusion.2), kind=kCustom, calls=%fused_computation.38 | custom fusion | flops 262144 | bytes 6820864 | tf_op jit(solution)/shard_map/scatter | solution.py:101
  118.6 2.8 fusion.7
  121.5 0.2 all-reduce.11.cloned.1.call-start
  121.7 0.1 fusion.54
  121.8 116.7 %all-reduce.7.cloned.1.call-done = bf16[3072,128]{1,0:T(8,128)(2,1)} async-done(((bf16[3072,128]{1,0:T(8,128)(2,1)}), bf16[3072,128]{1,0:T(8,128)(2,1)}) %all-reduce.7.cloned.1.call-update) | async-done | bytes 786448 | tf_op jit(solution)/shard_map/psum | solution.py:9
  238.5 3.4 fusion.12
  241.9 2.0 fusion.23
  244.0 7.5 %subtract_convert_fusion.1 = bf16[3072,1024]{1,0:T(8,128)(2,1)} fusion(bf16[3072,1024]{1,0:T(8,128)(2,1)} %get-tuple-element.192, bf16[3072,128]{1,0:T(8,128)(2,1)} %all-reduce.7.cloned.1.call-done, bf16[128,1024]{1,0:T(8,128)(2,1)S(1)} %get-tuple-element.193, pred[1024]{0:T(1024)(128)(4,1)S(1)} %get-tuple-element.191), kind=kOutput, calls=%fused_computation.17 | convolution fusion | flops 814874624 | bytes 13632512 | tf_op jit(solution)/shard_map/dot_general | solution.py:31
  251.5 4.6 gather_fusion.1
  256.2 1.7 slice_select_fusion.1
  257.8 0.8 broadcast_select_fusion
  258.8 68.6 %all-reduce.11.cloned.1.call-done = (bf16[128,1024]{1,0:T(8,128)(2,1)}, bf16[128,1024]{1,0:T(8,128)(2,1)}) async-done(((bf16[128,1024]{1,0:T(8,128)(2,1)}, bf16[128,1024]{1,0:T(8,128)(2,1)}), (bf16[128,1024]{1,0:T(8,128)(2,1)}, bf16[128,1024]{1,0:T(8,128)(2,1)})) %all-reduce.11.cloned.1.call-update) | async-done | bytes 524304 | tf_op jit(solution)/shard_map/psum | solution.py:90
  327.4 1.1 pad_maximum_fusion.1
  328.4 10.2 %scatter_custom_fusion.1 = bf16[3072,1024]{1,0:T(8,128)(2,1)} fusion(bf16[3072,1024]{1,0:T(8,128)(2,1)} %subtract_convert_fusion.1, s32[256]{0:T(256)S(1)} %bitcast.88, pred[256]{0:T(512)(128)(4,1)S(1)} %get-tuple-element.179, bf16[]{:T(256)} %constant.270.clone.2, bf16[256,1024]{1,0:T(8,128)(2,1)S(1)} %pad_maximum_fusion.1, s32[1024]{0:T(1024)S(1)} %pad_clamp_fusion), kind=kCustom, calls=%fused_computation.36 | custom fusion | flops 262144 | bytes 6820864 | tf_op jit(solution)/shard_map/scatter | solution.py:101
  338.7 2.8 fusion.9
  341.5 117.0 %all-reduce.9.cloned.1.call-done = bf16[3072,128]{1,0:T(8,128)(2,1)} async-done(((bf16[3072,128]{1,0:T(8,128)(2,1)}), bf16[3072,128]{1,0:T(8,128)(2,1)}) %all-reduce.9.cloned.1.call-update) | async-done | bytes 786448 | tf_op jit(solution)/shard_map/psum | solution.py:9
  458.5 3.4 fusion.13
  462.0 2.0 fusion.22
  464.0 7.5 %subtract_convert_fusion = bf16[3072,1024]{1,0:T(8,128)(2,1)} fusion(bf16[3072,1024]{1,0:T(8,128)(2,1)} %get-tuple-element.194, bf16[3072,128]{1,0:T(8,128)(2,1)} %all-reduce.9.cloned.1.call-done, bf16[128,1024]{1,0:T(8,128)(2,1)S(1)} %get-tuple-element.195, pred[1024]{0:T(1024)(128)(4,1)S(1)} %get-tuple-element.190), kind=kOutput, calls=%fused_computation.16 | convolution fusion | flops 814874624 | bytes 13632512 | tf_op jit(solution)/shard_map/dot_general | solution.py:31
  (409 shorter events, 8.9 us)
Async XLA Ops:
  6.5 6.3 %copy-start.2 = (s32[2,128]{1,0:T(2,128)S(1)}, s32[2,128]{1,0:T(2,128)}, u32[]{:S(2)}) copy-start(s32[2,128]{1,0:T(2,128)} %param.10) | copy-start | bytes 3076
  6.5 100.8 %all-reduce.13.cloned.1.call-start = ((), (), s32[]{:S(2)}) async-start(), calls=%async_computation.3 | async-start | bytes 1048576 | tf_op jit(solution)/shard_map/psum | solution.py:90
  12.7 21.6 %copy-start.3 = (s32[256]{0:T(256)S(1)}, s32[256]{0:T(256)}, u32[]{:S(2)}) copy-start(s32[256]{0:T(256)} %param.11) | copy-start | bytes 3076
  27.6 91.0 %copy-start.4 = (f32[2,128,128]{2,1,0:T(8,128)S(1)}, f32[2,128,128]{2,1,0:T(8,128)}, u32[]{:S(2)}) copy-start(f32[2,128,128]{2,1,0:T(8,128)} %param.13) | copy-start | bytes 393220
  34.3 204.2 %all-reduce.7.cloned.1.call-start = ((), (), s32[]{:S(2)}) async-start(), calls=%async_computation | async-start | bytes 1572864 | tf_op jit(solution)/shard_map/psum | solution.py:9
  108.4 133.6 %copy-start = (bf16[128,1024]{1,0:T(8,128)(2,1)S(1)}, bf16[128,1024]{1,0:T(8,128)(2,1)}, u32[]{:S(2)}) copy-start(bf16[128,1024]{1,0:T(8,128)(2,1)} %get-tuple-element.178) | copy-start | bytes 786436
  108.4 133.6 %copy-start.5 = (f32[2,128,128]{2,1,0:T(8,128)S(1)}, f32[2,128,128]{2,1,0:T(8,128)}, u32[]{:S(2)}) copy-start(f32[2,128,128]{2,1,0:T(8,128)} %param.12) | copy-start | bytes 393220
  121.5 205.9 %all-reduce.11.cloned.1.call-start = ((), (), s32[]{:S(2)}) async-start(), calls=%async_computation.2 | async-start | bytes 1048576 | tf_op jit(solution)/shard_map/psum | solution.py:90
  258.6 199.9 %all-reduce.9.cloned.1.call-start = ((), (), s32[]{:S(2)}) async-start(), calls=%async_computation.1 | async-start | bytes 1572864 | tf_op jit(solution)/shard_map/psum | solution.py:9
  328.4 133.5 %copy-start.1 = (bf16[128,1024]{1,0:T(8,128)(2,1)S(1)}, bf16[128,1024]{1,0:T(8,128)(2,1)}, u32[]{:S(2)}) copy-start(bf16[128,1024]{1,0:T(8,128)(2,1)} %get-tuple-element.176) | copy-start | bytes 786436
Sparse Core Ops, SparseCore 0:
  34.4 72.8 all-reduce.12
  121.6 116.8 all-reduce.6
  258.8 68.5 all-reduce.10
  341.6 116.8 all-reduce.8
where the time goes:
time: 479 us; the launch traced here: 478 us
  waiting for transfers between devices  369 us (77%)
  other arithmetic  42.7 us (9%)
  matrix products  24.8 us (5%)
  between operations  18.2 us (4%)
  local copies, waits for them, and re-layouts  17.7 us (4%)
  loops' own time  5.12 us (1%)
    psum x2, waiting for transfers between devices, broadcast(): return lax.psum(block, axis)  234 us
    psum x2, waiting for transfers between devices, local(): summed_old = lax.psum(root_top, 'prow').astype(jnp.float32)  136 us
    scatter x2, other arithmetic, local(): panel_current = panel_current.at[where_to].set(values, mode='drop')  20.5 us
    dot_general x2, matrix products, lower_update(): product = jnp.dot(lowered, upper_zero, preferred_element_type=jnp.float32)  15.1 us
  transfers between devices with their start and end apart: 4, of which 4 were waited for; matrix products, arithmetic and copies ran while one was open for 0% of the time, Pallas kernels for 0%

commit v1 on v0

v1 whole, which is shorter than its diff:
```python
import jax
import jax.numpy as jnp
from jax import lax
from jax.experimental import pallas as pl
from jax.experimental.pallas import tpu as pltpu
from jax.sharding import PartitionSpec as P

NB = 128
TOP = 2 * NB
PY, PX, CORES = 4, 4, 2
VMEM_BYTES = 50 * 1024 * 1024

BF = jnp.bfloat16
F32 = jnp.float32


def split3(x):
    high = x.astype(BF)
    rest = x - high.astype(F32)
    mid = rest.astype(BF)
    low = (rest - mid.astype(F32)).astype(BF)
    return high, mid, low


def dot(a, b):
    return jnp.dot(a, b, preferred_element_type=F32)


def dot_right(x, w):
    high, mid, low = split3(w)
    return dot(x, low) + dot(x, mid) + dot(x, high)


def dot_left(w, x):
    high, mid, low = split3(w)
    return dot(low, x) + dot(mid, x) + dot(high, x)


def local_row(rows, prow, prow_count):
    here = (rows // NB) % prow_count == prow
    return jnp.where(here & (rows >= 0), rows // (NB * prow_count) * NB + rows % NB, -1)


def fetch_kernel(prow_count, where_ref, piv_hbm, cols_hbm, a_ref, index_ref, rows_ref, own_ref, send_ref, order, piv_ref, cols_ref, slab, picked, sems, panel_sems, top_sems):
    prow, core = where_ref[0], where_ref[2]
    slots = a_ref.shape[1] // NB
    chunk_top = 3 * NB // PY
    block_rows = a_ref.shape[0] // PY
    firsts = (
        pltpu.make_async_copy(cols_hbm, cols_ref, top_sems.at[0]),
        pltpu.make_async_copy(piv_hbm, piv_ref, top_sems.at[1]),
        pltpu.make_async_copy(a_ref.at[pl.ds(0, NB), :], rows_ref.at[pl.ds(TOP, NB), :], top_sems.at[2]),
    )
    for copy in firsts:
        copy.start()
    firsts[0].wait()

    def place(t, carry):
        index_ref[1, cols_ref[t]] = t
        return carry

    lax.fori_loop(0, cols_ref.shape[0], place, 0, unroll=16)
    copies = []
    for n, (out, panel) in enumerate(((own_ref, core), (send_ref, 1 - core))):
        start = pl.multiple_of(index_ref[1, panel] % slots * NB, NB)
        for j in range(PY):
            copies.append(
                pltpu.make_async_copy(
                    a_ref.at[pl.ds(j * block_rows, block_rows), pl.ds(start, NB)],
                    out.at[j, pl.ds(chunk_top, block_rows), :],
                    panel_sems.at[n, j],
                )
            )
    for copy in copies:
        copy.start()

    def init(t, carry):
        order[t] = t
        index_ref[0, t] = -1
        return carry

    lax.fori_loop(0, TOP, init, 0, unroll=16)
    firsts[1].wait()
    for k in range(2):

        def untouched(i, carry):
            far = piv_ref[k, i]
            order[far] = far
            return carry

        lax.fori_loop(0, NB, untouched, 0, unroll=16)
    for k in range(2):

        def exchange(i, carry):
            far = piv_ref[k, i]
            near_value = order[k * NB + i]
            far_value = order[far]
            order[k * NB + i] = far_value
            order[far] = near_value
            return carry

        lax.fori_loop(0, NB, exchange, 0, unroll=16)

    def held(g):
        row = order[g]
        return (row >> 7) & (prow_count - 1) == prow, (row >> 10) * NB + (row & (NB - 1))

    def slab_copy(g, line):
        first = pl.multiple_of(line >> 4 << 4, 16)
        return pltpu.make_async_copy(a_ref.at[pl.ds(first, 16), :], slab.at[g], sems.at[g])

    def begin(g, carry):
        here, line = held(g)

        @pl.when(here)
        def _():
            slab_copy(g, line).start()

        return carry

    lax.fori_loop(0, TOP, begin, 0, unroll=8)
    picked[...] = jnp.zeros_like(picked)
    for k in range(2):

        def emit(i, carry):
            far = piv_ref[k, i]
            below = far >= TOP
            index_ref[0, jnp.where(below, order[far], TOP)] = jnp.where(below, far, -1)
            return carry

        lax.fori_loop(0, NB, emit, 0, unroll=16)
    line16 = lax.broadcasted_iota(jnp.int32, (16, a_ref.shape[1]), 0)

    def take(g, carry):
        here, line = held(g)

        @pl.when(here)
        def _():
            slab_copy(g, line).wait()
            chosen = jnp.where(line16 == (line & 15), slab[g].astype(F32), 0.0)
            picked[pl.ds(g, 1), :] = jnp.sum(chosen, axis=0, keepdims=True)

        return carry

    lax.fori_loop(0, TOP, take, 0, unroll=2)
    rows_ref[0:TOP, :] = picked[...].astype(BF)
    firsts[2].wait()
    old = rows_ref[TOP:TOP + NB, :]
    zero = jnp.zeros_like(old)
    rows_ref[TOP:TOP + NB, :] = jnp.where(prow == 0, old, zero)
    rows_ref[TOP + NB:, :] = jnp.where(prow == 1, old, zero)
    for copy in copies:
        copy.wait()
    for out, panel in ((own_ref, core), (send_ref, 1 - core)):
        start = pl.multiple_of(index_ref[1, panel] % slots * NB, NB)
        near = rows_ref[pl.ds(pl.multiple_of((1 - panel) * NB, NB), NB), pl.ds(start, NB)]
        small = jnp.concatenate([near, rows_ref[TOP:, pl.ds(start, NB)]], axis=0)
        for j in range(PY):
            out[j, 0:chunk_top, :] = small[j * chunk_top:(j + 1) * chunk_top]


def fetch(where, pivots, col_blocks, matrix, prow_count):
    rows_here, cols_here = matrix.shape
    chunk = (rows_here + 3 * NB) // PY
    smem = pl.BlockSpec(memory_space=pltpu.SMEM)
    vmem = pl.BlockSpec(memory_space=pltpu.VMEM)
    hbm = pl.BlockSpec(memory_space=pl.ANY)
    return pl.pallas_call(
        lambda *refs: fetch_kernel(prow_count, *refs),
        out_shape=(
            jax.ShapeDtypeStruct((2, 2 * TOP), jnp.int32),
            jax.ShapeDtypeStruct((2 * TOP, cols_here), BF),
            jax.ShapeDtypeStruct((PY, chunk, NB), BF),
            jax.ShapeDtypeStruct((PY, chunk, NB), BF),
        ),
        in_specs=[smem, hbm, hbm, hbm],
        out_specs=(smem, vmem, vmem, vmem),
        scratch_shapes=[
            pltpu.SMEM((rows_here * prow_count,), jnp.int32),
            pltpu.SMEM(pivots.shape, jnp.int32),
            pltpu.SMEM(col_blocks.shape, jnp.int32),
            pltpu.VMEM((TOP, 16, cols_here), BF),
            pltpu.VMEM((TOP, cols_here), F32),
            pltpu.SemaphoreType.DMA((TOP,)),
            pltpu.SemaphoreType.DMA((2, PY)),
            pltpu.SemaphoreType.DMA((3,)),
        ],
        compiler_params=pltpu.CompilerParams(vmem_limit_bytes=VMEM_BYTES),
        name="fetch",
    )(where, pivots, col_blocks, matrix)


def factor_kernel(prow_count, where_ref, index_vec, mine_ref, other_ref, lower_ref, upper_ref, out_ref, low_ref):
    prow, core = where_ref[0], where_ref[2]
    chunk = mine_ref.shape[1]
    chunk_top = 3 * NB // PY
    block_rows = chunk - chunk_top

    def panel(k, j, part):
        mine, other = mine_ref[j, part, :], other_ref[j, part, :]
        return jnp.where(core == k, mine, other)

    small = [jnp.concatenate([panel(k, j, slice(0, chunk_top)) for j in range(PY)], axis=0) for k in range(2)]
    near_mid, near_top = small[0][0:NB], small[1][0:NB]
    far = [small[0][NB:], small[1][NB:]]
    top_mid = dot_left(lower_ref[0], near_top).astype(BF)
    low_ref[...] = dot_right(near_mid, upper_ref[0]).astype(BF)
    dest = local_row(index_vec[0:1, 0:TOP], prow, prow_count)
    for j in range(PY):
        line = lax.broadcasted_iota(jnp.int32, (block_rows, TOP), 0) + j * block_rows
        hot = jnp.where(line == dest, 1.0, 0.0)
        kept = jnp.sum(hot, axis=1, keepdims=True) == 0.0
        hot = hot.astype(BF)
        raw = [
            jnp.where(kept, panel(k, j, slice(chunk_top, chunk)).astype(F32), dot(hot, far[k])) for k in range(2)
        ]
        first = dot_right(raw[0].astype(BF), upper_ref[0]).astype(BF)
        if j == 0:
            above = (lax.broadcasted_iota(jnp.int32, (block_rows, NB), 0) < NB) & (prow == 0)
            first = jnp.where(above, jnp.zeros_like(first), first)
        middle = (raw[1] - dot(first, top_mid)).astype(BF)
        second = dot_right(middle, upper_ref[1]).astype(BF)
        if j == 0:
            above = (lax.broadcasted_iota(jnp.int32, (block_rows, NB), 0) < NB) & (prow < 2)
            second = jnp.where(above, jnp.zeros_like(second), second)
        out_ref[j * block_rows:(j + 1) * block_rows, 0:NB] = first
        out_ref[j * block_rows:(j + 1) * block_rows, NB:] = second


def factor(where, index, mine, other, lower_inv, upper_inv, prow_count):
    rows_here = PY * (mine.shape[1] - 3 * NB // PY)
    smem = pl.BlockSpec(memory_space=pltpu.SMEM)
    vmem = pl.BlockSpec(memory_space=pltpu.VMEM)
    return pl.pallas_call(
        lambda *refs: factor_kernel(prow_count, *refs),
        out_shape=(jax.ShapeDtypeStruct((rows_here, TOP), BF), jax.ShapeDtypeStruct((NB, NB), BF)),
        in_specs=[smem] + [vmem] * 5,
        out_specs=(vmem, vmem),
        compiler_params=pltpu.CompilerParams(vmem_limit_bytes=VMEM_BYTES),
        name="factor",
    )(where, index, mine, other, lower_inv, upper_inv)


def update_kernel(prow_count, where_ref, index_ref, cols_ref, index_vec, rows_ref, low_ref, lower_ref, a_ref, l_ref, out_ref, right):
    step = pl.program_id(0)
    prow, pcol = where_ref[0], where_ref[1]
    block_rows, cols_here = a_ref.shape
    slots = cols_here // NB
    lanes = lambda s: slice(s * NB, (s + 1) * NB)

    @pl.when(step == 0)
    def _():
        top = dot_left(lower_ref[0], rows_ref[0:NB, :]).astype(BF)
        for s in range(slots):
            block = cols_ref[pcol * slots + s]
            right[0:NB, lanes(s)] = jnp.where(block >= 1, -top[:, lanes(s)], jnp.zeros((NB, NB), BF))
        mid = (rows_ref[NB:TOP, :].astype(F32) + dot(low_ref[...], right[0:NB, :])).astype(BF)
        low = dot_left(lower_ref[1], mid).astype(BF)
        for s in range(slots):
            block = cols_ref[pcol * slots + s]
            right[NB:TOP, lanes(s)] = jnp.where(block >= 2, -low[:, lanes(s)], jnp.zeros((NB, NB), BF))
        right[TOP:, :] = rows_ref[TOP:, :]

    line = lax.broadcasted_iota(jnp.int32, (block_rows, TOP), 0) + step * block_rows
    hot = jnp.where(line == local_row(index_vec[0:1, 0:TOP], prow, prow_count), 1.0, 0.0)
    kept = jnp.sum(hot, axis=1, keepdims=True) == 0.0
    left = jnp.concatenate([l_ref[...], hot.astype(BF)], axis=1)
    old = a_ref[...].astype(F32)
    out_ref[...] = (jnp.where(kept, old, 0.0) + dot(left, right[...])).astype(BF)

    for k in range(2):
        slot = index_ref[1, k]

        @pl.when(slot // slots == pcol)
        def _():
            start = pl.multiple_of(slot % slots * NB, NB)
            out_ref[:, pl.ds(start, NB)] = l_ref[:, k * NB:(k + 1) * NB]

    @pl.when((step == 0) & (prow == 0))
    def _():
        for s in range(slots):
            block = cols_ref[pcol * slots + s]
            out_ref[0:NB, lanes(s)] = jnp.where(block >= 1, -right[0:NB, lanes(s)], rows_ref[0:NB, lanes(s)])

    @pl.when((step == 0) & (prow == 1))
    def _():
        mid = (rows_ref[NB:TOP, :].astype(F32) + dot(low_ref[...], right[0:NB, :])).astype(BF)
        for s in range(slots):
            block = cols_ref[pcol * slots + s]
            changed = jnp.where(block == 1, mid[:, lanes(s)], -right[NB:TOP, lanes(s)])
            out_ref[0:NB, lanes(s)] = jnp.where(block == 0, low_ref[...], changed)


def update(where, index, col_blocks, rows, low, lower_inv, matrix, left, prow_count):
    rows_here, cols_here = matrix.shape
    steps = 6
    block_rows = rows_here // steps
    smem = pl.BlockSpec(memory_space=pltpu.SMEM)
    whole = lambda x: pl.BlockSpec(x.shape, lambda i: (0,) * x.ndim)
    return pl.pallas_call(
        lambda *refs: update_kernel(prow_count, *refs),
        grid=(steps,),
        out_shape=jax.ShapeDtypeStruct(matrix.shape, BF),
        in_specs=[
            smem,
            smem,
            smem,
            whole(index),
            whole(rows),
            whole(low),
            whole(lower_inv),
            pl.BlockSpec((block_rows, cols_here), lambda i: (i, 0)),
            pl.BlockSpec((block_rows, TOP), lambda i: (i, 0)),
        ],
        out_specs=pl.BlockSpec((block_rows, cols_here), lambda i: (i, 0)),
        scratch_shapes=[pltpu.VMEM((2 * TOP, cols_here), BF)],
        compiler_params=pltpu.CompilerParams(vmem_limit_bytes=VMEM_BYTES),
        name="update",
    )(where, index, col_blocks, index, rows, low, lower_inv, matrix, left)


CORE_SWAP = [(i, i ^ 1) for i in range(PY * PX * CORES)]
Y_GROUPS = [[(y * PX + x) * CORES + c for y in range(PY)] for x in range(PX) for c in range(CORES)]
X_GROUPS = [[(y * PX + x) * CORES + c for x in range(PX)] for y in range(PY) for c in range(CORES)]


def spread(x, axis, groups, count):
    x = jnp.broadcast_to(x[None], (count,) + x.shape)
    return lax.all_to_all(x, axis, 0, 0, axis_index_groups=groups)


def local(matrix, pivots, col_blocks, lower_inv, upper_inv):
    prow_count = lax.axis_size("prow")
    prow = lax.axis_index("prow")
    pcol = lax.axis_index("pcol")
    core = pcol % CORES
    where = jnp.stack([prow, pcol, core]).astype(jnp.int32)
    slots = matrix.shape[1] // NB

    index, rows, own, send = fetch(where, pivots, col_blocks, matrix, prow_count)
    rows = lax.psum(rows, "prow")

    def broadcast(own, send, index):
        owner = lax.dynamic_index_in_dim(index[1, :2], core, 0, keepdims=False) // slots
        received = lax.ppermute(send, "pcol", CORE_SWAP)
        panel = jnp.where(owner % CORES == core, own, received)
        panel = lax.all_to_all(panel, "pcol", 0, 0, axis_index_groups=Y_GROUPS)
        panel = lax.dynamic_index_in_dim(panel, owner // (CORES * PX), 0, keepdims=False)
        chunk_top = 3 * NB // PY
        small = jnp.sum(spread(panel[:chunk_top], "prow", None, prow_count), axis=0, dtype=BF)
        panel = jnp.concatenate([small, panel[chunk_top:]], axis=0)
        panel = spread(panel, "pcol", X_GROUPS, PX)
        panel = lax.dynamic_index_in_dim(panel, owner // CORES % PX, 0, keepdims=False)
        mine = spread(panel, "pcol", Y_GROUPS, PY)
        return mine, lax.ppermute(mine, "pcol", CORE_SWAP)

    mine, other = lax.cond(pivots[0, 0] >= 0, broadcast, lambda own, send, index: (own, send), own, send, index)
    left, low = factor(where, index, mine, other, lower_inv, upper_inv, prow_count)
    return update(where, index, col_blocks, rows, low, lower_inv, matrix, left, prow_count)


def solution(mesh):
    in_specs = (P("prow", "pcol"), P(), P(), P(), P())
    out_specs = P("prow", "pcol")
    return jax.shard_map(local, mesh=mesh, in_specs=in_specs, out_specs=out_specs, check_vma=False)
```

time: 479 us -> 125 us (0.26)
  waiting for transfers between devices: 369 us -> 31.8 us
  other arithmetic: 42.7 us -> 1.14 us
  Pallas kernels: 0 us -> 29.2 us
  matrix products: 24.8 us -> 0 us
  starting transfers between devices: 0.31 us -> 22.9 us
  blocking collectives: 0 us -> 14.6 us
  local copies, waits for them, and re-layouts: 17.7 us -> 5.73 us
    psum x4 -> x1, waiting for transfers between devices: 369 us -> 0.02 us  [local(): rows = lax.psum(rows, 'prow')]
    all_to_all x0 -> x3, waiting for transfers between devices: none -> 29.4 us  [the longest x2 17.3 us: spread(): return lax.all_to_all(x, axis, 0, 0, axis_index_groups=groups)]
    pallas_call x0 -> x3, Pallas kernels: none -> 29.2 us  [the longest x1 14.7 us: fetch(): pl.pallas_call(lambda *refs: fetch_kernel(prow_count, *refs), out_shape=(...]
    dot_general x6 -> x0, matrix products: 24.8 us -> none  [the longest x2 15.1 us: lower_update(): product = jnp.dot(lowered, upper_zero, preferred_element_type=jnp.float32)]
    scatter x2 -> x0, other arithmetic: 20.5 us -> none  [local(): panel_current = panel_current.at[where_to].set(values, mode='drop')]
    all_to_all x0 -> x1, blocking collectives: none -> 14.6 us  [spread(): return lax.all_to_all(x, axis, 0, 0, axis_index_groups=groups)]
    all_to_all x0 -> x3, starting transfers between devices: none -> 14.5 us  [the longest x2 11 us: spread(): return lax.all_to_all(x, axis, 0, 0, axis_index_groups=groups)]
    select_n x133 -> x1, other arithmetic: 11.1 us -> 1.01 us  [broadcast(): panel = jnp.where(owner % CORES == core, own, received)]
  transfers between devices with their start and end apart: 4 -> 6, of which waited for: 4 -> 4; matrix products, arithmetic and copies ran while one was open for 0% -> 3% of each run, Pallas kernels for 0% -> 4%
where the time goes in v1:
time: 125 us; the launch traced here: 123 us
  waiting for transfers between devices  31.8 us (25%)
  Pallas kernels  29.2 us (23%)
  starting transfers between devices  22.9 us (18%)
  blocking collectives  14.6 us (12%)
  between operations  14.2 us (11%)
  local copies, waits for them, and re-layouts  5.73 us (5%)
  loops' own time  2.89 us (2%)
    all_to_all x2, waiting for transfers between devices, spread(): return lax.all_to_all(x, axis, 0, 0, axis_index_groups=groups)  17.3 us
    pallas_call x1, Pallas kernels, fetch(): pl.pallas_call(lambda *refs: fetch_kernel(prow_count, *refs), out_shape=(...  14.7 us
    all_to_all x1, blocking collectives, spread(): return lax.all_to_all(x, axis, 0, 0, axis_index_groups=groups)  14.6 us
    all_to_all x1, waiting for transfers between devices, broadcast(): panel = lax.all_to_all(panel, 'pcol', 0, 0, axis_index_groups=Y_GROUPS)  12.1 us
    all_to_all x2, starting transfers between devices, spread(): return lax.all_to_all(x, axis, 0, 0, axis_index_groups=groups)  11 us
    pallas_call x1, Pallas kernels, update(): pl.pallas_call(lambda *refs: update_kernel(prow_count, *refs), grid=(step...  9.61 us
    ppermute x1, starting transfers between devices, broadcast(): return (mine, lax.ppermute(mine, 'pcol', CORE_SWAP))  5.08 us
    pallas_call x1, Pallas kernels, factor(): pl.pallas_call(lambda *refs: factor_kernel(prow_count, *refs), out_shape=...  4.92 us
  transfers between devices with their start and end apart: 6, of which 4 were waited for; matrix products, arithmetic and copies ran while one was open for 3% of the time, Pallas kernels for 4%

profile of v1, /device:TPU:1, one launch (start us, length us, event | category | flops | bytes accessed | tf_op | source)
XLA Modules:
  0.0 122.5 jit_solution(11614186084426375444)
XLA Ops:
  6.5 0.0 copy-start.6
  6.5 0.0 all-reduce.2.cloned.1.call-start
  6.5 0.1 pad_add_fusion.refs_0_
  6.6 0.0 copy-start.3
  6.6 0.7 copy-done.3
  7.3 0.0 copy-start.5
  7.3 0.7 copy-done.5
  8.0 14.7 %fetch.1 = (s32[2,512]{1,0:T(2,128)S(1)}, bf16[512,1024]{1,0:T(8,128)(2,1)}, bf16[4,864,128]{2,1,0:T(8,128)(2,1)}, bf16[4,864,128]{2,1,0:T(8,128)(2,1)}) custom-call(s32[3]{0:T(128)S(1)} %pad_add_fusion.refs_0_, s32[2,128]{1,0:T(2,128)S(1)} %copy-done.5, s32[256]{0:T(256)S(1)} %copy-done.3, bf16[3072,1024]{1,0:T(8,128)(2,1)} %refs_7_.1), custom_call_target="tpu_custom_call" | custom-call | tf_op jit(solution)/shard_map/fetch/pallas_call | solution.py:168
  22.7 0.0 all-reduce.2.cloned.1.call-update
  22.7 0.0 copy-done.6
  22.7 0.0 copy-start.1
  22.7 0.0 copy-start.2
  22.8 0.6 slice.16
  24.0 0.0 copy-start.4
  24.1 75.8 %conditional.1 = ((bf16[4,864,128]{2,1,0:T(8,128)(2,1)}, bf16[4,864,128]{2,1,0:T(8,128)(2,1)})) conditional(s32[]{:T(128)} %bitcast.7, (bf16[4,864,128]{2,1,0:T(8,128)(2,1)}, bf16[4,864,128]{2,1,0:T(8,128)(2,1)}) %tuple.12, (s32[2,512]{1,0:T(2,128)S(1)}, s32[]{:T(128)}, bf16[4,864,128]{2,1,0:T(8,128)(2,1)}, bf16[4,864,128]{2,1,0:T(8,128)(2,1)}) %tuple.13), branch_computations={%region_1.2_spmd, %region_2.4_spmd} | conditional | flops 970818 | bytes 21382040 | solution.py:357
  24.1 3.3 %collective-permute-start = (bf16[4,864,128]{2,1,0:T(8,128)(2,1)}, bf16[4,864,128]{2,1,0:T(8,128)(2,1)S(1)}, u32[]{:S(2)}, u32[]{:S(2)}) collective-permute-start(bf16[4,864,128]{2,1,0:T(8,128)(2,1)} %get-tuple-element.20), channel_id=1, source_target_pairs={{0,1},{1,0},{2,3},{3,2},{4,5},{5,4},{6,7},{7,6},{8,9},{9,8},{10,11... | collective-permute-start | bytes 2654216 | tf_op jit(solution)/shard_map/cond/branch_1_fun/ppermute | solution.py:345
  27.4 0.7 constant_dynamic-slice_fusion
  30.9 0.0 collective-permute-done
  30.9 1.0 broadcast_select_fusion
  31.9 3.5 %all-to-all-start = ((bf16[4,864,128]{2,1,0:T(8,128)(2,1)}), bf16[4,864,128]{2,1,0:T(8,128)(2,1)S(1)}, u32[]{:S(2)}, u32[]{:S(2)}) async-start(bf16[4,864,128]{2,1,0:T(8,128)(2,1)} %broadcast_select_fusion), calls=%async_computation | async-start | bytes 1769472 | tf_op jit(solution)/shard_map/cond/branch_1_fun/all_to_all | solution.py:347
  35.4 12.1 %all-to-all-done = bf16[4,864,128]{2,1,0:T(8,128)(2,1)S(1)} async-done(((bf16[4,864,128]{2,1,0:T(8,128)(2,1)}), bf16[4,864,128]{2,1,0:T(8,128)(2,1)S(1)}, u32[]{:S(2)}, u32[]{:S(2)}) %all-to-all-start) | async-done | bytes 884768 | tf_op jit(solution)/shard_map/cond/branch_1_fun/all_to_all | solution.py:347
  47.5 0.7 broadcast_in_dim.1
  48.2 6.9 %all-to-all-start.1 = ((bf16[8,96,128]{2,1,0:T(8,128)(2,1)}), bf16[8,96,128]{2,1,0:T(8,128)(2,1)S(1)}, u32[]{:S(2)}, u32[]{:S(2)}) async-start(bf16[8,96,128]{2,1,0:T(8,128)(2,1)} %broadcast_in_dim.1), calls=%async_computation.1 | async-start | bytes 393216 | tf_op jit(solution)/shard_map/cond/branch_1_fun/all_to_all | solution.py:329
  55.1 8.4 %all-to-all-done.1 = bf16[8,96,128]{2,1,0:T(8,128)(2,1)S(1)} async-done(((bf16[8,96,128]{2,1,0:T(8,128)(2,1)}), bf16[8,96,128]{2,1,0:T(8,128)(2,1)S(1)}, u32[]{:S(2)}, u32[]{:S(2)}) %all-to-all-start.1) | async-done | bytes 196640 | tf_op jit(solution)/shard_map/cond/branch_1_fun/all_to_all | solution.py:329
  63.6 1.0 broadcast_in_dim.2
  64.6 4.1 %all-to-all-start.2 = ((bf16[4,864,128]{2,1,0:T(8,128)(2,1)}), bf16[4,864,128]{2,1,0:T(8,128)(2,1)S(1)}, u32[]{:S(2)}, u32[]{:S(2)}) async-start(bf16[4,864,128]{2,1,0:T(8,128)(2,1)} %broadcast_in_dim.2), calls=%async_computation.2 | async-start | bytes 1769472 | tf_op jit(solution)/shard_map/cond/branch_1_fun/all_to_all | solution.py:329
  68.8 8.9 %all-to-all-done.2 = bf16[4,864,128]{2,1,0:T(8,128)(2,1)S(1)} async-done(((bf16[4,864,128]{2,1,0:T(8,128)(2,1)}), bf16[4,864,128]{2,1,0:T(8,128)(2,1)S(1)}, u32[]{:S(2)}, u32[]{:S(2)}) %all-to-all-start.2) | async-done | bytes 884768 | tf_op jit(solution)/shard_map/cond/branch_1_fun/all_to_all | solution.py:329
  77.6 0.1 broadcast_in_dim.4
  77.8 14.6 %all_to_all.16 = bf16[4,864,128]{2,1,0:T(8,128)(2,1)} all-to-all(bf16[4,864,128]{2,1,0:T(8,128)(2,1)S(1)} %broadcast_in_dim.4), channel_id=1, replica_groups={{0,8,16,24},{1,9,17,25},{2,10,18,26},{3,11,19,27},{4,12,20,28},{5,13,21..., dimensions={0} | all-to-all | bytes 1769472 | tf_op jit(solution)/shard_map/cond/branch_1_fun/all_to_all | solution.py:329
  92.4 5.1 %collective-permute-start.1 = (bf16[4,864,128]{2,1,0:T(8,128)(2,1)}, bf16[4,864,128]{2,1,0:T(8,128)(2,1)}, u32[]{:S(2)}, u32[]{:S(2)}) collective-permute-start(bf16[4,864,128]{2,1,0:T(8,128)(2,1)} %all_to_all.16), channel_id=1, source_target_pairs={{0,1},{1,0},{2,3},{3,2},{4,5},{5,4},{6,7},{7,6},{8,9},{9,8},{10,11... | collective-permute-start | bytes 2654216 | tf_op jit(solution)/shard_map/cond/branch_1_fun/ppermute | solution.py:355
  97.5 2.4 %collective-permute-done.1 = bf16[4,864,128]{2,1,0:T(8,128)(2,1)} collective-permute-done((bf16[4,864,128]{2,1,0:T(8,128)(2,1)}, bf16[4,864,128]{2,1,0:T(8,128)(2,1)}, u32[]{:S(2)}, u32[]{:S(2)}) %collective-permute-start.1) | collective-permute-done | bytes 884768 | tf_op jit(solution)/shard_map/cond/branch_1_fun/ppermute | solution.py:355
  99.9 0.0 copy-done.1
  99.9 0.0 copy-done.2
  99.9 4.9 %factor.1 = (bf16[3072,256]{1,0:T(8,128)(2,1)S(1)}, bf16[128,128]{1,0:T(8,128)(2,1)S(1)}) custom-call(s32[3]{0:T(128)S(1)} %pad_add_fusion.refs_0_, s32[2,512]{1,0:T(2,128)S(1)} %get-tuple-element.29.refs_1_.refs_3_, bf16[4,864,128]{2,1,0:T(8,128)(2,1)} %get-tuple-element.33.refs_2_, bf16[4,864,128]{2,1,0:T(8,128)(2,1)} %get-tuple-element.34.refs_3_, ...), custom_call_target="tpu_custom_call" | custom-call | tf_op jit(solution)/shard_map/factor/pallas_call | solution.py:234
  104.8 0.0 all-reduce.2.cloned.1.call-done.refs_4_
  104.8 0.0 copy-done.4
  104.8 0.0 copy-start
  104.9 1.2 copy-done
  106.1 9.6 %update.1 = bf16[3072,1024]{1,0:T(8,128)(2,1)} custom-call(s32[3]{0:T(128)S(1)} %pad_add_fusion.refs_0_, s32[2,512]{1,0:T(2,128)S(1)} %get-tuple-element.29.refs_1_.refs_3_, s32[256]{0:T(256)S(1)} %copy-done.4, s32[2,512]{1,0:T(2,128)S(1)} %get-tuple-element.29.refs_1_.refs_3_, bf16[512,1024]{1,0:T(8,128)(2,1)S(1)} %copy-done, ...), custom_call_target="tpu_custom_call" | custom-call | tf_op jit(solution)/shard_map/update/pallas_call | solution.py:300
  (6 shorter events, 0.1 us)
Async XLA Ops:
  6.5 16.2 %copy-start.6 = (s32[2,128]{1,0:T(2,128)S(1)}, s32[2,128]{1,0:T(2,128)}, u32[]{:S(2)}) copy-start(s32[2,128]{1,0:T(2,128)} %refs_1_.1) | copy-start | bytes 3076
  6.5 98.3 %all-reduce.2.cloned.1.call-start = ((), (), s32[]{:S(2)}) async-start(), calls=%async_computation.4 | async-start | bytes 2097152 | tf_op jit(solution)/shard_map/psum | solution.py:341
  6.6 0.7 copy-start.3
  7.3 0.7 copy-start.5
  22.7 77.2 %copy-start.1 = (f32[2,128,128]{2,1,0:T(8,128)S(1)}, f32[2,128,128]{2,1,0:T(8,128)}, u32[]{:S(2)}) copy-start(f32[2,128,128]{2,1,0:T(8,128)} %refs_6_.1) | copy-start | bytes 393220
  22.7 77.1 %copy-start.2 = (f32[2,128,128]{2,1,0:T(8,128)S(1)}, f32[2,128,128]{2,1,0:T(8,128)}, u32[]{:S(2)}) copy-start(f32[2,128,128]{2,1,0:T(8,128)} %refs_5_.1) | copy-start | bytes 393220
  24.0 80.8 %copy-start.4 = (s32[256]{0:T(256)S(1)}, s32[256]{0:T(256)}, u32[]{:S(2)}) copy-start(s32[256]{0:T(256)} %refs_2_.3) | copy-start | bytes 3076
  24.1 6.8 %collective-permute-start = (bf16[4,864,128]{2,1,0:T(8,128)(2,1)}, bf16[4,864,128]{2,1,0:T(8,128)(2,1)S(1)}, u32[]{:S(2)}, u32[]{:S(2)}) collective-permute-start(bf16[4,864,128]{2,1,0:T(8,128)(2,1)} %get-tuple-element.20), channel_id=1, source_target_pairs={{0,1},{1,0},{2,3},{3,2},{4,5},{5,4},{6,7},{7,6},{8,9},{9,8},{10,11... | collective-permute-start | bytes 2654216 | tf_op jit(solution)/shard_map/cond/branch_1_fun/ppermute | solution.py:345
  31.9 15.7 %all-to-all-start = ((bf16[4,864,128]{2,1,0:T(8,128)(2,1)}), bf16[4,864,128]{2,1,0:T(8,128)(2,1)S(1)}, u32[]{:S(2)}, u32[]{:S(2)}) async-start(bf16[4,864,128]{2,1,0:T(8,128)(2,1)} %broadcast_select_fusion), calls=%async_computation | async-start | bytes 1769472 | tf_op jit(solution)/shard_map/cond/branch_1_fun/all_to_all | solution.py:347
  48.2 15.3 %all-to-all-start.1 = ((bf16[8,96,128]{2,1,0:T(8,128)(2,1)}), bf16[8,96,128]{2,1,0:T(8,128)(2,1)S(1)}, u32[]{:S(2)}, u32[]{:S(2)}) async-start(bf16[8,96,128]{2,1,0:T(8,128)(2,1)} %broadcast_in_dim.1), calls=%async_computation.1 | async-start | bytes 393216 | tf_op jit(solution)/shard_map/cond/branch_1_fun/all_to_all | solution.py:329
  64.6 13.0 %all-to-all-start.2 = ((bf16[4,864,128]{2,1,0:T(8,128)(2,1)}), bf16[4,864,128]{2,1,0:T(8,128)(2,1)S(1)}, u32[]{:S(2)}, u32[]{:S(2)}) async-start(bf16[4,864,128]{2,1,0:T(8,128)(2,1)} %broadcast_in_dim.2), calls=%async_computation.2 | async-start | bytes 1769472 | tf_op jit(solution)/shard_map/cond/branch_1_fun/all_to_all | solution.py:329
  92.4 7.5 %collective-permute-start.1 = (bf16[4,864,128]{2,1,0:T(8,128)(2,1)}, bf16[4,864,128]{2,1,0:T(8,128)(2,1)}, u32[]{:S(2)}, u32[]{:S(2)}) collective-permute-start(bf16[4,864,128]{2,1,0:T(8,128)(2,1)} %all_to_all.16), channel_id=1, source_target_pairs={{0,1},{1,0},{2,3},{3,2},{4,5},{5,4},{6,7},{7,6},{8,9},{9,8},{10,11... | collective-permute-start | bytes 2654216 | tf_op jit(solution)/shard_map/cond/branch_1_fun/ppermute | solution.py:355
  104.8 1.2 %copy-start = (bf16[512,1024]{1,0:T(8,128)(2,1)S(1)}, bf16[512,1024]{1,0:T(8,128)(2,1)}, u32[]{:S(2)}) copy-start(bf16[512,1024]{1,0:T(8,128)(2,1)} %all-reduce.2.cloned.1.call-done.refs_4_) | copy-start | bytes 3145732
Sparse Core Ops, SparseCore 0:
  22.8 77.9 all-reduce.1

commit v2 on v1

v2 whole, which is shorter than its diff:
```python
import jax
import jax.numpy as jnp
from jax import lax
from jax.experimental import pallas as pl
from jax.experimental.pallas import tpu as pltpu
from jax.sharding import PartitionSpec as P

NB = 128
TOP = 2 * NB
PY, PX, CORES = 4, 4, 2
CHUNKS = PY
SMALL = 3 * NB
STEPS = 6
PLAN = 'U1 D1|U2 D2 U3 D3|U4 G1|G2|G3|G4'
VMEM_BYTES = 50 * 1024 * 1024

BF = jnp.bfloat16
F32 = jnp.float32


def split3(x):
    high = x.astype(BF)
    rest = x - high.astype(F32)
    mid = rest.astype(BF)
    low = (rest - mid.astype(F32)).astype(BF)
    return high, mid, low


def dot(a, b):
    return jnp.dot(a, b, preferred_element_type=F32)


def dot_right(x, w):
    high, mid, low = split3(w)
    return dot(x, low) + dot(x, mid) + dot(x, high)


def dot_left(w, x):
    high, mid, low = split3(w)
    return dot(low, x) + dot(mid, x) + dot(high, x)


def local_row(rows, prow, prow_count):
    here = (rows // NB) % prow_count == prow
    return jnp.where(here & (rows >= 0), rows // (NB * prow_count) * NB + rows % NB, -1)


def fetch_kernel(where_ref, piv_ref, meta_ref, a_ref, index_ref, parts_ref, own_ref, send_ref, order, held, slab, picked, old, sems, panel_sems, top_sem):
    prow, core = where_ref[0], where_ref[2]
    prow_count = parts_ref.shape[0]
    slots = a_ref.shape[1] // NB
    chunk_top = SMALL // CHUNKS
    block_rows = a_ref.shape[0] // CHUNKS
    top_part, old_part = TOP // prow_count, NB // prow_count
    old_copy = pltpu.make_async_copy(a_ref.at[pl.ds(0, NB), :], old, top_sem)
    old_copy.start()
    places = [
        jnp.sum(jnp.where(meta_ref[2:4, :] == k, meta_ref[4:6, :], 0).astype(F32)).astype(jnp.int32) for k in range(2)
    ]
    panels = []
    for n, (out, panel) in enumerate(((own_ref, core), (send_ref, 1 - core))):
        place = jnp.where(panel == 0, places[0], places[1])
        start = pl.multiple_of(place % slots * NB, NB)
        copies = [
            pltpu.make_async_copy(
                a_ref.at[pl.ds(j * block_rows, block_rows), pl.ds(start, NB)],
                out.at[j, pl.ds(chunk_top, block_rows), :],
                panel_sems.at[n, j],
            )
            for j in range(CHUNKS)
        ]
        panels.append((out, panel, start, place // slots % CORES == core, copies))

        @pl.when(panels[n][3])
        def _():
            for copy in copies:
                copy.start()

    for k in range(2):
        index_ref[TOP + k] = places[k]

    def init(t, carry):
        order[t] = t
        index_ref[t] = -1
        return carry

    lax.fori_loop(0, TOP, init, 0, unroll=TOP)

    def untouched(t, carry):
        far = piv_ref[t]
        order[far] = far
        return carry

    lax.fori_loop(0, TOP, untouched, 0, unroll=TOP)

    def exchange(t, carry):
        far = piv_ref[t]
        near_value = order[t]
        far_value = order[far]
        order[t] = far_value
        order[far] = near_value
        return carry

    lax.fori_loop(0, TOP, exchange, 0, unroll=TOP)

    def collect(g, count):
        held[count] = g
        return count + ((order[g] >> 7) & (prow_count - 1) == prow).astype(jnp.int32)

    count = lax.fori_loop(0, TOP, collect, 0, unroll=TOP)

    def line_of(n):
        row = order[held[n]]
        return (row >> 10) * NB + (row & (NB - 1))

    def slab_copy(n, line):
        first = pl.multiple_of(line >> 4 << 4, 16)
        return pltpu.make_async_copy(a_ref.at[pl.ds(first, 16), :], slab.at[n], sems.at[n])

    def begin(n, carry):
        slab_copy(n, line_of(n)).start()
        return carry

    lax.fori_loop(0, count, begin, 0)
    picked[...] = jnp.zeros_like(picked)

    def emit(t, carry):
        far = piv_ref[t]
        index_ref[jnp.where(far >= TOP, order[far], TOP + NB)] = far
        return carry

    lax.fori_loop(0, TOP, emit, 0, unroll=TOP)
    line16 = lax.broadcasted_iota(jnp.int32, (16, a_ref.shape[1]), 0)

    def take(n, carry):
        line = line_of(n)
        slab_copy(n, line).wait()
        chosen = jnp.where(line16 == (line & 15), slab[n].astype(F32), 0.0)
        picked[pl.ds(held[n], 1), :] = jnp.sum(chosen, axis=0, keepdims=True)
        return carry

    lax.fori_loop(0, count, take, 0)
    old_copy.wait()
    for q in range(prow_count):
        parts_ref[q, 0:top_part, :] = picked[q * top_part:(q + 1) * top_part, :].astype(BF)
        for k in range(2):
            first = top_part + k * old_part
            mine = old[q * old_part:(q + 1) * old_part, :]
            parts_ref[q, first:first + old_part, :] = jnp.where(prow == k, mine, jnp.zeros_like(mine))
    for out, panel, start, valid, copies in panels:

        @pl.when(valid)
        def _():
            near = picked[pl.ds(pl.multiple_of((1 - panel) * NB, NB), NB), pl.ds(start, NB)].astype(BF)
            far = old[:, pl.ds(start, NB)]
            zero = jnp.zeros_like(far)
            small = jnp.concatenate([near, jnp.where(prow == 0, far, zero), jnp.where(prow == 1, far, zero)], axis=0)
            for copy in copies:
                copy.wait()
            for j in range(CHUNKS):
                out[j, 0:chunk_top, :] = small[j * chunk_top:(j + 1) * chunk_top]

        @pl.when(jnp.logical_not(valid))
        def _():
            out[...] = jnp.zeros_like(out)


def fetch(where, meta, matrix, prow_count):
    rows_here, cols_here = matrix.shape
    chunk = (rows_here + SMALL) // CHUNKS
    part = 2 * TOP // prow_count
    smem = pl.BlockSpec(memory_space=pltpu.SMEM)
    vmem = pl.BlockSpec(memory_space=pltpu.VMEM)
    hbm = pl.BlockSpec(memory_space=pltpu.HBM)
    return pl.pallas_call(
        fetch_kernel,
        out_shape=(
            jax.ShapeDtypeStruct((2 * TOP,), jnp.int32),
            jax.ShapeDtypeStruct((prow_count, part, cols_here), BF),
            jax.ShapeDtypeStruct((CHUNKS, chunk, NB), BF),
            jax.ShapeDtypeStruct((CHUNKS, chunk, NB), BF),
        ),
        in_specs=[smem, smem, vmem, hbm],
        out_specs=(smem, vmem, vmem, vmem),
        scratch_shapes=[
            pltpu.SMEM((rows_here * prow_count,), jnp.int32),
            pltpu.SMEM((TOP + 1,), jnp.int32),
            pltpu.VMEM((TOP, 16, cols_here), BF),
            pltpu.VMEM((TOP, cols_here), F32),
            pltpu.VMEM((NB, cols_here), BF),
            pltpu.SemaphoreType.DMA((TOP,)),
            pltpu.SemaphoreType.DMA((2, CHUNKS)),
            pltpu.SemaphoreType.DMA(()),
        ],
        compiler_params=pltpu.CompilerParams(vmem_limit_bytes=VMEM_BYTES),
        name="fetch",
    )(where, meta, meta.reshape(-1, NB), matrix)


def factor_kernel(prow_count, where_ref, index_vec, mine_ref, other_ref, lower_ref, upper_ref, out_ref, low_ref):
    prow, core = where_ref[0], where_ref[2]
    chunk = mine_ref.shape[1]
    chunk_top = SMALL // CHUNKS
    block_rows = chunk - chunk_top

    def panel(k, j, part):
        mine, other = mine_ref[j, part, :], other_ref[j, part, :]
        return jnp.where(core == k, mine, other)

    small = [jnp.concatenate([panel(k, j, slice(0, chunk_top)) for j in range(CHUNKS)], axis=0) for k in range(2)]
    near_mid, near_top = small[0][0:NB], small[1][0:NB]
    far = [small[0][NB:NB + TOP], small[1][NB:NB + TOP]]
    top_mid = dot_left(lower_ref[0], near_top).astype(BF)
    low_ref[...] = dot_right(near_mid, upper_ref[0]).astype(BF)
    dest = local_row(jnp.concatenate([index_vec[0:1, :], index_vec[1:2, :]], axis=1), prow, prow_count)
    for j in range(CHUNKS):
        line = lax.broadcasted_iota(jnp.int32, (block_rows, TOP), 0) + j * block_rows
        hot = jnp.where(line == dest, 1.0, 0.0)
        kept = jnp.sum(hot, axis=1, keepdims=True) == 0.0
        hot = hot.astype(BF)
        raw = [
            jnp.where(kept, panel(k, j, slice(chunk_top, chunk)).astype(F32), dot(hot, far[k])) for k in range(2)
        ]
        first = dot_right(raw[0].astype(BF), upper_ref[0]).astype(BF)
        if j == 0:
            above = (lax.broadcasted_iota(jnp.int32, (block_rows, NB), 0) < NB) & (prow == 0)
            first = jnp.where(above, jnp.zeros_like(first), first)
        middle = (raw[1] - dot(first, top_mid)).astype(BF)
        second = dot_right(middle, upper_ref[1]).astype(BF)
        if j == 0:
            above = (lax.broadcasted_iota(jnp.int32, (block_rows, NB), 0) < NB) & (prow < 2)
            second = jnp.where(above, jnp.zeros_like(second), second)
        out_ref[j * block_rows:(j + 1) * block_rows, 0:NB] = first
        out_ref[j * block_rows:(j + 1) * block_rows, NB:] = second


def factor(where, index, mine, other, lower_inv, upper_inv, prow_count):
    rows_here = CHUNKS * (mine.shape[1] - SMALL // CHUNKS)
    smem = pl.BlockSpec(memory_space=pltpu.SMEM)
    vmem = pl.BlockSpec(memory_space=pltpu.VMEM)
    return pl.pallas_call(
        lambda *refs: factor_kernel(prow_count, *refs),
        out_shape=(jax.ShapeDtypeStruct((rows_here, TOP), BF), jax.ShapeDtypeStruct((NB, NB), BF)),
        in_specs=[smem] + [vmem] * 5,
        out_specs=(vmem, vmem),
        compiler_params=pltpu.CompilerParams(vmem_limit_bytes=VMEM_BYTES),
        name="factor",
    )(where, index.reshape(-1, NB), mine, other, lower_inv, upper_inv)


def update_kernel(prow_count, where_ref, index_ref, cols_ref, index_vec, *refs):
    parts = refs[:prow_count]
    low_ref, lower_ref, l_ref, matrix_ref, out_ref, a_ref, rows_ref, right, stages, sems, load_sems = refs[prow_count:]
    prow, pcol = where_ref[0], where_ref[1]
    steps, block_rows = STEPS, a_ref.shape[0] // STEPS
    slots = a_ref.shape[1] // NB
    lanes = lambda s: slice(s * NB, (s + 1) * NB)
    loads = []
    for step in range(steps):
        lines = pl.ds(step * block_rows, block_rows)
        loads.append(pltpu.make_async_copy(matrix_ref.at[lines, :], a_ref.at[lines, :], load_sems.at[step]))
        loads[step].start()
    top_part, old_part = TOP // prow_count, NB // prow_count
    for shift, part in enumerate(parts):
        source = lax.rem(prow + prow_count - shift, prow_count)
        rows_ref[pl.ds(pl.multiple_of(source * top_part, top_part), top_part), :] = part[0:top_part, :]
        for k in range(2):
            first = top_part + k * old_part
            line = pl.multiple_of(TOP + k * NB + source * old_part, old_part)
            right[pl.ds(line, old_part), :] = part[first:first + old_part, :]
    top = dot_left(lower_ref[0], rows_ref[0:NB, :]).astype(BF)
    for s in range(slots):
        block = cols_ref[pcol * slots + s]
        right[0:NB, lanes(s)] = jnp.where(block >= 1, -top[:, lanes(s)], jnp.zeros((NB, NB), BF))
    mid = (rows_ref[NB:TOP, :].astype(F32) + dot(low_ref[...], right[0:NB, :])).astype(BF)
    low = dot_left(lower_ref[1], mid).astype(BF)
    for s in range(slots):
        block = cols_ref[pcol * slots + s]
        right[NB:TOP, lanes(s)] = jnp.where(block >= 2, -low[:, lanes(s)], jnp.zeros((NB, NB), BF))

    dest = local_row(jnp.concatenate([index_vec[0:1, :], index_vec[1:2, :]], axis=1), prow, prow_count)
    copies = []
    for step in range(steps):
        lines = slice(step * block_rows, (step + 1) * block_rows)
        stage = stages.at[step % 2]
        if step >= 2:
            copies[step - 2].wait()
        loads[step].wait()
        line = lax.broadcasted_iota(jnp.int32, (block_rows, TOP), 0) + step * block_rows
        hot = jnp.where(line == dest, 1.0, 0.0)
        kept = jnp.sum(hot, axis=1, keepdims=True) == 0.0
        left = jnp.concatenate([l_ref[lines, :], hot.astype(BF)], axis=1)
        old = a_ref[lines, :].astype(F32)
        stage[...] = (jnp.where(kept, old, 0.0) + dot(left, right[...])).astype(BF)
        for k in range(2):
            slot = index_ref[TOP + k]

            @pl.when(slot // slots == pcol)
            def _():
                start = pl.multiple_of(slot % slots * NB, NB)
                stage[:, pl.ds(start, NB)] = l_ref[lines, k * NB:(k + 1) * NB]

        if step == 0:

            @pl.when(prow == 0)
            def _():
                for s in range(slots):
                    block = cols_ref[pcol * slots + s]
                    stage[0:NB, lanes(s)] = jnp.where(block >= 1, -right[0:NB, lanes(s)], rows_ref[0:NB, lanes(s)])

            @pl.when(prow == 1)
            def _():
                for s in range(slots):
                    block = cols_ref[pcol * slots + s]
                    changed = jnp.where(block == 1, mid[:, lanes(s)], -right[NB:TOP, lanes(s)])
                    stage[0:NB, lanes(s)] = jnp.where(block == 0, low_ref[...], changed)

        copies.append(pltpu.make_async_copy(stage, out_ref.at[pl.ds(step * block_rows, block_rows), :], sems.at[step % 2]))
        copies[step].start()
    for copy in copies[-2:]:
        copy.wait()


def update(where, index, col_blocks, parts, low, lower_inv, matrix, left, prow_count):
    rows_here, cols_here = matrix.shape
    smem = pl.BlockSpec(memory_space=pltpu.SMEM)
    vmem = pl.BlockSpec(memory_space=pltpu.VMEM)
    return pl.pallas_call(
        lambda *refs: update_kernel(prow_count, *refs),
        out_shape=jax.ShapeDtypeStruct(matrix.shape, BF),
        in_specs=[smem] * 3 + [vmem] * (1 + prow_count + 3) + [pl.BlockSpec(memory_space=pltpu.HBM)],
        out_specs=pl.BlockSpec(memory_space=pltpu.HBM),
        scratch_shapes=[
            pltpu.VMEM(matrix.shape, BF),
            pltpu.VMEM((TOP, cols_here), BF),
            pltpu.VMEM((2 * TOP, cols_here), BF),
            pltpu.VMEM((2, rows_here // STEPS, cols_here), BF),
            pltpu.SemaphoreType.DMA((2,)),
            pltpu.SemaphoreType.DMA((STEPS,)),
        ],
        compiler_params=pltpu.CompilerParams(vmem_limit_bytes=VMEM_BYTES),
        name="update",
    )(where, index, col_blocks, index.reshape(-1, NB), *parts, low, lower_inv, left, matrix)


CORE_SWAP = [(i, i ^ 1) for i in range(PY * PX * CORES)]
Y_GROUPS = [[(y * PX + x) * CORES + c for y in range(PY)] for x in range(PX) for c in range(CORES)]
X_GROUPS = [[(y * PX + x) * CORES + c for x in range(PX)] for y in range(PY) for c in range(CORES)]


def spread(x, axis, groups, count):
    x = jnp.broadcast_to(x[None], (count,) + x.shape)
    return lax.all_to_all(x, axis, 0, 0, axis_index_groups=groups)


def local(matrix, pivots, col_blocks, lower_inv, upper_inv):
    prow_count = lax.axis_size("prow")
    prow = lax.axis_index("prow")
    pcol = lax.axis_index("pcol")
    core = pcol % CORES
    where = jnp.stack([prow, pcol, core]).astype(jnp.int32)
    slots = matrix.shape[1] // NB

    top = jnp.arange(TOP, dtype=jnp.int32)
    meta = jnp.concatenate([pivots.reshape(-1), col_blocks, top, top])
    index, parts, own, send = fetch(where, meta, matrix, prow_count)
    barrier = lax.optimization_barrier
    ups = [(i, (i + 1) % prow_count) for i in range(prow_count)]
    downs = [(i, (i - 1) % prow_count) for i in range(prow_count)]

    def part_at(offset):
        return lax.dynamic_index_in_dim(parts, (prow + offset) % prow_count, 0, keepdims=False)

    def go_up(x, step):
        return lax.ppermute(x, "prow", ups) + part_at(4 - step)

    def go_down(x, step):
        x = lax.ppermute(x, "prow", downs)
        return x + part_at(step - 3) if step < 3 else x

    got = {}

    def gather_step(step):
        got[step] = lax.ppermute(got[step - 1], "prow", ups)
        if step < 4:
            got[prow_count - step] = lax.ppermute(got[(prow_count - step + 1) % prow_count], "prow", downs)

    state = {}

    def ring(names):
        for name in names.split():
            kind, step = name[0], int(name[1])
            if kind == "U":
                state["up"] = go_up(state["up"] if step > 1 else part_at(4), step)
            elif kind == "D":
                state["down"] = go_down(state["down"] if step > 1 else part_at(-3), step)
            elif kind == "G":
                if step == 1:
                    got[0] = state.pop("up") + state.pop("down")
                gather_step(step)

    def fence(panel, extra=()):
        flat, tree = jax.tree.flatten((panel, dict(got), dict(state), extra))
        panel, now, then, extra = jax.tree.unflatten(tree, barrier(flat))
        got.update(now)
        state.update(then)
        return panel, extra

    windows = PLAN.split("|")
    owner = lax.dynamic_index_in_dim(index[TOP:TOP + 2], core, 0, keepdims=False) // slots
    chip_y, chip_x = owner // (CORES * PX), owner // CORES % PX
    chunk_top = SMALL // CHUNKS
    ring(windows[0])
    panel = own + lax.ppermute(send, "pcol", CORE_SWAP)
    panel = lax.all_to_all(panel, "pcol", 0, 0, axis_index_groups=Y_GROUPS)
    ring(windows[1])
    panel, (chip_y, chip_x) = fence(panel, (chip_y, chip_x))

    panel = lax.dynamic_index_in_dim(panel, chip_y, 0, keepdims=False)
    small = jnp.sum(spread(panel[:chunk_top], "prow", None, prow_count), axis=0, dtype=BF)
    panel = jnp.concatenate([small, panel[chunk_top:]], axis=0)
    ring(windows[2])
    panel, _ = fence(panel)

    panel = spread(panel, "pcol", X_GROUPS, PX)
    ring(windows[3])
    panel, _ = fence(panel)

    panel = lax.dynamic_index_in_dim(panel, chip_x, 0, keepdims=False)
    mine = spread(panel, "pcol", Y_GROUPS, PY)
    ring(windows[4])
    mine, _ = fence(mine)
    ring(windows[5])
    other = lax.ppermute(mine, "pcol", CORE_SWAP)

    left, low = factor(where, index, mine, other, lower_inv, upper_inv, prow_count)
    return update(where, index, col_blocks, [got[s] for s in range(prow_count)], low, lower_inv, matrix, left, prow_count)


def solution(mesh):
    in_specs = (P("prow", "pcol"), P(), P(), P(), P())
    out_specs = P("prow", "pcol")
    return jax.shard_map(local, mesh=mesh, in_specs=in_specs, out_specs=out_specs, check_vma=False)
```

time: 125 us -> 105 us (0.84); the launches traced: 123 us -> 105 us
  starting transfers between devices: 22.9 us -> 43.6 us
  blocking collectives: 14.6 us -> 0 us
  between operations: 14.2 us -> 2.95 us
  Pallas kernels: 29.2 us -> 20.5 us
  loops' own time: 2.89 us -> 0 us
  other arithmetic: 1.14 us -> 3.96 us
  local copies, waits for them, and re-layouts: 5.73 us -> 3.43 us
  waiting for transfers between devices: 31.8 us -> 30.3 us
    ppermute x2 -> x16, starting transfers between devices: 8.41 us -> 26 us  [the longest x3 9.07 us: go_down(): x = lax.ppermute(x, 'prow', downs)]
    all_to_all x1 -> x0, blocking collectives: 14.6 us -> none  [spread(): return lax.all_to_all(x, axis, 0, 0, axis_index_groups=groups)]
    ppermute x2 -> x16, waiting for transfers between devices: 2.4 us -> 14.2 us  [the longest x4 6.07 us: gather_step(): got[step] = lax.ppermute(got[step - 1], 'prow', ups)]
    all_to_all x1, waiting for transfers between devices: 12.1 us -> 1.28 us  [local(): panel = lax.all_to_all(panel, 'pcol', 0, 0, axis_index_groups=Y_GROUPS)]
    pallas_call x2, Pallas kernels: 24.3 us -> 16.4 us  [the longest x1 8.28 us: update(): pl.pallas_call(lambda *refs: update_kernel(prow_count, *refs), out_shape=...]
    another operation x1 -> x0, loops' own time: 2.89 us -> none  [local(): lax.cond(pivots[0, 0] >= 0, broadcast, lambda own, send, index: (own, sen...]
    unnamed x14 -> x6, local copies, waits for them, and re-layouts: 2.6 us -> 0.01 us
    add x0 -> x5, other arithmetic: none -> 2.42 us  [the longest x1 2.31 us: local(): panel = own + lax.ppermute(send, 'pcol', CORE_SWAP)]
  transfers between devices with their start and end apart: 6 -> 20, of which waited for: 4 -> 11; matrix products, arithmetic and copies ran while one was open for 3% -> 4% of each run, Pallas kernels for 4% -> 4%
where the time goes in v2:
time: 105 us
  starting transfers between devices  43.6 us (42%)
  waiting for transfers between devices  30.3 us (29%)
  Pallas kernels  20.5 us (20%)
  other arithmetic  3.96 us (4%)
  local copies, waits for them, and re-layouts  3.43 us (3%)
  between operations  2.95 us (3%)
    all_to_all x3, waiting for transfers between devices, spread(): return lax.all_to_all(x, axis, 0, 0, axis_index_groups=groups)  14.9 us
    all_to_all x3, starting transfers between devices, spread(): return lax.all_to_all(x, axis, 0, 0, axis_index_groups=groups)  13.2 us
    ppermute x3, starting transfers between devices, go_down(): x = lax.ppermute(x, 'prow', downs)  9.07 us
    pallas_call x1, Pallas kernels, update(): pl.pallas_call(lambda *refs: update_kernel(prow_count, *refs), out_shape=...  8.28 us
    pallas_call x1, Pallas kernels, fetch(): pl.pallas_call(fetch_kernel, out_shape=(jax.ShapeDtypeStruct((2 * TOP,),...  8.09 us
    ppermute x3, starting transfers between devices, gather_step(): lax.ppermute(got[(prow_count - step + 1) % prow_count], 'prow', downs)  8.08 us
    ppermute x4, waiting for transfers between devices, gather_step(): got[step] = lax.ppermute(got[step - 1], 'prow', ups)  6.07 us
    ppermute x4, waiting for transfers between devices, go_up(): return lax.ppermute(x, 'prow', ups) + part_at(4 - step)  6.05 us
  transfers between devices with their start and end apart: 20, of which 11 were waited for; matrix products, arithmetic and copies ran while one was open for 4% of the time, Pallas kernels for 4%

profile of v2, /device:TPU:1, one launch (start us, length us, event | category | flops | bytes accessed | tf_op | source)
XLA Modules:
  0.0 104.7 jit_solution(16138485521072655330)
XLA Ops:
  0.0 0.7 pad_add_fusion.piv_ref
  0.7 0.7 pad_add_fusion.1.meta_ref
  1.4 0.1 pad_add_fusion.2.where_ref.refs_0_
  1.5 8.1 %fetch.1 = (s32[512]{0:T(512)S(1)}, bf16[8,64,1024]{2,1,0:T(8,128)(2,1)S(1)}, bf16[4,864,128]{2,1,0:T(8,128)(2,1)S(1)}, bf16[4,864,128]{2,1,0:T(8,128)(2,1)S(1)}) custom-call(s32[3]{0:T(128)S(1)} %pad_add_fusion.2.where_ref.refs_0_, s32[1024]{0:T(1024)S(1)} %pad_add_fusion.piv_ref, s32[8,128]{1,0:T(8,128)S(1)} %pad_add_fusion.1.meta_ref, ...), custom_call_target="tpu_custom_call" | custom-call | tf_op jit(solution)/shard_map/fetch/pallas_call | solution.py:175
  9.6 3.2 %collective-permute-start = (bf16[4,864,128]{2,1,0:T(8,128)(2,1)S(1)}, bf16[4,864,128]{2,1,0:T(8,128)(2,1)}, u32[]{:S(2)}, u32[]{:S(2)}) collective-permute-start(bf16[4,864,128]{2,1,0:T(8,128)(2,1)S(1)} %get-tuple-element.36), channel_id=1, source_target_pairs={{0,1},{1,0},{2,3},{3,2},{4,5},{5,4},{6,7},{7,6},{8,9},{9,8},{10,11... | collective-permute-start | bytes 2654216 | tf_op jit(solution)/shard_map/ppermute | solution.py:414
  12.8 0.1 collective-permute-start.4
  12.9 3.6 %collective-permute-start.1 = (bf16[64,1024]{1,0:T(8,128)(2,1)S(1)}, bf16[64,1024]{1,0:T(8,128)(2,1)S(1)}, u32[]{:S(2)}, u32[]{:S(2)}) collective-permute-start(bf16[64,1024]{1,0:T(8,128)(2,1)S(1)} %get-tuple-element.68), channel_id=1, source_target_pairs={{0,224},{32,0},{64,32},{96,64},{128,96},{160,128},{192,160},{224,1... | collective-permute-start | bytes 393224 | tf_op jit(solution)/shard_map/ppermute | solution.py:378
  16.5 3.7 %collective-permute-done.4 = bf16[64,1024]{1,0:T(8,128)(2,1)S(1)} collective-permute-done((bf16[64,1024]{1,0:T(8,128)(2,1)S(1)}, bf16[64,1024]{1,0:T(8,128)(2,1)S(1)}, u32[]{:S(2)}, u32[]{:S(2)}) %collective-permute-start.4) | collective-permute-done | bytes 131104 | tf_op jit(solution)/shard_map/ppermute | solution.py:375
  20.2 0.1 collective-permute-start.5
  20.3 0.0 collective-permute-done
  20.4 2.3 %add.118 = bf16[4,864,128]{2,1,0:T(8,128)(2,1)} add(bf16[4,864,128]{2,1,0:T(8,128)(2,1)S(1)} %get-tuple-element.35, bf16[4,864,128]{2,1,0:T(8,128)(2,1)} %collective-permute-done) | non-fusion elementwise | flops 442368 | bytes 2654208 | tf_op jit(solution)/shard_map/add | solution.py:414
  22.7 4.3 %all-to-all-start = ((bf16[4,864,128]{2,1,0:T(8,128)(2,1)}), bf16[4,864,128]{2,1,0:T(8,128)(2,1)S(1)}, u32[]{:S(2)}, u32[]{:S(2)}) async-start(bf16[4,864,128]{2,1,0:T(8,128)(2,1)} %add.118), calls=%async_computation | async-start | bytes 1769472 | tf_op jit(solution)/shard_map/all_to_all | solution.py:415
  27.0 0.0 collective-permute-done.1
  27.0 0.0 collective-permute-done.5
  27.0 0.1 collective-permute-start.6
  27.1 2.7 %collective-permute-start.2 = (bf16[64,1024]{1,0:T(8,128)(2,1)S(1)}, bf16[64,1024]{1,0:T(8,128)(2,1)S(1)}, u32[]{:S(2)}, u32[]{:S(2)}) collective-permute-start(bf16[64,1024]{1,0:T(8,128)(2,1)S(1)} %get-tuple-element.66), channel_id=1, source_target_pairs={{0,224},{32,0},{64,32},{96,64},{128,96},{160,128},{192,160},{224,1... | collective-permute-start | bytes 393224 | tf_op jit(solution)/shard_map/ppermute | solution.py:378
  29.8 2.3 %collective-permute-done.6 = bf16[64,1024]{1,0:T(8,128)(2,1)S(1)} collective-permute-done((bf16[64,1024]{1,0:T(8,128)(2,1)S(1)}, bf16[64,1024]{1,0:T(8,128)(2,1)S(1)}, u32[]{:S(2)}, u32[]{:S(2)}) %collective-permute-start.6) | collective-permute-done | bytes 131104 | tf_op jit(solution)/shard_map/ppermute | solution.py:375
  32.1 0.0 collective-permute-done.2
  32.2 2.8 %collective-permute-start.3 = (bf16[64,1024]{1,0:T(8,128)(2,1)S(1)}, bf16[64,1024]{1,0:T(8,128)(2,1)S(1)}, u32[]{:S(2)}, u32[]{:S(2)}) collective-permute-start(bf16[64,1024]{1,0:T(8,128)(2,1)S(1)} %get-tuple-element.64), channel_id=1, source_target_pairs={{0,224},{32,0},{64,32},{96,64},{128,96},{160,128},{192,160},{224,1... | collective-permute-start | bytes 393224 | tf_op jit(solution)/shard_map/ppermute | solution.py:378
  35.0 0.6 dynamic_slice.43
  38.2 0.0 collective-permute-done.3
  38.2 1.3 %all-to-all-done = bf16[4,864,128]{2,1,0:T(8,128)(2,1)S(1)} async-done(((bf16[4,864,128]{2,1,0:T(8,128)(2,1)}), bf16[4,864,128]{2,1,0:T(8,128)(2,1)S(1)}, u32[]{:S(2)}, u32[]{:S(2)}) %all-to-all-start) | async-done | bytes 884768 | tf_op jit(solution)/shard_map/all_to_all | solution.py:415
  39.5 0.0 collective-permute-start.7
  39.5 0.7 broadcast_in_dim.11
  40.2 5.7 %all-to-all-start.1 = ((bf16[8,96,128]{2,1,0:T(8,128)(2,1)}), bf16[8,96,128]{2,1,0:T(8,128)(2,1)S(1)}, u32[]{:S(2)}, u32[]{:S(2)}) async-start(bf16[8,96,128]{2,1,0:T(8,128)(2,1)} %broadcast_in_dim.11), calls=%async_computation.1 | async-start | bytes 393216 | tf_op jit(solution)/shard_map/all_to_all | solution.py:353
  45.8 0.0 collective-permute-done.7
  45.9 2.7 %collective-permute-start.9 = (bf16[64,1024]{1,0:T(8,128)(2,1)S(1)}, bf16[64,1024]{1,0:T(8,128)(2,1)S(1)}, u32[]{:S(2)}, u32[]{:S(2)}) collective-permute-start(bf16[64,1024]{1,0:T(8,128)(2,1)S(1)} %fusion.refs_4_), channel_id=1, source_target_pairs={{0,224},{32,0},{64,32},{96,64},{128,96},{160,128},{192,160},{224,1... | collective-permute-start | bytes 393224 | tf_op jit(solution)/shard_map/ppermute | solution.py:386
  48.6 0.0 collective-permute-start.8
  48.6 6.1 %all-to-all-done.1 = bf16[8,96,128]{2,1,0:T(8,128)(2,1)S(1)} async-done(((bf16[8,96,128]{2,1,0:T(8,128)(2,1)}), bf16[8,96,128]{2,1,0:T(8,128)(2,1)S(1)}, u32[]{:S(2)}, u32[]{:S(2)}) %all-to-all-start.1) | async-done | bytes 196640 | tf_op jit(solution)/shard_map/all_to_all | solution.py:353
  54.8 1.2 %collective-permute-done.8.refs_5_ = bf16[64,1024]{1,0:T(8,128)(2,1)S(1)} collective-permute-done((bf16[64,1024]{1,0:T(8,128)(2,1)S(1)}, bf16[64,1024]{1,0:T(8,128)(2,1)S(1)}, u32[]{:S(2)}, u32[]{:S(2)}) %collective-permute-start.8) | collective-permute-done | bytes 131104 | tf_op jit(solution)/shard_map/ppermute | solution.py:384
  56.0 1.0 broadcast_in_dim.24
  57.0 4.0 %all-to-all-start.2 = ((bf16[4,864,128]{2,1,0:T(8,128)(2,1)}), bf16[4,864,128]{2,1,0:T(8,128)(2,1)S(1)}, u32[]{:S(2)}, u32[]{:S(2)}) async-start(bf16[4,864,128]{2,1,0:T(8,128)(2,1)} %broadcast_in_dim.24), calls=%async_computation.2 | async-start | bytes 1769472 | tf_op jit(solution)/shard_map/all_to_all | solution.py:353
  61.0 0.0 collective-permute-start.10
  61.0 2.7 %collective-permute-start.11 = (bf16[64,1024]{1,0:T(8,128)(2,1)S(1)}, bf16[64,1024]{1,0:T(8,128)(2,1)S(1)}, u32[]{:S(2)}, u32[]{:S(2)}) collective-permute-start(bf16[64,1024]{1,0:T(8,128)(2,1)S(1)} %collective-permute-done.9.refs_11_), channel_id=1, source_target_pairs={{0,224},{32,0},{64,32},{96,64},{128,96},{160,128},{192,160},{224,1... | collective-permute-start | bytes 393224 | tf_op jit(solution)/shard_map/ppermute | solution.py:386
  63.7 2.4 %collective-permute-done.10.refs_6_ = bf16[64,1024]{1,0:T(8,128)(2,1)S(1)} collective-permute-done((bf16[64,1024]{1,0:T(8,128)(2,1)S(1)}, bf16[64,1024]{1,0:T(8,128)(2,1)S(1)}, u32[]{:S(2)}, u32[]{:S(2)}) %collective-permute-start.10) | collective-permute-done | bytes 131104 | tf_op jit(solution)/shard_map/ppermute | solution.py:384
  66.0 5.0 %all-to-all-done.2 = bf16[4,864,128]{2,1,0:T(8,128)(2,1)S(1)} async-done(((bf16[4,864,128]{2,1,0:T(8,128)(2,1)}), bf16[4,864,128]{2,1,0:T(8,128)(2,1)S(1)}, u32[]{:S(2)}, u32[]{:S(2)}) %all-to-all-start.2) | async-done | bytes 884768 | tf_op jit(solution)/shard_map/all_to_all | solution.py:353
  71.1 1.0 broadcast_in_dim.26
  72.1 3.5 %all-to-all-start.3 = ((bf16[4,864,128]{2,1,0:T(8,128)(2,1)}), bf16[4,864,128]{2,1,0:T(8,128)(2,1)S(1)}, u32[]{:S(2)}, u32[]{:S(2)}) async-start(bf16[4,864,128]{2,1,0:T(8,128)(2,1)} %broadcast_in_dim.26), calls=%async_computation.3 | async-start | bytes 1769472 | tf_op jit(solution)/shard_map/all_to_all | solution.py:353
  75.7 0.1 collective-permute-start.12
  75.7 2.7 %collective-permute-start.13 = (bf16[64,1024]{1,0:T(8,128)(2,1)S(1)}, bf16[64,1024]{1,0:T(8,128)(2,1)S(1)}, u32[]{:S(2)}, u32[]{:S(2)}) collective-permute-start(bf16[64,1024]{1,0:T(8,128)(2,1)S(1)} %collective-permute-done.11.refs_10_), channel_id=1, source_target_pairs={{0,224},{32,0},{64,32},{96,64},{128,96},{160,128},{192,160},{224,1... | collective-permute-start | bytes 393224 | tf_op jit(solution)/shard_map/ppermute | solution.py:386
  78.4 2.4 %collective-permute-done.12.refs_7_ = bf16[64,1024]{1,0:T(8,128)(2,1)S(1)} collective-permute-done((bf16[64,1024]{1,0:T(8,128)(2,1)S(1)}, bf16[64,1024]{1,0:T(8,128)(2,1)S(1)}, u32[]{:S(2)}, u32[]{:S(2)}) %collective-permute-start.12) | collective-permute-done | bytes 131104 | tf_op jit(solution)/shard_map/ppermute | solution.py:384
  80.8 0.0 collective-permute-done.13.refs_9_
  80.8 3.8 %all-to-all-done.3.refs_2_ = bf16[4,864,128]{2,1,0:T(8,128)(2,1)S(1)} async-done(((bf16[4,864,128]{2,1,0:T(8,128)(2,1)}), bf16[4,864,128]{2,1,0:T(8,128)(2,1)S(1)}, u32[]{:S(2)}, u32[]{:S(2)}) %all-to-all-start.3) | async-done | bytes 884768 | tf_op jit(solution)/shard_map/all_to_all | solution.py:353
  84.5 5.4 %collective-permute-start.15 = (bf16[4,864,128]{2,1,0:T(8,128)(2,1)S(1)}, bf16[4,864,128]{2,1,0:T(8,128)(2,1)S(1)}, u32[]{:S(2)}, u32[]{:S(2)}) collective-permute-start(bf16[4,864,128]{2,1,0:T(8,128)(2,1)S(1)} %all-to-all-done.3.refs_2_), channel_id=1, source_target_pairs={{0,1},{1,0},{2,3},{3,2},{4,5},{5,4},{6,7},{7,6},{8,9},{9,8},{10,11... | collective-permute-start | bytes 2654216 | tf_op jit(solution)/shard_map/ppermute | solution.py:434
  89.9 2.0 %collective-permute-done.15.refs_3_ = bf16[4,864,128]{2,1,0:T(8,128)(2,1)S(1)} collective-permute-done((bf16[4,864,128]{2,1,0:T(8,128)(2,1)S(1)}, bf16[4,864,128]{2,1,0:T(8,128)(2,1)S(1)}, u32[]{:S(2)}, u32[]{:S(2)}) %collective-permute-start.15) | collective-permute-done | bytes 884768 | tf_op jit(solution)/shard_map/ppermute | solution.py:434
  92.0 4.1 %factor.1 = (bf16[3072,256]{1,0:T(8,128)(2,1)S(1)}, bf16[128,128]{1,0:T(8,128)(2,1)S(1)}) custom-call(s32[3]{0:T(128)S(1)} %pad_add_fusion.2.where_ref.refs_0_, s32[4,128]{1,0:T(4,128)S(1)} %bitcast.31, bf16[4,864,128]{2,1,0:T(8,128)(2,1)S(1)} %all-to-all-done.3.refs_2_, bf16[4,864,128]{2,1,0:T(8,128)(2,1)S(1)} %collective-permute-done.15.refs_3_, ...), custom_call_target="tpu_custom_call" | custom-call | tf_op jit(solution)/shard_map/factor/pallas_call | solution.py:241
  96.1 0.2 collective-permute-done.14.refs_8_
  96.3 8.3 %update.1 = bf16[3072,1024]{1,0:T(8,128)(2,1)} custom-call(s32[3]{0:T(128)S(1)} %pad_add_fusion.2.where_ref.refs_0_, s32[512]{0:T(512)S(1)} %get-tuple-element.34.refs_1_, s32[256]{0:T(256)S(1)} %copy-done.2, s32[4,128]{1,0:T(4,128)S(1)} %bitcast.32, bf16[64,1024]{1,0:T(8,128)(2,1)S(1)} %fusion.refs_4_, bf16[64,1024]{1,0:T(8,128)(2,1)S(1)} %collective-permute-done.8.refs_5_, ...), custom_call_target="tpu_custom_call" | custom-call | tf_op jit(solution)/shard_map/update/pallas_call | solution.py:328
  (22 shorter events, 0.2 us)
Async XLA Ops:
  9.6 10.8 %collective-permute-start = (bf16[4,864,128]{2,1,0:T(8,128)(2,1)S(1)}, bf16[4,864,128]{2,1,0:T(8,128)(2,1)}, u32[]{:S(2)}, u32[]{:S(2)}) collective-permute-start(bf16[4,864,128]{2,1,0:T(8,128)(2,1)S(1)} %get-tuple-element.36), channel_id=1, source_target_pairs={{0,1},{1,0},{2,3},{3,2},{4,5},{5,4},{6,7},{7,6},{8,9},{9,8},{10,11... | collective-permute-start | bytes 2654216 | tf_op jit(solution)/shard_map/ppermute | solution.py:414
  12.8 7.4 %collective-permute-start.4 = (bf16[64,1024]{1,0:T(8,128)(2,1)S(1)}, bf16[64,1024]{1,0:T(8,128)(2,1)S(1)}, u32[]{:S(2)}, u32[]{:S(2)}) collective-permute-start(bf16[64,1024]{1,0:T(8,128)(2,1)S(1)} %get-tuple-element.67), channel_id=1, source_target_pairs={{0,32},{32,64},{64,96},{96,128},{128,160},{160,192},{192,224},{224... | collective-permute-start | bytes 393224 | tf_op jit(solution)/shard_map/ppermute | solution.py:375
  12.9 14.1 %collective-permute-start.1 = (bf16[64,1024]{1,0:T(8,128)(2,1)S(1)}, bf16[64,1024]{1,0:T(8,128)(2,1)S(1)}, u32[]{:S(2)}, u32[]{:S(2)}) collective-permute-start(bf16[64,1024]{1,0:T(8,128)(2,1)S(1)} %get-tuple-element.68), channel_id=1, source_target_pairs={{0,224},{32,0},{64,32},{96,64},{128,96},{160,128},{192,160},{224,1... | collective-permute-start | bytes 393224 | tf_op jit(solution)/shard_map/ppermute | solution.py:378
  20.2 6.8 %collective-permute-start.5 = (bf16[64,1024]{1,0:T(8,128)(2,1)S(1)}, bf16[64,1024]{1,0:T(8,128)(2,1)S(1)}, u32[]{:S(2)}, u32[]{:S(2)}) collective-permute-start(bf16[64,1024]{1,0:T(8,128)(2,1)S(1)} %bitcast_add_fusion.3), channel_id=1, source_target_pairs={{0,32},{32,64},{64,96},{96,128},{128,160},{160,192},{192,224},{224... | collective-permute-start | bytes 393224 | tf_op jit(solution)/shard_map/ppermute | solution.py:375
  22.7 69.3 %copy-start = (f32[2,128,128]{2,1,0:T(8,128)S(1)}, f32[2,128,128]{2,1,0:T(8,128)}, u32[]{:S(2)}) copy-start(f32[2,128,128]{2,1,0:T(8,128)} %refs_13_.1) | copy-start | bytes 393220
  22.7 69.3 %copy-start.1 = (f32[2,128,128]{2,1,0:T(8,128)S(1)}, f32[2,128,128]{2,1,0:T(8,128)}, u32[]{:S(2)}) copy-start(f32[2,128,128]{2,1,0:T(8,128)} %refs_5_.1) | copy-start | bytes 393220
  22.7 16.8 %all-to-all-start = ((bf16[4,864,128]{2,1,0:T(8,128)(2,1)}), bf16[4,864,128]{2,1,0:T(8,128)(2,1)S(1)}, u32[]{:S(2)}, u32[]{:S(2)}) async-start(bf16[4,864,128]{2,1,0:T(8,128)(2,1)} %add.118), calls=%async_computation | async-start | bytes 1769472 | tf_op jit(solution)/shard_map/all_to_all | solution.py:415
  27.0 69.3 %copy-start.2 = (s32[256]{0:T(256)S(1)}, s32[256]{0:T(256)}, u32[]{:S(2)}) copy-start(s32[256]{0:T(256)} %refs_2_.1) | copy-start | bytes 3076
  27.0 5.1 %collective-permute-start.6 = (bf16[64,1024]{1,0:T(8,128)(2,1)S(1)}, bf16[64,1024]{1,0:T(8,128)(2,1)S(1)}, u32[]{:S(2)}, u32[]{:S(2)}) collective-permute-start(bf16[64,1024]{1,0:T(8,128)(2,1)S(1)} %get-tuple-element.65), channel_id=1, source_target_pairs={{0,32},{32,64},{64,96},{96,128},{128,160},{160,192},{192,224},{224... | collective-permute-start | bytes 393224 | tf_op jit(solution)/shard_map/ppermute | solution.py:375
  27.1 5.0 %collective-permute-start.2 = (bf16[64,1024]{1,0:T(8,128)(2,1)S(1)}, bf16[64,1024]{1,0:T(8,128)(2,1)S(1)}, u32[]{:S(2)}, u32[]{:S(2)}) collective-permute-start(bf16[64,1024]{1,0:T(8,128)(2,1)S(1)} %get-tuple-element.66), channel_id=1, source_target_pairs={{0,224},{32,0},{64,32},{96,64},{128,96},{160,128},{192,160},{224,1... | collective-permute-start | bytes 393224 | tf_op jit(solution)/shard_map/ppermute | solution.py:378
  32.2 6.0 %collective-permute-start.3 = (bf16[64,1024]{1,0:T(8,128)(2,1)S(1)}, bf16[64,1024]{1,0:T(8,128)(2,1)S(1)}, u32[]{:S(2)}, u32[]{:S(2)}) collective-permute-start(bf16[64,1024]{1,0:T(8,128)(2,1)S(1)} %get-tuple-element.64), channel_id=1, source_target_pairs={{0,224},{32,0},{64,32},{96,64},{128,96},{160,128},{192,160},{224,1... | collective-permute-start | bytes 393224 | tf_op jit(solution)/shard_map/ppermute | solution.py:378
  39.5 6.4 %collective-permute-start.7 = (bf16[64,1024]{1,0:T(8,128)(2,1)S(1)}, bf16[64,1024]{1,0:T(8,128)(2,1)S(1)}, u32[]{:S(2)}, u32[]{:S(2)}) collective-permute-start(bf16[64,1024]{1,0:T(8,128)(2,1)S(1)} %get-tuple-element.40), channel_id=1, source_target_pairs={{0,32},{32,64},{64,96},{96,128},{128,160},{160,192},{192,224},{224... | collective-permute-start | bytes 393224 | tf_op jit(solution)/shard_map/ppermute | solution.py:375
  40.2 14.5 %all-to-all-start.1 = ((bf16[8,96,128]{2,1,0:T(8,128)(2,1)}), bf16[8,96,128]{2,1,0:T(8,128)(2,1)S(1)}, u32[]{:S(2)}, u32[]{:S(2)}) async-start(bf16[8,96,128]{2,1,0:T(8,128)(2,1)} %broadcast_in_dim.11), calls=%async_computation.1 | async-start | bytes 393216 | tf_op jit(solution)/shard_map/all_to_all | solution.py:353
  45.9 8.9 %collective-permute-start.9 = (bf16[64,1024]{1,0:T(8,128)(2,1)S(1)}, bf16[64,1024]{1,0:T(8,128)(2,1)S(1)}, u32[]{:S(2)}, u32[]{:S(2)}) collective-permute-start(bf16[64,1024]{1,0:T(8,128)(2,1)S(1)} %fusion.refs_4_), channel_id=1, source_target_pairs={{0,224},{32,0},{64,32},{96,64},{128,96},{160,128},{192,160},{224,1... | collective-permute-start | bytes 393224 | tf_op jit(solution)/shard_map/ppermute | solution.py:386
  48.6 7.3 %collective-permute-start.8 = (bf16[64,1024]{1,0:T(8,128)(2,1)S(1)}, bf16[64,1024]{1,0:T(8,128)(2,1)S(1)}, u32[]{:S(2)}, u32[]{:S(2)}) collective-permute-start(bf16[64,1024]{1,0:T(8,128)(2,1)S(1)} %fusion.refs_4_), channel_id=1, source_target_pairs={{0,32},{32,64},{64,96},{96,128},{128,160},{160,192},{192,224},{224... | collective-permute-start | bytes 393224 | tf_op jit(solution)/shard_map/ppermute | solution.py:384
  57.0 14.1 %all-to-all-start.2 = ((bf16[4,864,128]{2,1,0:T(8,128)(2,1)}), bf16[4,864,128]{2,1,0:T(8,128)(2,1)S(1)}, u32[]{:S(2)}, u32[]{:S(2)}) async-start(bf16[4,864,128]{2,1,0:T(8,128)(2,1)} %broadcast_in_dim.24), calls=%async_computation.2 | async-start | bytes 1769472 | tf_op jit(solution)/shard_map/all_to_all | solution.py:353
  61.0 5.0 %collective-permute-start.10 = (bf16[64,1024]{1,0:T(8,128)(2,1)S(1)}, bf16[64,1024]{1,0:T(8,128)(2,1)S(1)}, u32[]{:S(2)}, u32[]{:S(2)}) collective-permute-start(bf16[64,1024]{1,0:T(8,128)(2,1)S(1)} %collective-permute-done.8.refs_5_), channel_id=1, source_target_pairs={{0,32},{32,64},{64,96},{96,128},{128,160},{160,192},{192,224},{224... | collective-permute-start | bytes 393224 | tf_op jit(solution)/shard_map/ppermute | solution.py:384
  61.0 5.0 %collective-permute-start.11 = (bf16[64,1024]{1,0:T(8,128)(2,1)S(1)}, bf16[64,1024]{1,0:T(8,128)(2,1)S(1)}, u32[]{:S(2)}, u32[]{:S(2)}) collective-permute-start(bf16[64,1024]{1,0:T(8,128)(2,1)S(1)} %collective-permute-done.9.refs_11_), channel_id=1, source_target_pairs={{0,224},{32,0},{64,32},{96,64},{128,96},{160,128},{192,160},{224,1... | collective-permute-start | bytes 393224 | tf_op jit(solution)/shard_map/ppermute | solution.py:386
  72.1 12.4 %all-to-all-start.3 = ((bf16[4,864,128]{2,1,0:T(8,128)(2,1)}), bf16[4,864,128]{2,1,0:T(8,128)(2,1)S(1)}, u32[]{:S(2)}, u32[]{:S(2)}) async-start(bf16[4,864,128]{2,1,0:T(8,128)(2,1)} %broadcast_in_dim.26), calls=%async_computation.3 | async-start | bytes 1769472 | tf_op jit(solution)/shard_map/all_to_all | solution.py:353
  75.7 5.1 %collective-permute-start.12 = (bf16[64,1024]{1,0:T(8,128)(2,1)S(1)}, bf16[64,1024]{1,0:T(8,128)(2,1)S(1)}, u32[]{:S(2)}, u32[]{:S(2)}) collective-permute-start(bf16[64,1024]{1,0:T(8,128)(2,1)S(1)} %collective-permute-done.10.refs_6_), channel_id=1, source_target_pairs={{0,32},{32,64},{64,96},{96,128},{128,160},{160,192},{192,224},{224... | collective-permute-start | bytes 393224 | tf_op jit(solution)/shard_map/ppermute | solution.py:384
  75.7 5.0 %collective-permute-start.13 = (bf16[64,1024]{1,0:T(8,128)(2,1)S(1)}, bf16[64,1024]{1,0:T(8,128)(2,1)S(1)}, u32[]{:S(2)}, u32[]{:S(2)}) collective-permute-start(bf16[64,1024]{1,0:T(8,128)(2,1)S(1)} %collective-permute-done.11.refs_10_), channel_id=1, source_target_pairs={{0,224},{32,0},{64,32},{96,64},{128,96},{160,128},{192,160},{224,1... | collective-permute-start | bytes 393224 | tf_op jit(solution)/shard_map/ppermute | solution.py:386
  84.5 7.4 %collective-permute-start.15 = (bf16[4,864,128]{2,1,0:T(8,128)(2,1)S(1)}, bf16[4,864,128]{2,1,0:T(8,128)(2,1)S(1)}, u32[]{:S(2)}, u32[]{:S(2)}) collective-permute-start(bf16[4,864,128]{2,1,0:T(8,128)(2,1)S(1)} %all-to-all-done.3.refs_2_), channel_id=1, source_target_pairs={{0,1},{1,0},{2,3},{3,2},{4,5},{5,4},{6,7},{7,6},{8,9},{9,8},{10,11... | collective-permute-start | bytes 2654216 | tf_op jit(solution)/shard_map/ppermute | solution.py:434
  89.9 6.3 %collective-permute-start.14 = (bf16[64,1024]{1,0:T(8,128)(2,1)S(1)}, bf16[64,1024]{1,0:T(8,128)(2,1)S(1)}, u32[]{:S(2)}, u32[]{:S(2)}) collective-permute-start(bf16[64,1024]{1,0:T(8,128)(2,1)S(1)} %collective-permute-done.12.refs_7_), channel_id=1, source_target_pairs={{0,32},{32,64},{64,96},{96,128},{128,160},{160,192},{192,224},{224... | collective-permute-start | bytes 393224 | tf_op jit(solution)/shard_map/ppermute | solution.py:384

commit v3 on v2

--- a/solution.py
+++ b/solution.py
@@ -8,10 +8,10 @@
 NB = 128
 TOP = 2 * NB
 PY, PX, CORES = 4, 4, 2
-CHUNKS = PY
-SMALL = 3 * NB
+CHUNKS = PY * PX
+SMALL = 4 * NB
 STEPS = 6
-PLAN = 'U1 D1|U2 D2 U3 D3|U4 G1|G2|G3|G4'
+PLAN = ("U1 D1", "U2 D2 U3 D3", "U4 G1", "G2 G3", "G4")
 VMEM_BYTES = 50 * 1024 * 1024
 
 BF = jnp.bfloat16
@@ -45,17 +45,20 @@
     return jnp.where(here & (rows >= 0), rows // (NB * prow_count) * NB + rows % NB, -1)
 
 
-def fetch_kernel(where_ref, piv_ref, meta_ref, a_ref, index_ref, parts_ref, own_ref, send_ref, order, held, slab, picked, old, sems, panel_sems, top_sem):
+def fetch_kernel(where_ref, meta_ref, a_ref, index_ref, parts_ref, own_ref, send_ref, order, piv_ref, held, slab, picked, old, sems, panel_sems, top_sems):
     prow, core = where_ref[0], where_ref[2]
     prow_count = parts_ref.shape[0]
     slots = a_ref.shape[1] // NB
     chunk_top = SMALL // CHUNKS
     block_rows = a_ref.shape[0] // CHUNKS
     top_part, old_part = TOP // prow_count, NB // prow_count
-    old_copy = pltpu.make_async_copy(a_ref.at[pl.ds(0, NB), :], old, top_sem)
+    piv_copy = pltpu.make_async_copy(meta_ref.at[pl.ds(0, 2), :], piv_ref, top_sems.at[0])
+    old_copy = pltpu.make_async_copy(a_ref.at[pl.ds(0, NB), :], old, top_sems.at[1])
+    piv_copy.start()
     old_copy.start()
+    at = lax.broadcasted_iota(jnp.int32, (2, NB), 0) * NB + lax.broadcasted_iota(jnp.int32, (2, NB), 1)
     places = [
-        jnp.sum(jnp.where(meta_ref[2:4, :] == k, meta_ref[4:6, :], 0).astype(F32)).astype(jnp.int32) for k in range(2)
+        jnp.sum(jnp.where(meta_ref[2:4, :] == k, at, 0).astype(F32)).astype(jnp.int32) for k in range(2)
     ]
     panels = []
     for n, (out, panel) in enumerate(((own_ref, core), (send_ref, 1 - core))):
@@ -85,23 +88,24 @@
         return carry
 
     lax.fori_loop(0, TOP, init, 0, unroll=TOP)
-
-    def untouched(t, carry):
-        far = piv_ref[t]
+    piv_copy.wait()
+
+    def untouched(t):
+        far = piv_ref[t // NB, t % NB]
         order[far] = far
-        return carry
-
-    lax.fori_loop(0, TOP, untouched, 0, unroll=TOP)
-
-    def exchange(t, carry):
-        far = piv_ref[t]
+
+    for t in range(TOP):
+        untouched(t)
+
+    def exchange(t):
+        far = piv_ref[t // NB, t % NB]
         near_value = order[t]
         far_value = order[far]
         order[t] = far_value
         order[far] = near_value
-        return carry
-
-    lax.fori_loop(0, TOP, exchange, 0, unroll=TOP)
+
+    for t in range(TOP):
+        exchange(t)
 
     def collect(g, count):
         held[count] = g
@@ -124,12 +128,12 @@
     lax.fori_loop(0, count, begin, 0)
     picked[...] = jnp.zeros_like(picked)
 
-    def emit(t, carry):
-        far = piv_ref[t]
+    def emit(t):
+        far = piv_ref[t // NB, t % NB]
         index_ref[jnp.where(far >= TOP, order[far], TOP + NB)] = far
-        return carry
-
-    lax.fori_loop(0, TOP, emit, 0, unroll=TOP)
+
+    for t in range(TOP):
+        emit(t)
     line16 = lax.broadcasted_iota(jnp.int32, (16, a_ref.shape[1]), 0)
 
     def take(n, carry):
@@ -154,7 +158,7 @@
             near = picked[pl.ds(pl.multiple_of((1 - panel) * NB, NB), NB), pl.ds(start, NB)].astype(BF)
             far = old[:, pl.ds(start, NB)]
             zero = jnp.zeros_like(far)
-            small = jnp.concatenate([near, jnp.where(prow == 0, far, zero), jnp.where(prow == 1, far, zero)], axis=0)
+            small = jnp.concatenate([near, jnp.where(prow == 0, far, zero), jnp.where(prow == 1, far, zero), zero], axis=0)
             for copy in copies:
                 copy.wait()
             for j in range(CHUNKS):
@@ -180,21 +184,22 @@
             jax.ShapeDtypeStruct((CHUNKS, chunk, NB), BF),
             jax.ShapeDtypeStruct((CHUNKS, chunk, NB), BF),
         ),
-        in_specs=[smem, smem, vmem, hbm],
+        in_specs=[smem, vmem, hbm],
         out_specs=(smem, vmem, vmem, vmem),
         scratch_shapes=[
             pltpu.SMEM((rows_here * prow_count,), jnp.int32),
+            pltpu.SMEM((2, NB), jnp.int32),
             pltpu.SMEM((TOP + 1,), jnp.int32),
             pltpu.VMEM((TOP, 16, cols_here), BF),
             pltpu.VMEM((TOP, cols_here), F32),
             pltpu.VMEM((NB, cols_here), BF),
             pltpu.SemaphoreType.DMA((TOP,)),
             pltpu.SemaphoreType.DMA((2, CHUNKS)),
-            pltpu.SemaphoreType.DMA(()),
+            pltpu.SemaphoreType.DMA((2,)),
         ],
         compiler_params=pltpu.CompilerParams(vmem_limit_bytes=VMEM_BYTES),
         name="fetch",
-    )(where, meta, meta.reshape(-1, NB), matrix)
+    )(where, meta, matrix)
 
 
 def factor_kernel(prow_count, where_ref, index_vec, mine_ref, other_ref, lower_ref, upper_ref, out_ref, low_ref):
@@ -213,14 +218,17 @@
     top_mid = dot_left(lower_ref[0], near_top).astype(BF)
     low_ref[...] = dot_right(near_mid, upper_ref[0]).astype(BF)
     dest = local_row(jnp.concatenate([index_vec[0:1, :], index_vec[1:2, :]], axis=1), prow, prow_count)
-    for j in range(CHUNKS):
+    group = CHUNKS // PY
+    block_rows *= group
+    for j in range(PY):
         line = lax.broadcasted_iota(jnp.int32, (block_rows, TOP), 0) + j * block_rows
         hot = jnp.where(line == dest, 1.0, 0.0)
         kept = jnp.sum(hot, axis=1, keepdims=True) == 0.0
         hot = hot.astype(BF)
-        raw = [
-            jnp.where(kept, panel(k, j, slice(chunk_top, chunk)).astype(F32), dot(hot, far[k])) for k in range(2)
-        ]
+        raw = []
+        for k in range(2):
+            here = jnp.concatenate([panel(k, j * group + i, slice(chunk_top, chunk)) for i in range(group)], axis=0)
+            raw.append(jnp.where(kept, here.astype(F32), dot(hot, far[k])))
         first = dot_right(raw[0].astype(BF), upper_ref[0]).astype(BF)
         if j == 0:
             above = (lax.broadcasted_iota(jnp.int32, (block_rows, NB), 0) < NB) & (prow == 0)
@@ -344,8 +352,7 @@
 
 
 CORE_SWAP = [(i, i ^ 1) for i in range(PY * PX * CORES)]
-Y_GROUPS = [[(y * PX + x) * CORES + c for y in range(PY)] for x in range(PX) for c in range(CORES)]
-X_GROUPS = [[(y * PX + x) * CORES + c for x in range(PX)] for y in range(PY) for c in range(CORES)]
+CHIP_GROUPS = [[i * CORES + c for i in range(PY * PX)] for c in range(CORES)]
 
 
 def spread(x, axis, groups, count):
@@ -361,8 +368,7 @@
     where = jnp.stack([prow, pcol, core]).astype(jnp.int32)
     slots = matrix.shape[1] // NB
 
-    top = jnp.arange(TOP, dtype=jnp.int32)
-    meta = jnp.concatenate([pivots.reshape(-1), col_blocks, top, top])
+    meta = jnp.concatenate([pivots, col_blocks.reshape(-1, NB)], axis=0)
     index, parts, own, send = fetch(where, meta, matrix, prow_count)
     barrier = lax.optimization_barrier
     ups = [(i, (i + 1) % prow_count) for i in range(prow_count)]
@@ -372,7 +378,10 @@
         return lax.dynamic_index_in_dim(parts, (prow + offset) % prow_count, 0, keepdims=False)
 
     def go_up(x, step):
-        return lax.ppermute(x, "prow", ups) + part_at(4 - step)
+        x = lax.ppermute(x, "prow", ups)
+        if step == 1:
+            x, _ = barrier((x, panel))
+        return x + part_at(4 - step)
 
     def go_down(x, step):
         x = lax.ppermute(x, "prow", downs)
@@ -406,31 +415,25 @@
         state.update(then)
         return panel, extra
 
-    windows = PLAN.split("|")
     owner = lax.dynamic_index_in_dim(index[TOP:TOP + 2], core, 0, keepdims=False) // slots
-    chip_y, chip_x = owner // (CORES * PX), owner // CORES % PX
+    chip = owner // CORES
     chunk_top = SMALL // CHUNKS
-    ring(windows[0])
     panel = own + lax.ppermute(send, "pcol", CORE_SWAP)
-    panel = lax.all_to_all(panel, "pcol", 0, 0, axis_index_groups=Y_GROUPS)
-    ring(windows[1])
-    panel, (chip_y, chip_x) = fence(panel, (chip_y, chip_x))
-
-    panel = lax.dynamic_index_in_dim(panel, chip_y, 0, keepdims=False)
+    ring(PLAN[0])
+    panel = lax.all_to_all(panel, "pcol", 0, 0, axis_index_groups=CHIP_GROUPS)
+    ring(PLAN[1])
+    panel, chip = fence(panel, chip)
+
+    panel = lax.dynamic_index_in_dim(panel, chip, 0, keepdims=False)
     small = jnp.sum(spread(panel[:chunk_top], "prow", None, prow_count), axis=0, dtype=BF)
     panel = jnp.concatenate([small, panel[chunk_top:]], axis=0)
-    ring(windows[2])
+    ring(PLAN[2])
     panel, _ = fence(panel)
 
-    panel = spread(panel, "pcol", X_GROUPS, PX)
-    ring(windows[3])
-    panel, _ = fence(panel)
-
-    panel = lax.dynamic_index_in_dim(panel, chip_x, 0, keepdims=False)
-    mine = spread(panel, "pcol", Y_GROUPS, PY)
-    ring(windows[4])
+    mine = spread(panel, "pcol", CHIP_GROUPS, CHUNKS)
+    ring(PLAN[3])
     mine, _ = fence(mine)
-    ring(windows[5])
+    ring(PLAN[4])
     other = lax.ppermute(mine, "pcol", CORE_SWAP)
 
     left, low = factor(where, index, mine, other, lower_inv, upper_inv, prow_count)

time: 105 us -> 96.1 us (0.915)
  waiting for transfers between devices: 30.3 us -> 22.7 us
    all_to_all x3 -> x2, waiting for transfers between devices: 14.9 us -> 5.04 us  [spread(): return lax.all_to_all(x, axis, 0, 0, axis_index_groups=groups)]
    all_to_all x3 -> x2, starting transfers between devices: 13.2 us -> 9.66 us  [spread(): return lax.all_to_all(x, axis, 0, 0, axis_index_groups=groups)]
    all_to_all x1, starting transfers between devices: 4.31 us -> 6.77 us  [local(): panel = lax.all_to_all(panel, 'pcol', 0, 0, axis_index_groups=CHIP_GROUPS)]
    ppermute x4, waiting for transfers between devices: 6.07 us -> 8.12 us  [gather_step(): got[step] = lax.ppermute(got[step - 1], 'prow', ups)]
    all_to_all x1, waiting for transfers between devices: 1.28 us -> 3.18 us  [local(): panel = lax.all_to_all(panel, 'pcol', 0, 0, axis_index_groups=CHIP_GROUPS)]
    ppermute x4, waiting for transfers between devices: 6.05 us -> 4.25 us  [go_up(): x = lax.ppermute(x, 'prow', ups)]
    broadcast_in_dim x5 -> x3, local copies, waits for them, and re-layouts: 2.78 us -> 1.68 us  [spread(): x = jnp.broadcast_to(x[None], (count,) + x.shape)]
  transfers between devices with their start and end apart: 20 -> 19, of which waited for: 11 -> 10; matrix products, arithmetic and copies ran while one was open for 4% -> 5% of each run, Pallas kernels for 4% -> 4%
where the time goes in v3:
time: 96.1 us; the launch traced here: 95.6 us
  starting transfers between devices  42.6 us (44%)
  waiting for transfers between devices  22.7 us (24%)
  Pallas kernels  21 us (22%)
  other arithmetic  3.26 us (3%)
  between operations  3.09 us (3%)
  local copies, waits for them, and re-layouts  3.03 us (3%)
    all_to_all x2, starting transfers between devices, spread(): return lax.all_to_all(x, axis, 0, 0, axis_index_groups=groups)  9.66 us
    ppermute x3, starting transfers between devices, go_down(): x = lax.ppermute(x, 'prow', downs)  8.85 us
    pallas_call x1, Pallas kernels, fetch(): pl.pallas_call(fetch_kernel, out_shape=(jax.ShapeDtypeStruct((2 * TOP,),...  8.6 us
    pallas_call x1, Pallas kernels, update(): pl.pallas_call(lambda *refs: update_kernel(prow_count, *refs), out_shape=...  8.28 us
    ppermute x4, waiting for transfers between devices, gather_step(): got[step] = lax.ppermute(got[step - 1], 'prow', ups)  8.12 us
    ppermute x3, starting transfers between devices, gather_step(): lax.ppermute(got[(prow_count - step + 1) % prow_count], 'prow', downs)  8.08 us
    all_to_all x1, starting transfers between devices, local(): panel = lax.all_to_all(panel, 'pcol', 0, 0, axis_index_groups=CHIP_GROUPS)  6.77 us
    ppermute x1, starting transfers between devices, local(): other = lax.ppermute(mine, 'pcol', CORE_SWAP)  5.65 us
  transfers between devices with their start and end apart: 19, of which 10 were waited for; matrix products, arithmetic and copies ran while one was open for 5% of the time, Pallas kernels for 4%

profile of v3, /device:TPU:1, one launch (start us, length us, event | category | flops | bytes accessed | tf_op | source)
XLA Modules:
  0.0 95.6 jit_solution(8653763560505940039)
XLA Ops:
  0.0 0.7 pad_add_fusion.meta_ref
  0.7 0.1 pad_add_fusion.1.where_ref.refs_0_
  0.8 8.6 %fetch.1 = (s32[512]{0:T(512)S(1)}, bf16[8,64,1024]{2,1,0:T(8,128)(2,1)S(1)}, bf16[16,224,128]{2,1,0:T(8,128)(2,1)S(1)}, bf16[16,224,128]{2,1,0:T(8,128)(2,1)S(1)}) custom-call(s32[3]{0:T(128)S(1)} %pad_add_fusion.1.where_ref.refs_0_, s32[4,128]{1,0:T(4,128)S(1)} %pad_add_fusion.meta_ref, bf16[3072,1024]{1,0:T(8,128)(2,1)} %refs_15_.1), custom_call_target="tpu_custom_call" | custom-call | tf_op jit(solution)/shard_map/fetch/pallas_call | solution.py:179
  9.4 0.0 copy-start
  9.4 0.0 copy-start.1
  9.4 3.3 %collective-permute-start = (bf16[16,224,128]{2,1,0:T(8,128)(2,1)S(1)}, bf16[16,224,128]{2,1,0:T(8,128)(2,1)}, u32[]{:S(2)}, u32[]{:S(2)}) collective-permute-start(bf16[16,224,128]{2,1,0:T(8,128)(2,1)S(1)} %get-tuple-element.30), channel_id=1, source_target_pairs={{0,1},{1,0},{2,3},{3,2},{4,5},{5,4},{6,7},{7,6},{8,9},{9,8},{10,11... | collective-permute-start | bytes 2752520 | tf_op jit(solution)/shard_map/ppermute | solution.py:421
  12.7 0.7 dynamic-slice_bitcast_fusion
  13.4 0.0 collective-permute-start.4
  13.4 3.6 %collective-permute-start.1 = (bf16[64,1024]{1,0:T(8,128)(2,1)S(1)}, bf16[64,1024]{1,0:T(8,128)(2,1)S(1)}, u32[]{:S(2)}, u32[]{:S(2)}) collective-permute-start(bf16[64,1024]{1,0:T(8,128)(2,1)S(1)} %get-tuple-element.56), channel_id=1, source_target_pairs={{0,224},{32,0},{64,32},{96,64},{128,96},{160,128},{192,160},{224,1... | collective-permute-start | bytes 393224 | tf_op jit(solution)/shard_map/ppermute | solution.py:387
  17.0 0.0 collective-permute-done
  17.0 2.4 %add.109 = bf16[16,224,128]{2,1,0:T(8,128)(2,1)} add(bf16[16,224,128]{2,1,0:T(8,128)(2,1)S(1)} %get-tuple-element.29, bf16[16,224,128]{2,1,0:T(8,128)(2,1)} %collective-permute-done) | non-fusion elementwise | flops 458752 | bytes 2752512 | tf_op jit(solution)/shard_map/add | solution.py:421
  19.4 1.7 %collective-permute-done.4 = bf16[64,1024]{1,0:T(8,128)(2,1)S(1)} collective-permute-done((bf16[64,1024]{1,0:T(8,128)(2,1)}, bf16[64,1024]{1,0:T(8,128)(2,1)S(1)}, u32[]{:S(2)}, u32[]{:S(2)}) %collective-permute-start.4) | collective-permute-done | bytes 131104 | tf_op jit(solution)/shard_map/ppermute | solution.py:381
  21.1 0.1 collective-permute-start.5
  21.2 6.8 %all-to-all-start = ((bf16[16,224,128]{2,1,0:T(8,128)(2,1)}), bf16[16,224,128]{2,1,0:T(8,128)(2,1)S(1)}, u32[]{:S(2)}, u32[]{:S(2)}) async-start(bf16[16,224,128]{2,1,0:T(8,128)(2,1)} %add.109), calls=%async_computation | async-start | bytes 1835008 | tf_op jit(solution)/shard_map/all_to_all | solution.py:423
  28.0 0.0 collective-permute-done.1
  28.0 0.0 collective-permute-done.5
  28.0 0.1 collective-permute-start.6
  28.1 2.7 %collective-permute-start.2 = (bf16[64,1024]{1,0:T(8,128)(2,1)S(1)}, bf16[64,1024]{1,0:T(8,128)(2,1)S(1)}, u32[]{:S(2)}, u32[]{:S(2)}) collective-permute-start(bf16[64,1024]{1,0:T(8,128)(2,1)S(1)} %get-tuple-element.54), channel_id=1, source_target_pairs={{0,224},{32,0},{64,32},{96,64},{128,96},{160,128},{192,160},{224,1... | collective-permute-start | bytes 393224 | tf_op jit(solution)/shard_map/ppermute | solution.py:387
  30.8 2.6 %collective-permute-done.6 = bf16[64,1024]{1,0:T(8,128)(2,1)S(1)} collective-permute-done((bf16[64,1024]{1,0:T(8,128)(2,1)S(1)}, bf16[64,1024]{1,0:T(8,128)(2,1)S(1)}, u32[]{:S(2)}, u32[]{:S(2)}) %collective-permute-start.6) | collective-permute-done | bytes 131104 | tf_op jit(solution)/shard_map/ppermute | solution.py:381
  33.4 0.0 collective-permute-done.2
  33.5 2.5 %collective-permute-start.3 = (bf16[64,1024]{1,0:T(8,128)(2,1)S(1)}, bf16[64,1024]{1,0:T(8,128)(2,1)S(1)}, u32[]{:S(2)}, u32[]{:S(2)}) collective-permute-start(bf16[64,1024]{1,0:T(8,128)(2,1)S(1)} %get-tuple-element.52), channel_id=1, source_target_pairs={{0,224},{32,0},{64,32},{96,64},{128,96},{160,128},{192,160},{224,1... | collective-permute-start | bytes 393224 | tf_op jit(solution)/shard_map/ppermute | solution.py:387
  36.0 0.6 dynamic_slice.40
  39.4 0.0 collective-permute-done.3
  39.4 3.2 %all-to-all-done = bf16[16,224,128]{2,1,0:T(8,128)(2,1)S(1)} async-done(((bf16[16,224,128]{2,1,0:T(8,128)(2,1)}), bf16[16,224,128]{2,1,0:T(8,128)(2,1)S(1)}, u32[]{:S(2)}, u32[]{:S(2)}) %all-to-all-start) | async-done | bytes 917536 | tf_op jit(solution)/shard_map/all_to_all | solution.py:423
  42.6 0.0 collective-permute-start.7
  42.6 0.6 broadcast_in_dim.7
  43.2 5.0 %all-to-all-start.1 = ((bf16[8,32,128]{2,1,0:T(8,128)(2,1)}), bf16[8,32,128]{2,1,0:T(8,128)(2,1)S(1)}, u32[]{:S(2)}, u32[]{:S(2)}) async-start(bf16[8,32,128]{2,1,0:T(8,128)(2,1)} %broadcast_in_dim.7), calls=%async_computation.1 | async-start | bytes 131072 | tf_op jit(solution)/shard_map/all_to_all | solution.py:360
  48.3 2.7 %collective-permute-start.9 = (bf16[64,1024]{1,0:T(8,128)(2,1)S(1)}, bf16[64,1024]{1,0:T(8,128)(2,1)S(1)}, u32[]{:S(2)}, u32[]{:S(2)}) collective-permute-start(bf16[64,1024]{1,0:T(8,128)(2,1)S(1)} %fusion.refs_4_), channel_id=1, source_target_pairs={{0,224},{32,0},{64,32},{96,64},{128,96},{160,128},{192,160},{224,1... | collective-permute-start | bytes 393224 | tf_op jit(solution)/shard_map/ppermute | solution.py:395
  51.0 0.0 collective-permute-start.8
  51.0 4.5 %all-to-all-done.1 = bf16[8,32,128]{2,1,0:T(8,128)(2,1)S(1)} async-done(((bf16[8,32,128]{2,1,0:T(8,128)(2,1)}), bf16[8,32,128]{2,1,0:T(8,128)(2,1)S(1)}, u32[]{:S(2)}, u32[]{:S(2)}) %all-to-all-start.1) | async-done | bytes 65568 | tf_op jit(solution)/shard_map/all_to_all | solution.py:360
  55.5 0.0 collective-permute-done.9.refs_11_
  55.5 1.2 %collective-permute-done.8.refs_5_ = bf16[64,1024]{1,0:T(8,128)(2,1)S(1)} collective-permute-done((bf16[64,1024]{1,0:T(8,128)(2,1)S(1)}, bf16[64,1024]{1,0:T(8,128)(2,1)S(1)}, u32[]{:S(2)}, u32[]{:S(2)}) %collective-permute-start.8) | collective-permute-done | bytes 131104 | tf_op jit(solution)/shard_map/ppermute | solution.py:393
  56.7 1.0 %broadcast_in_dim.16 = bf16[16,224,128]{2,1,0:T(8,128)(2,1)} broadcast(bf16[224,128]{1,0:T(8,128)(2,1)S(1)} %pad_maximum_fusion), dimensions={1,2} | broadcast | bytes 974848 | tf_op jit(solution)/shard_map/broadcast_in_dim | solution.py:359
  57.7 4.6 %all-to-all-start.2 = ((bf16[16,224,128]{2,1,0:T(8,128)(2,1)}), bf16[16,224,128]{2,1,0:T(8,128)(2,1)S(1)}, u32[]{:S(2)}, u32[]{:S(2)}) async-start(bf16[16,224,128]{2,1,0:T(8,128)(2,1)} %broadcast_in_dim.16), calls=%async_computation.2 | async-start | bytes 1835008 | tf_op jit(solution)/shard_map/all_to_all | solution.py:360
  62.4 0.1 collective-permute-start.10
  62.5 2.7 %collective-permute-start.12 = (bf16[64,1024]{1,0:T(8,128)(2,1)S(1)}, bf16[64,1024]{1,0:T(8,128)(2,1)S(1)}, u32[]{:S(2)}, u32[]{:S(2)}) collective-permute-start(bf16[64,1024]{1,0:T(8,128)(2,1)S(1)} %collective-permute-done.9.refs_11_), channel_id=1, source_target_pairs={{0,224},{32,0},{64,32},{96,64},{128,96},{160,128},{192,160},{224,1... | collective-permute-start | bytes 393224 | tf_op jit(solution)/shard_map/ppermute | solution.py:395
  65.1 2.4 %collective-permute-done.10.refs_6_ = bf16[64,1024]{1,0:T(8,128)(2,1)S(1)} collective-permute-done((bf16[64,1024]{1,0:T(8,128)(2,1)S(1)}, bf16[64,1024]{1,0:T(8,128)(2,1)S(1)}, u32[]{:S(2)}, u32[]{:S(2)}) %collective-permute-start.10) | collective-permute-done | bytes 131104 | tf_op jit(solution)/shard_map/ppermute | solution.py:393
  67.5 0.0 collective-permute-start.11
  67.5 0.0 collective-permute-done.12.refs_10_
  67.5 2.7 %collective-permute-start.13 = (bf16[64,1024]{1,0:T(8,128)(2,1)S(1)}, bf16[64,1024]{1,0:T(8,128)(2,1)S(1)}, u32[]{:S(2)}, u32[]{:S(2)}) collective-permute-start(bf16[64,1024]{1,0:T(8,128)(2,1)S(1)} %collective-permute-done.12.refs_10_), channel_id=1, source_target_pairs={{0,224},{32,0},{64,32},{96,64},{128,96},{160,128},{192,160},{224,1... | collective-permute-start | bytes 393224 | tf_op jit(solution)/shard_map/ppermute | solution.py:395
  70.2 3.7 %collective-permute-done.11.refs_7_ = bf16[64,1024]{1,0:T(8,128)(2,1)S(1)} collective-permute-done((bf16[64,1024]{1,0:T(8,128)(2,1)S(1)}, bf16[64,1024]{1,0:T(8,128)(2,1)S(1)}, u32[]{:S(2)}, u32[]{:S(2)}) %collective-permute-start.11) | collective-permute-done | bytes 131104 | tf_op jit(solution)/shard_map/ppermute | solution.py:393
  73.9 0.0 collective-permute-done.13.refs_9_
  73.9 0.6 all-to-all-done.2.refs_2_
  74.5 5.7 %collective-permute-start.15 = (bf16[16,224,128]{2,1,0:T(8,128)(2,1)S(1)}, bf16[16,224,128]{2,1,0:T(8,128)(2,1)S(1)}, u32[]{:S(2)}, u32[]{:S(2)}) collective-permute-start(bf16[16,224,128]{2,1,0:T(8,128)(2,1)S(1)} %all-to-all-done.2.refs_2_), channel_id=1, source_target_pairs={{0,1},{1,0},{2,3},{3,2},{4,5},{5,4},{6,7},{7,6},{8,9},{9,8},{10,11... | collective-permute-start | bytes 2752520 | tf_op jit(solution)/shard_map/ppermute | solution.py:437
  80.1 2.1 %collective-permute-done.15.refs_3_ = bf16[16,224,128]{2,1,0:T(8,128)(2,1)S(1)} collective-permute-done((bf16[16,224,128]{2,1,0:T(8,128)(2,1)S(1)}, bf16[16,224,128]{2,1,0:T(8,128)(2,1)S(1)}, u32[]{:S(2)}, u32[]{:S(2)}) %collective-permute-start.15) | collective-permute-done | bytes 917536 | tf_op jit(solution)/shard_map/ppermute | solution.py:437
  82.2 4.1 %factor.1 = (bf16[3072,256]{1,0:T(8,128)(2,1)S(1)}, bf16[128,128]{1,0:T(8,128)(2,1)S(1)}) custom-call(s32[3]{0:T(128)S(1)} %pad_add_fusion.1.where_ref.refs_0_, s32[4,128]{1,0:T(4,128)S(1)} %bitcast.28, bf16[16,224,128]{2,1,0:T(8,128)(2,1)S(1)} %all-to-all-done.2.refs_2_, bf16[16,224,128]{2,1,0:T(8,128)(2,1)S(1)} %collective-permute-done.15.refs_3_, ...), custom_call_target="tpu_custom_call" | custom-call | tf_op jit(solution)/shard_map/factor/pallas_call | solution.py:249
  86.3 0.9 collective-permute-done.14.refs_8_
  87.2 8.3 %update.1 = bf16[3072,1024]{1,0:T(8,128)(2,1)} custom-call(s32[3]{0:T(128)S(1)} %pad_add_fusion.1.where_ref.refs_0_, s32[512]{0:T(512)S(1)} %get-tuple-element.28.refs_1_, s32[256]{0:T(256)S(1)} %copy-done.2, s32[4,128]{1,0:T(4,128)S(1)} %bitcast.29, bf16[64,1024]{1,0:T(8,128)(2,1)S(1)} %fusion.refs_4_, bf16[64,1024]{1,0:T(8,128)(2,1)S(1)} %collective-permute-done.8.refs_5_, ...), custom_call_target="tpu_custom_call" | custom-call | tf_op jit(solution)/shard_map/update/pallas_call | solution.py:336
  (15 shorter events, 0.2 us)
Async XLA Ops:
  9.4 72.8 %copy-start = (f32[2,128,128]{2,1,0:T(8,128)S(1)}, f32[2,128,128]{2,1,0:T(8,128)}, u32[]{:S(2)}) copy-start(f32[2,128,128]{2,1,0:T(8,128)} %refs_13_.1) | copy-start | bytes 393220
  9.4 72.8 %copy-start.1 = (f32[2,128,128]{2,1,0:T(8,128)S(1)}, f32[2,128,128]{2,1,0:T(8,128)}, u32[]{:S(2)}) copy-start(f32[2,128,128]{2,1,0:T(8,128)} %refs_5_.1) | copy-start | bytes 393220
  9.4 7.6 %collective-permute-start = (bf16[16,224,128]{2,1,0:T(8,128)(2,1)S(1)}, bf16[16,224,128]{2,1,0:T(8,128)(2,1)}, u32[]{:S(2)}, u32[]{:S(2)}) collective-permute-start(bf16[16,224,128]{2,1,0:T(8,128)(2,1)S(1)} %get-tuple-element.30), channel_id=1, source_target_pairs={{0,1},{1,0},{2,3},{3,2},{4,5},{5,4},{6,7},{7,6},{8,9},{9,8},{10,11... | collective-permute-start | bytes 2752520 | tf_op jit(solution)/shard_map/ppermute | solution.py:421
  13.4 7.6 %collective-permute-start.4 = (bf16[64,1024]{1,0:T(8,128)(2,1)}, bf16[64,1024]{1,0:T(8,128)(2,1)S(1)}, u32[]{:S(2)}, u32[]{:S(2)}) collective-permute-start(bf16[64,1024]{1,0:T(8,128)(2,1)} %get-tuple-element.55), channel_id=1, source_target_pairs={{0,32},{32,64},{64,96},{96,128},{128,160},{160,192},{192,224},{224... | collective-permute-start | bytes 393224 | tf_op jit(solution)/shard_map/ppermute | solution.py:381
  13.4 14.6 %collective-permute-start.1 = (bf16[64,1024]{1,0:T(8,128)(2,1)S(1)}, bf16[64,1024]{1,0:T(8,128)(2,1)S(1)}, u32[]{:S(2)}, u32[]{:S(2)}) collective-permute-start(bf16[64,1024]{1,0:T(8,128)(2,1)S(1)} %get-tuple-element.56), channel_id=1, source_target_pairs={{0,224},{32,0},{64,32},{96,64},{128,96},{160,128},{192,160},{224,1... | collective-permute-start | bytes 393224 | tf_op jit(solution)/shard_map/ppermute | solution.py:387
  17.0 70.2 %copy-start.2 = (s32[256]{0:T(256)S(1)}, s32[256]{0:T(256)}, u32[]{:S(2)}) copy-start(s32[256]{0:T(256)} %refs_2_.1) | copy-start | bytes 3076
  21.1 6.9 %collective-permute-start.5 = (bf16[64,1024]{1,0:T(8,128)(2,1)S(1)}, bf16[64,1024]{1,0:T(8,128)(2,1)S(1)}, u32[]{:S(2)}, u32[]{:S(2)}) collective-permute-start(bf16[64,1024]{1,0:T(8,128)(2,1)S(1)} %bitcast_add_fusion.3), channel_id=1, source_target_pairs={{0,32},{32,64},{64,96},{96,128},{128,160},{160,192},{192,224},{224... | collective-permute-start | bytes 393224 | tf_op jit(solution)/shard_map/ppermute | solution.py:381
  21.2 21.4 %all-to-all-start = ((bf16[16,224,128]{2,1,0:T(8,128)(2,1)}), bf16[16,224,128]{2,1,0:T(8,128)(2,1)S(1)}, u32[]{:S(2)}, u32[]{:S(2)}) async-start(bf16[16,224,128]{2,1,0:T(8,128)(2,1)} %add.109), calls=%async_computation | async-start | bytes 1835008 | tf_op jit(solution)/shard_map/all_to_all | solution.py:423
  28.0 5.4 %collective-permute-start.6 = (bf16[64,1024]{1,0:T(8,128)(2,1)S(1)}, bf16[64,1024]{1,0:T(8,128)(2,1)S(1)}, u32[]{:S(2)}, u32[]{:S(2)}) collective-permute-start(bf16[64,1024]{1,0:T(8,128)(2,1)S(1)} %get-tuple-element.53), channel_id=1, source_target_pairs={{0,32},{32,64},{64,96},{96,128},{128,160},{160,192},{192,224},{224... | collective-permute-start | bytes 393224 | tf_op jit(solution)/shard_map/ppermute | solution.py:381
  28.1 5.3 %collective-permute-start.2 = (bf16[64,1024]{1,0:T(8,128)(2,1)S(1)}, bf16[64,1024]{1,0:T(8,128)(2,1)S(1)}, u32[]{:S(2)}, u32[]{:S(2)}) collective-permute-start(bf16[64,1024]{1,0:T(8,128)(2,1)S(1)} %get-tuple-element.54), channel_id=1, source_target_pairs={{0,224},{32,0},{64,32},{96,64},{128,96},{160,128},{192,160},{224,1... | collective-permute-start | bytes 393224 | tf_op jit(solution)/shard_map/ppermute | solution.py:387
  33.5 5.9 %collective-permute-start.3 = (bf16[64,1024]{1,0:T(8,128)(2,1)S(1)}, bf16[64,1024]{1,0:T(8,128)(2,1)S(1)}, u32[]{:S(2)}, u32[]{:S(2)}) collective-permute-start(bf16[64,1024]{1,0:T(8,128)(2,1)S(1)} %get-tuple-element.52), channel_id=1, source_target_pairs={{0,224},{32,0},{64,32},{96,64},{128,96},{160,128},{192,160},{224,1... | collective-permute-start | bytes 393224 | tf_op jit(solution)/shard_map/ppermute | solution.py:387
  42.6 5.7 %collective-permute-start.7 = (bf16[64,1024]{1,0:T(8,128)(2,1)S(1)}, bf16[64,1024]{1,0:T(8,128)(2,1)S(1)}, u32[]{:S(2)}, u32[]{:S(2)}) collective-permute-start(bf16[64,1024]{1,0:T(8,128)(2,1)S(1)} %get-tuple-element.35), channel_id=1, source_target_pairs={{0,32},{32,64},{64,96},{96,128},{128,160},{160,192},{192,224},{224... | collective-permute-start | bytes 393224 | tf_op jit(solution)/shard_map/ppermute | solution.py:381
  43.2 12.3 %all-to-all-start.1 = ((bf16[8,32,128]{2,1,0:T(8,128)(2,1)}), bf16[8,32,128]{2,1,0:T(8,128)(2,1)S(1)}, u32[]{:S(2)}, u32[]{:S(2)}) async-start(bf16[8,32,128]{2,1,0:T(8,128)(2,1)} %broadcast_in_dim.7), calls=%async_computation.1 | async-start | bytes 131072 | tf_op jit(solution)/shard_map/all_to_all | solution.py:360
  48.3 7.2 %collective-permute-start.9 = (bf16[64,1024]{1,0:T(8,128)(2,1)S(1)}, bf16[64,1024]{1,0:T(8,128)(2,1)S(1)}, u32[]{:S(2)}, u32[]{:S(2)}) collective-permute-start(bf16[64,1024]{1,0:T(8,128)(2,1)S(1)} %fusion.refs_4_), channel_id=1, source_target_pairs={{0,224},{32,0},{64,32},{96,64},{128,96},{160,128},{192,160},{224,1... | collective-permute-start | bytes 393224 | tf_op jit(solution)/shard_map/ppermute | solution.py:395
  51.0 5.7 %collective-permute-start.8 = (bf16[64,1024]{1,0:T(8,128)(2,1)S(1)}, bf16[64,1024]{1,0:T(8,128)(2,1)S(1)}, u32[]{:S(2)}, u32[]{:S(2)}) collective-permute-start(bf16[64,1024]{1,0:T(8,128)(2,1)S(1)} %fusion.refs_4_), channel_id=1, source_target_pairs={{0,32},{32,64},{64,96},{96,128},{128,160},{160,192},{192,224},{224... | collective-permute-start | bytes 393224 | tf_op jit(solution)/shard_map/ppermute | solution.py:393
  57.7 16.7 %all-to-all-start.2 = ((bf16[16,224,128]{2,1,0:T(8,128)(2,1)}), bf16[16,224,128]{2,1,0:T(8,128)(2,1)S(1)}, u32[]{:S(2)}, u32[]{:S(2)}) async-start(bf16[16,224,128]{2,1,0:T(8,128)(2,1)} %broadcast_in_dim.16), calls=%async_computation.2 | async-start | bytes 1835008 | tf_op jit(solution)/shard_map/all_to_all | solution.py:360
  62.4 5.1 %collective-permute-start.10 = (bf16[64,1024]{1,0:T(8,128)(2,1)S(1)}, bf16[64,1024]{1,0:T(8,128)(2,1)S(1)}, u32[]{:S(2)}, u32[]{:S(2)}) collective-permute-start(bf16[64,1024]{1,0:T(8,128)(2,1)S(1)} %collective-permute-done.8.refs_5_), channel_id=1, source_target_pairs={{0,32},{32,64},{64,96},{96,128},{128,160},{160,192},{192,224},{224... | collective-permute-start | bytes 393224 | tf_op jit(solution)/shard_map/ppermute | solution.py:393
  62.5 5.0 %collective-permute-start.12 = (bf16[64,1024]{1,0:T(8,128)(2,1)S(1)}, bf16[64,1024]{1,0:T(8,128)(2,1)S(1)}, u32[]{:S(2)}, u32[]{:S(2)}) collective-permute-start(bf16[64,1024]{1,0:T(8,128)(2,1)S(1)} %collective-permute-done.9.refs_11_), channel_id=1, source_target_pairs={{0,224},{32,0},{64,32},{96,64},{128,96},{160,128},{192,160},{224,1... | collective-permute-start | bytes 393224 | tf_op jit(solution)/shard_map/ppermute | solution.py:395
  67.5 6.4 %collective-permute-start.11 = (bf16[64,1024]{1,0:T(8,128)(2,1)S(1)}, bf16[64,1024]{1,0:T(8,128)(2,1)S(1)}, u32[]{:S(2)}, u32[]{:S(2)}) collective-permute-start(bf16[64,1024]{1,0:T(8,128)(2,1)S(1)} %collective-permute-done.10.refs_6_), channel_id=1, source_target_pairs={{0,32},{32,64},{64,96},{96,128},{128,160},{160,192},{192,224},{224... | collective-permute-start | bytes 393224 | tf_op jit(solution)/shard_map/ppermute | solution.py:393
  67.5 6.4 %collective-permute-start.13 = (bf16[64,1024]{1,0:T(8,128)(2,1)S(1)}, bf16[64,1024]{1,0:T(8,128)(2,1)S(1)}, u32[]{:S(2)}, u32[]{:S(2)}) collective-permute-start(bf16[64,1024]{1,0:T(8,128)(2,1)S(1)} %collective-permute-done.12.refs_10_), channel_id=1, source_target_pairs={{0,224},{32,0},{64,32},{96,64},{128,96},{160,128},{192,160},{224,1... | collective-permute-start | bytes 393224 | tf_op jit(solution)/shard_map/ppermute | solution.py:395
  74.5 7.8 %collective-permute-start.15 = (bf16[16,224,128]{2,1,0:T(8,128)(2,1)S(1)}, bf16[16,224,128]{2,1,0:T(8,128)(2,1)S(1)}, u32[]{:S(2)}, u32[]{:S(2)}) collective-permute-start(bf16[16,224,128]{2,1,0:T(8,128)(2,1)S(1)} %all-to-all-done.2.refs_2_), channel_id=1, source_target_pairs={{0,1},{1,0},{2,3},{3,2},{4,5},{5,4},{6,7},{7,6},{8,9},{9,8},{10,11... | collective-permute-start | bytes 2752520 | tf_op jit(solution)/shard_map/ppermute | solution.py:437
  80.1 7.1 %collective-permute-start.14 = (bf16[64,1024]{1,0:T(8,128)(2,1)S(1)}, bf16[64,1024]{1,0:T(8,128)(2,1)S(1)}, u32[]{:S(2)}, u32[]{:S(2)}) collective-permute-start(bf16[64,1024]{1,0:T(8,128)(2,1)S(1)} %collective-permute-done.11.refs_7_), channel_id=1, source_target_pairs={{0,32},{32,64},{64,96},{96,128},{128,160},{160,192},{192,224},{224... | collective-permute-start | bytes 393224 | tf_op jit(solution)/shard_map/ppermute | solution.py:393

commit v4 on v3

--- a/solution.py
+++ b/solution.py
@@ -10,8 +10,8 @@
 PY, PX, CORES = 4, 4, 2
 CHUNKS = PY * PX
 SMALL = 4 * NB
-STEPS = 6
-PLAN = ("U1 D1", "U2 D2 U3 D3", "U4 G1", "G2 G3", "G4")
+STEPS = 4
+PLAN = ("D1 U1", "D2 U2 D3 U3", "U4 G1", "G2 G3", "G4")
 VMEM_BYTES = 50 * 1024 * 1024
 
 BF = jnp.bfloat16

time: 96.1 us -> 96 us (level)
  no operation moved by 1% of the time
where the time goes in v4:
time: 96 us; the launch traced here: 95.4 us
  starting transfers between devices  43 us (45%)
  waiting for transfers between devices  22.7 us (24%)
  Pallas kernels  20.4 us (21%)
  other arithmetic  3.26 us (3%)
  between operations  3.09 us (3%)
  local copies, waits for them, and re-layouts  3.03 us (3%)
    all_to_all x2, starting transfers between devices, spread(): return lax.all_to_all(x, axis, 0, 0, axis_index_groups=groups)  9.62 us
    ppermute x3, starting transfers between devices, go_down(): x = lax.ppermute(x, 'prow', downs)  9.11 us
    pallas_call x1, Pallas kernels, fetch(): pl.pallas_call(fetch_kernel, out_shape=(jax.ShapeDtypeStruct((2 * TOP,),...  8.33 us
    ppermute x4, waiting for transfers between devices, gather_step(): got[step] = lax.ppermute(got[step - 1], 'prow', ups)  8.12 us
    ppermute x3, starting transfers between devices, gather_step(): lax.ppermute(got[(prow_count - step + 1) % prow_count], 'prow', downs)  8.08 us
    pallas_call x1, Pallas kernels, update(): pl.pallas_call(lambda *refs: update_kernel(prow_count, *refs), out_shape=...  7.96 us
    all_to_all x1, starting transfers between devices, local(): panel = lax.all_to_all(panel, 'pcol', 0, 0, axis_index_groups=CHIP_GROUPS)  6.77 us
    ppermute x1, starting transfers between devices, local(): other = lax.ppermute(mine, 'pcol', CORE_SWAP)  5.65 us
  transfers between devices with their start and end apart: 19, of which 10 were waited for; matrix products, arithmetic and copies ran while one was open for 5% of the time, Pallas kernels for 4%

profile of v4, /device:TPU:1, one launch (start us, length us, event | category | flops | bytes accessed | tf_op | source)
XLA Modules:
  0.0 95.4 jit_solution(16427414690309093367)
XLA Ops:
  0.0 0.7 pad_add_fusion.meta_ref
  0.7 0.1 pad_add_fusion.1.where_ref.refs_0_
  0.8 8.3 %fetch.1 = (s32[512]{0:T(512)S(1)}, bf16[8,64,1024]{2,1,0:T(8,128)(2,1)S(1)}, bf16[16,224,128]{2,1,0:T(8,128)(2,1)S(1)}, bf16[16,224,128]{2,1,0:T(8,128)(2,1)S(1)}) custom-call(s32[3]{0:T(128)S(1)} %pad_add_fusion.1.where_ref.refs_0_, s32[4,128]{1,0:T(4,128)S(1)} %pad_add_fusion.meta_ref, bf16[3072,1024]{1,0:T(8,128)(2,1)} %refs_15_.1), custom_call_target="tpu_custom_call" | custom-call | tf_op jit(solution)/shard_map/fetch/pallas_call | solution.py:179
  9.1 0.0 copy-start
  9.1 0.0 copy-start.1
  9.1 3.3 %collective-permute-start = (bf16[16,224,128]{2,1,0:T(8,128)(2,1)S(1)}, bf16[16,224,128]{2,1,0:T(8,128)(2,1)}, u32[]{:S(2)}, u32[]{:S(2)}) collective-permute-start(bf16[16,224,128]{2,1,0:T(8,128)(2,1)S(1)} %get-tuple-element.30), channel_id=1, source_target_pairs={{0,1},{1,0},{2,3},{3,2},{4,5},{5,4},{6,7},{7,6},{8,9},{9,8},{10,11... | collective-permute-start | bytes 2752520 | tf_op jit(solution)/shard_map/ppermute | solution.py:421
  12.5 0.7 dynamic-slice_bitcast_fusion
  13.1 0.2 collective-permute-start.4
  13.3 3.9 %collective-permute-start.1 = (bf16[64,1024]{1,0:T(8,128)(2,1)S(1)}, bf16[64,1024]{1,0:T(8,128)(2,1)S(1)}, u32[]{:S(2)}, u32[]{:S(2)}) collective-permute-start(bf16[64,1024]{1,0:T(8,128)(2,1)S(1)} %get-tuple-element.56), channel_id=1, source_target_pairs={{0,224},{32,0},{64,32},{96,64},{128,96},{160,128},{192,160},{224,1... | collective-permute-start | bytes 393224 | tf_op jit(solution)/shard_map/ppermute | solution.py:387
  17.2 0.0 collective-permute-done
  17.2 2.4 %add.109 = bf16[16,224,128]{2,1,0:T(8,128)(2,1)} add(bf16[16,224,128]{2,1,0:T(8,128)(2,1)S(1)} %get-tuple-element.29, bf16[16,224,128]{2,1,0:T(8,128)(2,1)} %collective-permute-done) | non-fusion elementwise | flops 458752 | bytes 2752512 | tf_op jit(solution)/shard_map/add | solution.py:421
  19.5 1.7 %collective-permute-done.4 = bf16[64,1024]{1,0:T(8,128)(2,1)S(1)} collective-permute-done((bf16[64,1024]{1,0:T(8,128)(2,1)}, bf16[64,1024]{1,0:T(8,128)(2,1)S(1)}, u32[]{:S(2)}, u32[]{:S(2)}) %collective-permute-start.4) | collective-permute-done | bytes 131104 | tf_op jit(solution)/shard_map/ppermute | solution.py:381
  21.2 0.1 collective-permute-start.5
  21.3 6.8 %all-to-all-start = ((bf16[16,224,128]{2,1,0:T(8,128)(2,1)}), bf16[16,224,128]{2,1,0:T(8,128)(2,1)S(1)}, u32[]{:S(2)}, u32[]{:S(2)}) async-start(bf16[16,224,128]{2,1,0:T(8,128)(2,1)} %add.109), calls=%async_computation | async-start | bytes 1835008 | tf_op jit(solution)/shard_map/all_to_all | solution.py:423
  28.1 0.0 collective-permute-done.1
  28.1 0.0 collective-permute-done.5
  28.2 0.1 collective-permute-start.6
  28.3 2.7 %collective-permute-start.2 = (bf16[64,1024]{1,0:T(8,128)(2,1)S(1)}, bf16[64,1024]{1,0:T(8,128)(2,1)S(1)}, u32[]{:S(2)}, u32[]{:S(2)}) collective-permute-start(bf16[64,1024]{1,0:T(8,128)(2,1)S(1)} %get-tuple-element.54), channel_id=1, source_target_pairs={{0,224},{32,0},{64,32},{96,64},{128,96},{160,128},{192,160},{224,1... | collective-permute-start | bytes 393224 | tf_op jit(solution)/shard_map/ppermute | solution.py:387
  31.0 2.6 %collective-permute-done.6 = bf16[64,1024]{1,0:T(8,128)(2,1)S(1)} collective-permute-done((bf16[64,1024]{1,0:T(8,128)(2,1)S(1)}, bf16[64,1024]{1,0:T(8,128)(2,1)S(1)}, u32[]{:S(2)}, u32[]{:S(2)}) %collective-permute-start.6) | collective-permute-done | bytes 131104 | tf_op jit(solution)/shard_map/ppermute | solution.py:381
  33.6 2.5 %collective-permute-start.3 = (bf16[64,1024]{1,0:T(8,128)(2,1)S(1)}, bf16[64,1024]{1,0:T(8,128)(2,1)S(1)}, u32[]{:S(2)}, u32[]{:S(2)}) collective-permute-start(bf16[64,1024]{1,0:T(8,128)(2,1)S(1)} %get-tuple-element.52), channel_id=1, source_target_pairs={{0,224},{32,0},{64,32},{96,64},{128,96},{160,128},{192,160},{224,1... | collective-permute-start | bytes 393224 | tf_op jit(solution)/shard_map/ppermute | solution.py:387
  36.1 0.6 dynamic_slice.40
  39.5 0.0 collective-permute-done.3
  39.5 3.2 %all-to-all-done = bf16[16,224,128]{2,1,0:T(8,128)(2,1)S(1)} async-done(((bf16[16,224,128]{2,1,0:T(8,128)(2,1)}), bf16[16,224,128]{2,1,0:T(8,128)(2,1)S(1)}, u32[]{:S(2)}, u32[]{:S(2)}) %all-to-all-start) | async-done | bytes 917536 | tf_op jit(solution)/shard_map/all_to_all | solution.py:423
  42.7 0.0 collective-permute-start.7
  42.7 0.6 broadcast_in_dim.7
  43.4 5.0 %all-to-all-start.1 = ((bf16[8,32,128]{2,1,0:T(8,128)(2,1)}), bf16[8,32,128]{2,1,0:T(8,128)(2,1)S(1)}, u32[]{:S(2)}, u32[]{:S(2)}) async-start(bf16[8,32,128]{2,1,0:T(8,128)(2,1)} %broadcast_in_dim.7), calls=%async_computation.1 | async-start | bytes 131072 | tf_op jit(solution)/shard_map/all_to_all | solution.py:360
  48.3 0.0 collective-permute-done.7
  48.4 2.7 %collective-permute-start.9 = (bf16[64,1024]{1,0:T(8,128)(2,1)S(1)}, bf16[64,1024]{1,0:T(8,128)(2,1)S(1)}, u32[]{:S(2)}, u32[]{:S(2)}) collective-permute-start(bf16[64,1024]{1,0:T(8,128)(2,1)S(1)} %fusion.refs_4_), channel_id=1, source_target_pairs={{0,224},{32,0},{64,32},{96,64},{128,96},{160,128},{192,160},{224,1... | collective-permute-start | bytes 393224 | tf_op jit(solution)/shard_map/ppermute | solution.py:395
  51.1 0.0 collective-permute-start.8
  51.1 4.5 %all-to-all-done.1 = bf16[8,32,128]{2,1,0:T(8,128)(2,1)S(1)} async-done(((bf16[8,32,128]{2,1,0:T(8,128)(2,1)}), bf16[8,32,128]{2,1,0:T(8,128)(2,1)S(1)}, u32[]{:S(2)}, u32[]{:S(2)}) %all-to-all-start.1) | async-done | bytes 65568 | tf_op jit(solution)/shard_map/all_to_all | solution.py:360
  55.6 1.2 %collective-permute-done.8.refs_5_ = bf16[64,1024]{1,0:T(8,128)(2,1)S(1)} collective-permute-done((bf16[64,1024]{1,0:T(8,128)(2,1)S(1)}, bf16[64,1024]{1,0:T(8,128)(2,1)S(1)}, u32[]{:S(2)}, u32[]{:S(2)}) %collective-permute-start.8) | collective-permute-done | bytes 131104 | tf_op jit(solution)/shard_map/ppermute | solution.py:393
  56.8 1.0 %broadcast_in_dim.16 = bf16[16,224,128]{2,1,0:T(8,128)(2,1)} broadcast(bf16[224,128]{1,0:T(8,128)(2,1)S(1)} %pad_maximum_fusion), dimensions={1,2} | broadcast | bytes 974848 | tf_op jit(solution)/shard_map/broadcast_in_dim | solution.py:359
  57.8 4.6 %all-to-all-start.2 = ((bf16[16,224,128]{2,1,0:T(8,128)(2,1)}), bf16[16,224,128]{2,1,0:T(8,128)(2,1)S(1)}, u32[]{:S(2)}, u32[]{:S(2)}) async-start(bf16[16,224,128]{2,1,0:T(8,128)(2,1)} %broadcast_in_dim.16), calls=%async_computation.2 | async-start | bytes 1835008 | tf_op jit(solution)/shard_map/all_to_all | solution.py:360
  62.5 0.1 collective-permute-start.10
  62.6 2.7 %collective-permute-start.12 = (bf16[64,1024]{1,0:T(8,128)(2,1)S(1)}, bf16[64,1024]{1,0:T(8,128)(2,1)S(1)}, u32[]{:S(2)}, u32[]{:S(2)}) collective-permute-start(bf16[64,1024]{1,0:T(8,128)(2,1)S(1)} %collective-permute-done.9.refs_11_), channel_id=1, source_target_pairs={{0,224},{32,0},{64,32},{96,64},{128,96},{160,128},{192,160},{224,1... | collective-permute-start | bytes 393224 | tf_op jit(solution)/shard_map/ppermute | solution.py:395
  65.2 2.4 %collective-permute-done.10.refs_6_ = bf16[64,1024]{1,0:T(8,128)(2,1)S(1)} collective-permute-done((bf16[64,1024]{1,0:T(8,128)(2,1)S(1)}, bf16[64,1024]{1,0:T(8,128)(2,1)S(1)}, u32[]{:S(2)}, u32[]{:S(2)}) %collective-permute-start.10) | collective-permute-done | bytes 131104 | tf_op jit(solution)/shard_map/ppermute | solution.py:393
  67.6 0.0 collective-permute-start.11
  67.6 0.0 collective-permute-done.12.refs_10_
  67.6 2.7 %collective-permute-start.13 = (bf16[64,1024]{1,0:T(8,128)(2,1)S(1)}, bf16[64,1024]{1,0:T(8,128)(2,1)S(1)}, u32[]{:S(2)}, u32[]{:S(2)}) collective-permute-start(bf16[64,1024]{1,0:T(8,128)(2,1)S(1)} %collective-permute-done.12.refs_10_), channel_id=1, source_target_pairs={{0,224},{32,0},{64,32},{96,64},{128,96},{160,128},{192,160},{224,1... | collective-permute-start | bytes 393224 | tf_op jit(solution)/shard_map/ppermute | solution.py:395
  70.3 3.7 %collective-permute-done.11.refs_7_ = bf16[64,1024]{1,0:T(8,128)(2,1)S(1)} collective-permute-done((bf16[64,1024]{1,0:T(8,128)(2,1)S(1)}, bf16[64,1024]{1,0:T(8,128)(2,1)S(1)}, u32[]{:S(2)}, u32[]{:S(2)}) %collective-permute-start.11) | collective-permute-done | bytes 131104 | tf_op jit(solution)/shard_map/ppermute | solution.py:393
  74.0 0.0 collective-permute-done.13.refs_9_
  74.0 0.6 all-to-all-done.2.refs_2_
  74.6 5.7 %collective-permute-start.15 = (bf16[16,224,128]{2,1,0:T(8,128)(2,1)S(1)}, bf16[16,224,128]{2,1,0:T(8,128)(2,1)S(1)}, u32[]{:S(2)}, u32[]{:S(2)}) collective-permute-start(bf16[16,224,128]{2,1,0:T(8,128)(2,1)S(1)} %all-to-all-done.2.refs_2_), channel_id=1, source_target_pairs={{0,1},{1,0},{2,3},{3,2},{4,5},{5,4},{6,7},{7,6},{8,9},{9,8},{10,11... | collective-permute-start | bytes 2752520 | tf_op jit(solution)/shard_map/ppermute | solution.py:437
  80.2 0.0 collective-permute-start.14
  80.2 2.1 %collective-permute-done.15.refs_3_ = bf16[16,224,128]{2,1,0:T(8,128)(2,1)S(1)} collective-permute-done((bf16[16,224,128]{2,1,0:T(8,128)(2,1)S(1)}, bf16[16,224,128]{2,1,0:T(8,128)(2,1)S(1)}, u32[]{:S(2)}, u32[]{:S(2)}) %collective-permute-start.15) | collective-permute-done | bytes 917536 | tf_op jit(solution)/shard_map/ppermute | solution.py:437
  82.3 4.1 %factor.1 = (bf16[3072,256]{1,0:T(8,128)(2,1)S(1)}, bf16[128,128]{1,0:T(8,128)(2,1)S(1)}) custom-call(s32[3]{0:T(128)S(1)} %pad_add_fusion.1.where_ref.refs_0_, s32[4,128]{1,0:T(4,128)S(1)} %bitcast.28, bf16[16,224,128]{2,1,0:T(8,128)(2,1)S(1)} %all-to-all-done.2.refs_2_, bf16[16,224,128]{2,1,0:T(8,128)(2,1)S(1)} %collective-permute-done.15.refs_3_, ...), custom_call_target="tpu_custom_call" | custom-call | tf_op jit(solution)/shard_map/factor/pallas_call | solution.py:249
  86.4 0.9 collective-permute-done.14.refs_8_
  87.3 8.0 %update.1 = bf16[3072,1024]{1,0:T(8,128)(2,1)} custom-call(s32[3]{0:T(128)S(1)} %pad_add_fusion.1.where_ref.refs_0_, s32[512]{0:T(512)S(1)} %get-tuple-element.28.refs_1_, s32[256]{0:T(256)S(1)} %copy-done.2, s32[4,128]{1,0:T(4,128)S(1)} %bitcast.29, bf16[64,1024]{1,0:T(8,128)(2,1)S(1)} %fusion.refs_4_, bf16[64,1024]{1,0:T(8,128)(2,1)S(1)} %collective-permute-done.8.refs_5_, ...), custom_call_target="tpu_custom_call" | custom-call | tf_op jit(solution)/shard_map/update/pallas_call | solution.py:336
  (15 shorter events, 0.2 us)
Async XLA Ops:
  9.1 73.2 %copy-start = (f32[2,128,128]{2,1,0:T(8,128)S(1)}, f32[2,128,128]{2,1,0:T(8,128)}, u32[]{:S(2)}) copy-start(f32[2,128,128]{2,1,0:T(8,128)} %refs_13_.1) | copy-start | bytes 393220
  9.1 73.2 %copy-start.1 = (f32[2,128,128]{2,1,0:T(8,128)S(1)}, f32[2,128,128]{2,1,0:T(8,128)}, u32[]{:S(2)}) copy-start(f32[2,128,128]{2,1,0:T(8,128)} %refs_5_.1) | copy-start | bytes 393220
  9.1 8.0 %collective-permute-start = (bf16[16,224,128]{2,1,0:T(8,128)(2,1)S(1)}, bf16[16,224,128]{2,1,0:T(8,128)(2,1)}, u32[]{:S(2)}, u32[]{:S(2)}) collective-permute-start(bf16[16,224,128]{2,1,0:T(8,128)(2,1)S(1)} %get-tuple-element.30), channel_id=1, source_target_pairs={{0,1},{1,0},{2,3},{3,2},{4,5},{5,4},{6,7},{7,6},{8,9},{9,8},{10,11... | collective-permute-start | bytes 2752520 | tf_op jit(solution)/shard_map/ppermute | solution.py:421
  13.1 8.1 %collective-permute-start.4 = (bf16[64,1024]{1,0:T(8,128)(2,1)}, bf16[64,1024]{1,0:T(8,128)(2,1)S(1)}, u32[]{:S(2)}, u32[]{:S(2)}) collective-permute-start(bf16[64,1024]{1,0:T(8,128)(2,1)} %get-tuple-element.55), channel_id=1, source_target_pairs={{0,32},{32,64},{64,96},{96,128},{128,160},{160,192},{192,224},{224... | collective-permute-start | bytes 393224 | tf_op jit(solution)/shard_map/ppermute | solution.py:381
  13.3 14.8 %collective-permute-start.1 = (bf16[64,1024]{1,0:T(8,128)(2,1)S(1)}, bf16[64,1024]{1,0:T(8,128)(2,1)S(1)}, u32[]{:S(2)}, u32[]{:S(2)}) collective-permute-start(bf16[64,1024]{1,0:T(8,128)(2,1)S(1)} %get-tuple-element.56), channel_id=1, source_target_pairs={{0,224},{32,0},{64,32},{96,64},{128,96},{160,128},{192,160},{224,1... | collective-permute-start | bytes 393224 | tf_op jit(solution)/shard_map/ppermute | solution.py:387
  17.2 70.1 %copy-start.2 = (s32[256]{0:T(256)S(1)}, s32[256]{0:T(256)}, u32[]{:S(2)}) copy-start(s32[256]{0:T(256)} %refs_2_.1) | copy-start | bytes 3076
  21.2 6.9 %collective-permute-start.5 = (bf16[64,1024]{1,0:T(8,128)(2,1)S(1)}, bf16[64,1024]{1,0:T(8,128)(2,1)S(1)}, u32[]{:S(2)}, u32[]{:S(2)}) collective-permute-start(bf16[64,1024]{1,0:T(8,128)(2,1)S(1)} %bitcast_add_fusion.3), channel_id=1, source_target_pairs={{0,32},{32,64},{64,96},{96,128},{128,160},{160,192},{192,224},{224... | collective-permute-start | bytes 393224 | tf_op jit(solution)/shard_map/ppermute | solution.py:381
  21.3 21.4 %all-to-all-start = ((bf16[16,224,128]{2,1,0:T(8,128)(2,1)}), bf16[16,224,128]{2,1,0:T(8,128)(2,1)S(1)}, u32[]{:S(2)}, u32[]{:S(2)}) async-start(bf16[16,224,128]{2,1,0:T(8,128)(2,1)} %add.109), calls=%async_computation | async-start | bytes 1835008 | tf_op jit(solution)/shard_map/all_to_all | solution.py:423
  28.2 5.4 %collective-permute-start.6 = (bf16[64,1024]{1,0:T(8,128)(2,1)S(1)}, bf16[64,1024]{1,0:T(8,128)(2,1)S(1)}, u32[]{:S(2)}, u32[]{:S(2)}) collective-permute-start(bf16[64,1024]{1,0:T(8,128)(2,1)S(1)} %get-tuple-element.53), channel_id=1, source_target_pairs={{0,32},{32,64},{64,96},{96,128},{128,160},{160,192},{192,224},{224... | collective-permute-start | bytes 393224 | tf_op jit(solution)/shard_map/ppermute | solution.py:381
  28.3 5.3 %collective-permute-start.2 = (bf16[64,1024]{1,0:T(8,128)(2,1)S(1)}, bf16[64,1024]{1,0:T(8,128)(2,1)S(1)}, u32[]{:S(2)}, u32[]{:S(2)}) collective-permute-start(bf16[64,1024]{1,0:T(8,128)(2,1)S(1)} %get-tuple-element.54), channel_id=1, source_target_pairs={{0,224},{32,0},{64,32},{96,64},{128,96},{160,128},{192,160},{224,1... | collective-permute-start | bytes 393224 | tf_op jit(solution)/shard_map/ppermute | solution.py:387
  33.6 5.9 %collective-permute-start.3 = (bf16[64,1024]{1,0:T(8,128)(2,1)S(1)}, bf16[64,1024]{1,0:T(8,128)(2,1)S(1)}, u32[]{:S(2)}, u32[]{:S(2)}) collective-permute-start(bf16[64,1024]{1,0:T(8,128)(2,1)S(1)} %get-tuple-element.52), channel_id=1, source_target_pairs={{0,224},{32,0},{64,32},{96,64},{128,96},{160,128},{192,160},{224,1... | collective-permute-start | bytes 393224 | tf_op jit(solution)/shard_map/ppermute | solution.py:387
  42.7 5.6 %collective-permute-start.7 = (bf16[64,1024]{1,0:T(8,128)(2,1)S(1)}, bf16[64,1024]{1,0:T(8,128)(2,1)S(1)}, u32[]{:S(2)}, u32[]{:S(2)}) collective-permute-start(bf16[64,1024]{1,0:T(8,128)(2,1)S(1)} %get-tuple-element.35), channel_id=1, source_target_pairs={{0,32},{32,64},{64,96},{96,128},{128,160},{160,192},{192,224},{224... | collective-permute-start | bytes 393224 | tf_op jit(solution)/shard_map/ppermute | solution.py:381
  43.4 12.2 %all-to-all-start.1 = ((bf16[8,32,128]{2,1,0:T(8,128)(2,1)}), bf16[8,32,128]{2,1,0:T(8,128)(2,1)S(1)}, u32[]{:S(2)}, u32[]{:S(2)}) async-start(bf16[8,32,128]{2,1,0:T(8,128)(2,1)} %broadcast_in_dim.7), calls=%async_computation.1 | async-start | bytes 131072 | tf_op jit(solution)/shard_map/all_to_all | solution.py:360
  48.4 7.2 %collective-permute-start.9 = (bf16[64,1024]{1,0:T(8,128)(2,1)S(1)}, bf16[64,1024]{1,0:T(8,128)(2,1)S(1)}, u32[]{:S(2)}, u32[]{:S(2)}) collective-permute-start(bf16[64,1024]{1,0:T(8,128)(2,1)S(1)} %fusion.refs_4_), channel_id=1, source_target_pairs={{0,224},{32,0},{64,32},{96,64},{128,96},{160,128},{192,160},{224,1... | collective-permute-start | bytes 393224 | tf_op jit(solution)/shard_map/ppermute | solution.py:395
  51.1 5.7 %collective-permute-start.8 = (bf16[64,1024]{1,0:T(8,128)(2,1)S(1)}, bf16[64,1024]{1,0:T(8,128)(2,1)S(1)}, u32[]{:S(2)}, u32[]{:S(2)}) collective-permute-start(bf16[64,1024]{1,0:T(8,128)(2,1)S(1)} %fusion.refs_4_), channel_id=1, source_target_pairs={{0,32},{32,64},{64,96},{96,128},{128,160},{160,192},{192,224},{224... | collective-permute-start | bytes 393224 | tf_op jit(solution)/shard_map/ppermute | solution.py:393
  57.8 16.7 %all-to-all-start.2 = ((bf16[16,224,128]{2,1,0:T(8,128)(2,1)}), bf16[16,224,128]{2,1,0:T(8,128)(2,1)S(1)}, u32[]{:S(2)}, u32[]{:S(2)}) async-start(bf16[16,224,128]{2,1,0:T(8,128)(2,1)} %broadcast_in_dim.16), calls=%async_computation.2 | async-start | bytes 1835008 | tf_op jit(solution)/shard_map/all_to_all | solution.py:360
  62.5 5.1 %collective-permute-start.10 = (bf16[64,1024]{1,0:T(8,128)(2,1)S(1)}, bf16[64,1024]{1,0:T(8,128)(2,1)S(1)}, u32[]{:S(2)}, u32[]{:S(2)}) collective-permute-start(bf16[64,1024]{1,0:T(8,128)(2,1)S(1)} %collective-permute-done.8.refs_5_), channel_id=1, source_target_pairs={{0,32},{32,64},{64,96},{96,128},{128,160},{160,192},{192,224},{224... | collective-permute-start | bytes 393224 | tf_op jit(solution)/shard_map/ppermute | solution.py:393
  62.6 5.0 %collective-permute-start.12 = (bf16[64,1024]{1,0:T(8,128)(2,1)S(1)}, bf16[64,1024]{1,0:T(8,128)(2,1)S(1)}, u32[]{:S(2)}, u32[]{:S(2)}) collective-permute-start(bf16[64,1024]{1,0:T(8,128)(2,1)S(1)} %collective-permute-done.9.refs_11_), channel_id=1, source_target_pairs={{0,224},{32,0},{64,32},{96,64},{128,96},{160,128},{192,160},{224,1... | collective-permute-start | bytes 393224 | tf_op jit(solution)/shard_map/ppermute | solution.py:395
  67.6 6.4 %collective-permute-start.11 = (bf16[64,1024]{1,0:T(8,128)(2,1)S(1)}, bf16[64,1024]{1,0:T(8,128)(2,1)S(1)}, u32[]{:S(2)}, u32[]{:S(2)}) collective-permute-start(bf16[64,1024]{1,0:T(8,128)(2,1)S(1)} %collective-permute-done.10.refs_6_), channel_id=1, source_target_pairs={{0,32},{32,64},{64,96},{96,128},{128,160},{160,192},{192,224},{224... | collective-permute-start | bytes 393224 | tf_op jit(solution)/shard_map/ppermute | solution.py:393
  67.6 6.4 %collective-permute-start.13 = (bf16[64,1024]{1,0:T(8,128)(2,1)S(1)}, bf16[64,1024]{1,0:T(8,128)(2,1)S(1)}, u32[]{:S(2)}, u32[]{:S(2)}) collective-permute-start(bf16[64,1024]{1,0:T(8,128)(2,1)S(1)} %collective-permute-done.12.refs_10_), channel_id=1, source_target_pairs={{0,224},{32,0},{64,32},{96,64},{128,96},{160,128},{192,160},{224,1... | collective-permute-start | bytes 393224 | tf_op jit(solution)/shard_map/ppermute | solution.py:395
  74.6 7.8 %collective-permute-start.15 = (bf16[16,224,128]{2,1,0:T(8,128)(2,1)S(1)}, bf16[16,224,128]{2,1,0:T(8,128)(2,1)S(1)}, u32[]{:S(2)}, u32[]{:S(2)}) collective-permute-start(bf16[16,224,128]{2,1,0:T(8,128)(2,1)S(1)} %all-to-all-done.2.refs_2_), channel_id=1, source_target_pairs={{0,1},{1,0},{2,3},{3,2},{4,5},{5,4},{6,7},{7,6},{8,9},{9,8},{10,11... | collective-permute-start | bytes 2752520 | tf_op jit(solution)/shard_map/ppermute | solution.py:437
  80.2 7.1 %collective-permute-start.14 = (bf16[64,1024]{1,0:T(8,128)(2,1)S(1)}, bf16[64,1024]{1,0:T(8,128)(2,1)S(1)}, u32[]{:S(2)}, u32[]{:S(2)}) collective-permute-start(bf16[64,1024]{1,0:T(8,128)(2,1)S(1)} %collective-permute-done.11.refs_7_), channel_id=1, source_target_pairs={{0,32},{32,64},{64,96},{96,128},{128,160},{160,192},{192,224},{224... | collective-permute-start | bytes 393224 | tf_op jit(solution)/shard_map/ppermute | solution.py:393

commit v5 on v4

--- a/solution.py
+++ b/solution.py
@@ -384,7 +384,7 @@
         return x + part_at(4 - step)
 
     def go_down(x, step):
-        x = lax.ppermute(x, "prow", downs)
+        x = lax.ppermute(barrier((x, panel))[0] if step == 1 else x, "prow", downs)
         return x + part_at(step - 3) if step < 3 else x
 
     got = {}

time: 96 us -> 95.9 us (level)
  waiting for transfers between devices: 22.7 us -> 24.6 us
  starting transfers between devices: 43 us -> 41.3 us
    ppermute x3, starting transfers between devices: 9.11 us -> 6.65 us  [go_down(): x = lax.ppermute(barrier((x, panel))[0] if step == 1 else x, 'prow', downs)]
    ppermute x1, waiting for transfers between devices: 0.01 us -> 2.1 us  [local(): panel = own + lax.ppermute(send, 'pcol', CORE_SWAP)]
    ppermute x4, waiting for transfers between devices: 8.12 us -> 6.59 us  [gather_step(): got[step] = lax.ppermute(got[step - 1], 'prow', ups)]
    ppermute x1, starting transfers between devices: 5.65 us -> 6.93 us  [local(): other = lax.ppermute(mine, 'pcol', CORE_SWAP)]
    ppermute x4, waiting for transfers between devices: 4.25 us -> 5.52 us  [go_up(): x = lax.ppermute(x, 'prow', ups)]
  transfers between devices with their start and end apart: 19 -> 19, of which waited for: 10 -> 11; matrix products, arithmetic and copies ran while one was open for 5% -> 4% of each run, Pallas kernels for 4% -> 4%
where the time goes in v5:
time: 95.9 us; the launch traced here: 95.2 us
  starting transfers between devices  41.3 us (43%)
  waiting for transfers between devices  24.6 us (26%)
  Pallas kernels  20.6 us (21%)
  other arithmetic  3.26 us (3%)
  between operations  3.1 us (3%)
  local copies, waits for them, and re-layouts  2.37 us (2%)
    all_to_all x2, starting transfers between devices, spread(): return lax.all_to_all(x, axis, 0, 0, axis_index_groups=groups)  8.77 us
    pallas_call x1, Pallas kernels, fetch(): pl.pallas_call(fetch_kernel, out_shape=(jax.ShapeDtypeStruct((2 * TOP,),...  8.59 us
    ppermute x3, starting transfers between devices, gather_step(): lax.ppermute(got[(prow_count - step + 1) % prow_count], 'prow', downs)  8.08 us
    pallas_call x1, Pallas kernels, update(): pl.pallas_call(lambda *refs: update_kernel(prow_count, *refs), out_shape=...  7.95 us
    ppermute x1, starting transfers between devices, local(): other = lax.ppermute(mine, 'pcol', CORE_SWAP)  6.93 us
    all_to_all x1, starting transfers between devices, local(): panel = lax.all_to_all(panel, 'pcol', 0, 0, axis_index_groups=CHIP_GROUPS)  6.75 us
    ppermute x3, starting transfers between devices, go_down(): x = lax.ppermute(barrier((x, panel))[0] if step == 1 else x, 'prow', downs)  6.65 us
    ppermute x4, waiting for transfers between devices, gather_step(): got[step] = lax.ppermute(got[step - 1], 'prow', ups)  6.59 us
  transfers between devices with their start and end apart: 19, of which 11 were waited for; matrix products, arithmetic and copies ran while one was open for 4% of the time, Pallas kernels for 4%

profile of v5, /device:TPU:1, one launch (start us, length us, event | category | flops | bytes accessed | tf_op | source)
XLA Modules:
  0.0 95.2 jit_solution(14868075209650514007)
XLA Ops:
  0.0 0.7 pad_add_fusion.meta_ref
  0.7 0.1 pad_add_fusion.1.where_ref.refs_0_
  0.8 8.6 %fetch.1 = (s32[512]{0:T(512)S(1)}, bf16[8,64,1024]{2,1,0:T(8,128)(2,1)S(1)}, bf16[16,224,128]{2,1,0:T(8,128)(2,1)S(1)}, bf16[16,224,128]{2,1,0:T(8,128)(2,1)S(1)}) custom-call(s32[3]{0:T(128)S(1)} %pad_add_fusion.1.where_ref.refs_0_, s32[4,128]{1,0:T(4,128)S(1)} %pad_add_fusion.meta_ref, bf16[3072,1024]{1,0:T(8,128)(2,1)} %refs_15_.1), custom_call_target="tpu_custom_call" | custom-call | tf_op jit(solution)/shard_map/fetch/pallas_call | solution.py:179
  9.4 0.0 copy-start
  9.4 0.0 copy-start.1
  9.4 3.2 %collective-permute-start = (bf16[16,224,128]{2,1,0:T(8,128)(2,1)S(1)}, bf16[16,224,128]{2,1,0:T(8,128)(2,1)}, u32[]{:S(2)}, u32[]{:S(2)}) collective-permute-start(bf16[16,224,128]{2,1,0:T(8,128)(2,1)S(1)} %get-tuple-element.31), channel_id=1, source_target_pairs={{0,1},{1,0},{2,3},{3,2},{4,5},{5,4},{6,7},{7,6},{8,9},{9,8},{10,11... | collective-permute-start | bytes 2752520 | tf_op jit(solution)/shard_map/ppermute | solution.py:421
  12.6 0.1 collective-permute-start.4
  12.7 2.1 %collective-permute-done = bf16[16,224,128]{2,1,0:T(8,128)(2,1)} collective-permute-done((bf16[16,224,128]{2,1,0:T(8,128)(2,1)S(1)}, bf16[16,224,128]{2,1,0:T(8,128)(2,1)}, u32[]{:S(2)}, u32[]{:S(2)}) %collective-permute-start) | collective-permute-done | bytes 917536 | tf_op jit(solution)/shard_map/ppermute | solution.py:421
  14.8 2.4 %add.109 = bf16[16,224,128]{2,1,0:T(8,128)(2,1)} add(bf16[16,224,128]{2,1,0:T(8,128)(2,1)S(1)} %get-tuple-element.30, bf16[16,224,128]{2,1,0:T(8,128)(2,1)} %collective-permute-done) | non-fusion elementwise | flops 458752 | bytes 2752512 | tf_op jit(solution)/shard_map/add | solution.py:421
  17.2 3.2 %collective-permute-done.4 = bf16[64,1024]{1,0:T(8,128)(2,1)S(1)} collective-permute-done((bf16[64,1024]{1,0:T(8,128)(2,1)S(1)}, bf16[64,1024]{1,0:T(8,128)(2,1)S(1)}, u32[]{:S(2)}, u32[]{:S(2)}) %collective-permute-start.4) | collective-permute-done | bytes 131104 | tf_op jit(solution)/shard_map/ppermute | solution.py:381
  20.3 1.3 %collective-permute-start.1 = (bf16[64,1024]{1,0:T(8,128)(2,1)S(1)}, bf16[64,1024]{1,0:T(8,128)(2,1)S(1)}, u32[]{:S(2)}, u32[]{:S(2)}) collective-permute-start(bf16[64,1024]{1,0:T(8,128)(2,1)S(1)} %get-tuple-element.33), channel_id=1, source_target_pairs={{0,224},{32,0},{64,32},{96,64},{128,96},{160,128},{192,160},{224,1... | collective-permute-start | bytes 393224 | tf_op jit(solution)/shard_map/ppermute | solution.py:387
  21.6 0.3 collective-permute-start.5
  21.9 6.8 %all-to-all-start = ((bf16[16,224,128]{2,1,0:T(8,128)(2,1)}), bf16[16,224,128]{2,1,0:T(8,128)(2,1)S(1)}, u32[]{:S(2)}, u32[]{:S(2)}) async-start(bf16[16,224,128]{2,1,0:T(8,128)(2,1)} %add.109), calls=%async_computation | async-start | bytes 1835008 | tf_op jit(solution)/shard_map/all_to_all | solution.py:423
  28.7 0.0 collective-permute-done.1
  28.7 0.0 collective-permute-done.5
  28.8 0.1 collective-permute-start.6
  28.9 2.7 %collective-permute-start.2 = (bf16[64,1024]{1,0:T(8,128)(2,1)S(1)}, bf16[64,1024]{1,0:T(8,128)(2,1)S(1)}, u32[]{:S(2)}, u32[]{:S(2)}) collective-permute-start(bf16[64,1024]{1,0:T(8,128)(2,1)S(1)} %get-tuple-element.56), channel_id=1, source_target_pairs={{0,224},{32,0},{64,32},{96,64},{128,96},{160,128},{192,160},{224,1... | collective-permute-start | bytes 393224 | tf_op jit(solution)/shard_map/ppermute | solution.py:387
  31.5 2.4 %collective-permute-done.6 = bf16[64,1024]{1,0:T(8,128)(2,1)S(1)} collective-permute-done((bf16[64,1024]{1,0:T(8,128)(2,1)S(1)}, bf16[64,1024]{1,0:T(8,128)(2,1)S(1)}, u32[]{:S(2)}, u32[]{:S(2)}) %collective-permute-start.6) | collective-permute-done | bytes 131104 | tf_op jit(solution)/shard_map/ppermute | solution.py:381
  33.9 0.0 collective-permute-done.2
  33.9 2.7 %collective-permute-start.3 = (bf16[64,1024]{1,0:T(8,128)(2,1)S(1)}, bf16[64,1024]{1,0:T(8,128)(2,1)S(1)}, u32[]{:S(2)}, u32[]{:S(2)}) collective-permute-start(bf16[64,1024]{1,0:T(8,128)(2,1)S(1)} %get-tuple-element.54), channel_id=1, source_target_pairs={{0,224},{32,0},{64,32},{96,64},{128,96},{160,128},{192,160},{224,1... | collective-permute-start | bytes 393224 | tf_op jit(solution)/shard_map/ppermute | solution.py:387
  36.7 0.6 dynamic_slice.40
  40.1 0.0 collective-permute-done.3
  40.1 2.7 %all-to-all-done = bf16[16,224,128]{2,1,0:T(8,128)(2,1)S(1)} async-done(((bf16[16,224,128]{2,1,0:T(8,128)(2,1)}), bf16[16,224,128]{2,1,0:T(8,128)(2,1)S(1)}, u32[]{:S(2)}, u32[]{:S(2)}) %all-to-all-start) | async-done | bytes 917536 | tf_op jit(solution)/shard_map/all_to_all | solution.py:423
  42.7 0.3 collective-permute-start.7
  43.0 0.6 broadcast_in_dim.7
  43.7 4.7 %all-to-all-start.1 = ((bf16[8,32,128]{2,1,0:T(8,128)(2,1)}), bf16[8,32,128]{2,1,0:T(8,128)(2,1)S(1)}, u32[]{:S(2)}, u32[]{:S(2)}) async-start(bf16[8,32,128]{2,1,0:T(8,128)(2,1)} %broadcast_in_dim.7), calls=%async_computation.1 | async-start | bytes 131072 | tf_op jit(solution)/shard_map/all_to_all | solution.py:360
  48.4 0.0 collective-permute-done.7
  48.4 2.7 %collective-permute-start.9 = (bf16[64,1024]{1,0:T(8,128)(2,1)S(1)}, bf16[64,1024]{1,0:T(8,128)(2,1)S(1)}, u32[]{:S(2)}, u32[]{:S(2)}) collective-permute-start(bf16[64,1024]{1,0:T(8,128)(2,1)S(1)} %fusion.refs_4_), channel_id=1, source_target_pairs={{0,224},{32,0},{64,32},{96,64},{128,96},{160,128},{192,160},{224,1... | collective-permute-start | bytes 393224 | tf_op jit(solution)/shard_map/ppermute | solution.py:395
  51.2 0.0 collective-permute-start.8
  51.2 4.6 %all-to-all-done.1 = bf16[8,32,128]{2,1,0:T(8,128)(2,1)S(1)} async-done(((bf16[8,32,128]{2,1,0:T(8,128)(2,1)}), bf16[8,32,128]{2,1,0:T(8,128)(2,1)S(1)}, u32[]{:S(2)}, u32[]{:S(2)}) %all-to-all-start.1) | async-done | bytes 65568 | tf_op jit(solution)/shard_map/all_to_all | solution.py:360
  55.8 0.0 collective-permute-done.9.refs_11_
  55.9 0.9 collective-permute-done.8.refs_5_
  56.8 1.0 %broadcast_in_dim.16 = bf16[16,224,128]{2,1,0:T(8,128)(2,1)} broadcast(bf16[224,128]{1,0:T(8,128)(2,1)S(1)} %pad_maximum_fusion), dimensions={1,2} | broadcast | bytes 974848 | tf_op jit(solution)/shard_map/broadcast_in_dim | solution.py:359
  57.8 4.0 %all-to-all-start.2 = ((bf16[16,224,128]{2,1,0:T(8,128)(2,1)}), bf16[16,224,128]{2,1,0:T(8,128)(2,1)S(1)}, u32[]{:S(2)}, u32[]{:S(2)}) async-start(bf16[16,224,128]{2,1,0:T(8,128)(2,1)} %broadcast_in_dim.16), calls=%async_computation.2 | async-start | bytes 1835008 | tf_op jit(solution)/shard_map/all_to_all | solution.py:360
  61.9 0.1 collective-permute-start.10
  62.0 2.7 %collective-permute-start.12 = (bf16[64,1024]{1,0:T(8,128)(2,1)S(1)}, bf16[64,1024]{1,0:T(8,128)(2,1)S(1)}, u32[]{:S(2)}, u32[]{:S(2)}) collective-permute-start(bf16[64,1024]{1,0:T(8,128)(2,1)S(1)} %collective-permute-done.9.refs_11_), channel_id=1, source_target_pairs={{0,224},{32,0},{64,32},{96,64},{128,96},{160,128},{192,160},{224,1... | collective-permute-start | bytes 393224 | tf_op jit(solution)/shard_map/ppermute | solution.py:395
  64.6 2.4 %collective-permute-done.10.refs_6_ = bf16[64,1024]{1,0:T(8,128)(2,1)S(1)} collective-permute-done((bf16[64,1024]{1,0:T(8,128)(2,1)S(1)}, bf16[64,1024]{1,0:T(8,128)(2,1)S(1)}, u32[]{:S(2)}, u32[]{:S(2)}) %collective-permute-start.10) | collective-permute-done | bytes 131104 | tf_op jit(solution)/shard_map/ppermute | solution.py:393
  67.0 0.0 collective-permute-start.11
  67.0 2.7 %collective-permute-start.13 = (bf16[64,1024]{1,0:T(8,128)(2,1)S(1)}, bf16[64,1024]{1,0:T(8,128)(2,1)S(1)}, u32[]{:S(2)}, u32[]{:S(2)}) collective-permute-start(bf16[64,1024]{1,0:T(8,128)(2,1)S(1)} %collective-permute-done.12.refs_10_), channel_id=1, source_target_pairs={{0,224},{32,0},{64,32},{96,64},{128,96},{160,128},{192,160},{224,1... | collective-permute-start | bytes 393224 | tf_op jit(solution)/shard_map/ppermute | solution.py:395
  69.7 2.8 %collective-permute-done.11.refs_7_ = bf16[64,1024]{1,0:T(8,128)(2,1)S(1)} collective-permute-done((bf16[64,1024]{1,0:T(8,128)(2,1)S(1)}, bf16[64,1024]{1,0:T(8,128)(2,1)S(1)}, u32[]{:S(2)}, u32[]{:S(2)}) %collective-permute-start.11) | collective-permute-done | bytes 131104 | tf_op jit(solution)/shard_map/ppermute | solution.py:393
  72.4 0.0 collective-permute-done.13.refs_9_
  72.4 0.9 all-to-all-done.2.refs_2_
  73.4 6.9 %collective-permute-start.15 = (bf16[16,224,128]{2,1,0:T(8,128)(2,1)S(1)}, bf16[16,224,128]{2,1,0:T(8,128)(2,1)S(1)}, u32[]{:S(2)}, u32[]{:S(2)}) collective-permute-start(bf16[16,224,128]{2,1,0:T(8,128)(2,1)S(1)} %all-to-all-done.2.refs_2_), channel_id=1, source_target_pairs={{0,1},{1,0},{2,3},{3,2},{4,5},{5,4},{6,7},{7,6},{8,9},{9,8},{10,11... | collective-permute-start | bytes 2752520 | tf_op jit(solution)/shard_map/ppermute | solution.py:437
  80.3 0.0 collective-permute-start.14
  80.3 2.1 %collective-permute-done.15.refs_3_ = bf16[16,224,128]{2,1,0:T(8,128)(2,1)S(1)} collective-permute-done((bf16[16,224,128]{2,1,0:T(8,128)(2,1)S(1)}, bf16[16,224,128]{2,1,0:T(8,128)(2,1)S(1)}, u32[]{:S(2)}, u32[]{:S(2)}) %collective-permute-start.15) | collective-permute-done | bytes 917536 | tf_op jit(solution)/shard_map/ppermute | solution.py:437
  82.4 4.1 %factor.1 = (bf16[3072,256]{1,0:T(8,128)(2,1)S(1)}, bf16[128,128]{1,0:T(8,128)(2,1)S(1)}) custom-call(s32[3]{0:T(128)S(1)} %pad_add_fusion.1.where_ref.refs_0_, s32[4,128]{1,0:T(4,128)S(1)} %bitcast.28, bf16[16,224,128]{2,1,0:T(8,128)(2,1)S(1)} %all-to-all-done.2.refs_2_, bf16[16,224,128]{2,1,0:T(8,128)(2,1)S(1)} %collective-permute-done.15.refs_3_, ...), custom_call_target="tpu_custom_call" | custom-call | tf_op jit(solution)/shard_map/factor/pallas_call | solution.py:249
  86.5 0.5 collective-permute-done.14.refs_8_
  87.1 8.0 %update.1 = bf16[3072,1024]{1,0:T(8,128)(2,1)} custom-call(s32[3]{0:T(128)S(1)} %pad_add_fusion.1.where_ref.refs_0_, s32[512]{0:T(512)S(1)} %get-tuple-element.29.refs_1_, s32[256]{0:T(256)S(1)} %copy-done.2, s32[4,128]{1,0:T(4,128)S(1)} %bitcast.29, bf16[64,1024]{1,0:T(8,128)(2,1)S(1)} %fusion.refs_4_, bf16[64,1024]{1,0:T(8,128)(2,1)S(1)} %collective-permute-done.8.refs_5_, ...), custom_call_target="tpu_custom_call" | custom-call | tf_op jit(solution)/shard_map/update/pallas_call | solution.py:336
  (15 shorter events, 0.2 us)
Async XLA Ops:
  9.4 73.0 %copy-start = (f32[2,128,128]{2,1,0:T(8,128)S(1)}, f32[2,128,128]{2,1,0:T(8,128)}, u32[]{:S(2)}) copy-start(f32[2,128,128]{2,1,0:T(8,128)} %refs_13_.1) | copy-start | bytes 393220
  9.4 73.0 %copy-start.1 = (f32[2,128,128]{2,1,0:T(8,128)S(1)}, f32[2,128,128]{2,1,0:T(8,128)}, u32[]{:S(2)}) copy-start(f32[2,128,128]{2,1,0:T(8,128)} %refs_5_.1) | copy-start | bytes 393220
  9.4 5.4 %collective-permute-start = (bf16[16,224,128]{2,1,0:T(8,128)(2,1)S(1)}, bf16[16,224,128]{2,1,0:T(8,128)(2,1)}, u32[]{:S(2)}, u32[]{:S(2)}) collective-permute-start(bf16[16,224,128]{2,1,0:T(8,128)(2,1)S(1)} %get-tuple-element.31), channel_id=1, source_target_pairs={{0,1},{1,0},{2,3},{3,2},{4,5},{5,4},{6,7},{7,6},{8,9},{9,8},{10,11... | collective-permute-start | bytes 2752520 | tf_op jit(solution)/shard_map/ppermute | solution.py:421
  12.6 7.7 %collective-permute-start.4 = (bf16[64,1024]{1,0:T(8,128)(2,1)S(1)}, bf16[64,1024]{1,0:T(8,128)(2,1)S(1)}, u32[]{:S(2)}, u32[]{:S(2)}) collective-permute-start(bf16[64,1024]{1,0:T(8,128)(2,1)S(1)} %get-tuple-element.57), channel_id=1, source_target_pairs={{0,32},{32,64},{64,96},{96,128},{128,160},{160,192},{192,224},{224... | collective-permute-start | bytes 393224 | tf_op jit(solution)/shard_map/ppermute | solution.py:381
  14.8 72.2 %copy-start.2 = (s32[256]{0:T(256)S(1)}, s32[256]{0:T(256)}, u32[]{:S(2)}) copy-start(s32[256]{0:T(256)} %refs_2_.1) | copy-start | bytes 3076
  20.3 8.4 %collective-permute-start.1 = (bf16[64,1024]{1,0:T(8,128)(2,1)S(1)}, bf16[64,1024]{1,0:T(8,128)(2,1)S(1)}, u32[]{:S(2)}, u32[]{:S(2)}) collective-permute-start(bf16[64,1024]{1,0:T(8,128)(2,1)S(1)} %get-tuple-element.33), channel_id=1, source_target_pairs={{0,224},{32,0},{64,32},{96,64},{128,96},{160,128},{192,160},{224,1... | collective-permute-start | bytes 393224 | tf_op jit(solution)/shard_map/ppermute | solution.py:387
  21.6 7.1 %collective-permute-start.5 = (bf16[64,1024]{1,0:T(8,128)(2,1)S(1)}, bf16[64,1024]{1,0:T(8,128)(2,1)S(1)}, u32[]{:S(2)}, u32[]{:S(2)}) collective-permute-start(bf16[64,1024]{1,0:T(8,128)(2,1)S(1)} %bitcast_add_fusion.3), channel_id=1, source_target_pairs={{0,32},{32,64},{64,96},{96,128},{128,160},{160,192},{192,224},{224... | collective-permute-start | bytes 393224 | tf_op jit(solution)/shard_map/ppermute | solution.py:381
  21.9 20.8 %all-to-all-start = ((bf16[16,224,128]{2,1,0:T(8,128)(2,1)}), bf16[16,224,128]{2,1,0:T(8,128)(2,1)S(1)}, u32[]{:S(2)}, u32[]{:S(2)}) async-start(bf16[16,224,128]{2,1,0:T(8,128)(2,1)} %add.109), calls=%async_computation | async-start | bytes 1835008 | tf_op jit(solution)/shard_map/all_to_all | solution.py:423
  28.8 5.1 %collective-permute-start.6 = (bf16[64,1024]{1,0:T(8,128)(2,1)S(1)}, bf16[64,1024]{1,0:T(8,128)(2,1)S(1)}, u32[]{:S(2)}, u32[]{:S(2)}) collective-permute-start(bf16[64,1024]{1,0:T(8,128)(2,1)S(1)} %get-tuple-element.55), channel_id=1, source_target_pairs={{0,32},{32,64},{64,96},{96,128},{128,160},{160,192},{192,224},{224... | collective-permute-start | bytes 393224 | tf_op jit(solution)/shard_map/ppermute | solution.py:381
  28.9 5.0 %collective-permute-start.2 = (bf16[64,1024]{1,0:T(8,128)(2,1)S(1)}, bf16[64,1024]{1,0:T(8,128)(2,1)S(1)}, u32[]{:S(2)}, u32[]{:S(2)}) collective-permute-start(bf16[64,1024]{1,0:T(8,128)(2,1)S(1)} %get-tuple-element.56), channel_id=1, source_target_pairs={{0,224},{32,0},{64,32},{96,64},{128,96},{160,128},{192,160},{224,1... | collective-permute-start | bytes 393224 | tf_op jit(solution)/shard_map/ppermute | solution.py:387
  33.9 6.1 %collective-permute-start.3 = (bf16[64,1024]{1,0:T(8,128)(2,1)S(1)}, bf16[64,1024]{1,0:T(8,128)(2,1)S(1)}, u32[]{:S(2)}, u32[]{:S(2)}) collective-permute-start(bf16[64,1024]{1,0:T(8,128)(2,1)S(1)} %get-tuple-element.54), channel_id=1, source_target_pairs={{0,224},{32,0},{64,32},{96,64},{128,96},{160,128},{192,160},{224,1... | collective-permute-start | bytes 393224 | tf_op jit(solution)/shard_map/ppermute | solution.py:387
  42.7 5.7 %collective-permute-start.7 = (bf16[64,1024]{1,0:T(8,128)(2,1)S(1)}, bf16[64,1024]{1,0:T(8,128)(2,1)S(1)}, u32[]{:S(2)}, u32[]{:S(2)}) collective-permute-start(bf16[64,1024]{1,0:T(8,128)(2,1)S(1)} %get-tuple-element.37), channel_id=1, source_target_pairs={{0,32},{32,64},{64,96},{96,128},{128,160},{160,192},{192,224},{224... | collective-permute-start | bytes 393224 | tf_op jit(solution)/shard_map/ppermute | solution.py:381
  43.7 12.1 %all-to-all-start.1 = ((bf16[8,32,128]{2,1,0:T(8,128)(2,1)}), bf16[8,32,128]{2,1,0:T(8,128)(2,1)S(1)}, u32[]{:S(2)}, u32[]{:S(2)}) async-start(bf16[8,32,128]{2,1,0:T(8,128)(2,1)} %broadcast_in_dim.7), calls=%async_computation.1 | async-start | bytes 131072 | tf_op jit(solution)/shard_map/all_to_all | solution.py:360
  48.4 7.4 %collective-permute-start.9 = (bf16[64,1024]{1,0:T(8,128)(2,1)S(1)}, bf16[64,1024]{1,0:T(8,128)(2,1)S(1)}, u32[]{:S(2)}, u32[]{:S(2)}) collective-permute-start(bf16[64,1024]{1,0:T(8,128)(2,1)S(1)} %fusion.refs_4_), channel_id=1, source_target_pairs={{0,224},{32,0},{64,32},{96,64},{128,96},{160,128},{192,160},{224,1... | collective-permute-start | bytes 393224 | tf_op jit(solution)/shard_map/ppermute | solution.py:395
  51.2 5.6 %collective-permute-start.8 = (bf16[64,1024]{1,0:T(8,128)(2,1)S(1)}, bf16[64,1024]{1,0:T(8,128)(2,1)S(1)}, u32[]{:S(2)}, u32[]{:S(2)}) collective-permute-start(bf16[64,1024]{1,0:T(8,128)(2,1)S(1)} %fusion.refs_4_), channel_id=1, source_target_pairs={{0,32},{32,64},{64,96},{96,128},{128,160},{160,192},{192,224},{224... | collective-permute-start | bytes 393224 | tf_op jit(solution)/shard_map/ppermute | solution.py:393
  57.8 15.5 %all-to-all-start.2 = ((bf16[16,224,128]{2,1,0:T(8,128)(2,1)}), bf16[16,224,128]{2,1,0:T(8,128)(2,1)S(1)}, u32[]{:S(2)}, u32[]{:S(2)}) async-start(bf16[16,224,128]{2,1,0:T(8,128)(2,1)} %broadcast_in_dim.16), calls=%async_computation.2 | async-start | bytes 1835008 | tf_op jit(solution)/shard_map/all_to_all | solution.py:360
  61.9 5.1 %collective-permute-start.10 = (bf16[64,1024]{1,0:T(8,128)(2,1)S(1)}, bf16[64,1024]{1,0:T(8,128)(2,1)S(1)}, u32[]{:S(2)}, u32[]{:S(2)}) collective-permute-start(bf16[64,1024]{1,0:T(8,128)(2,1)S(1)} %collective-permute-done.8.refs_5_), channel_id=1, source_target_pairs={{0,32},{32,64},{64,96},{96,128},{128,160},{160,192},{192,224},{224... | collective-permute-start | bytes 393224 | tf_op jit(solution)/shard_map/ppermute | solution.py:393
  62.0 5.0 %collective-permute-start.12 = (bf16[64,1024]{1,0:T(8,128)(2,1)S(1)}, bf16[64,1024]{1,0:T(8,128)(2,1)S(1)}, u32[]{:S(2)}, u32[]{:S(2)}) collective-permute-start(bf16[64,1024]{1,0:T(8,128)(2,1)S(1)} %collective-permute-done.9.refs_11_), channel_id=1, source_target_pairs={{0,224},{32,0},{64,32},{96,64},{128,96},{160,128},{192,160},{224,1... | collective-permute-start | bytes 393224 | tf_op jit(solution)/shard_map/ppermute | solution.py:395
  67.0 5.4 %collective-permute-start.11 = (bf16[64,1024]{1,0:T(8,128)(2,1)S(1)}, bf16[64,1024]{1,0:T(8,128)(2,1)S(1)}, u32[]{:S(2)}, u32[]{:S(2)}) collective-permute-start(bf16[64,1024]{1,0:T(8,128)(2,1)S(1)} %collective-permute-done.10.refs_6_), channel_id=1, source_target_pairs={{0,32},{32,64},{64,96},{96,128},{128,160},{160,192},{192,224},{224... | collective-permute-start | bytes 393224 | tf_op jit(solution)/shard_map/ppermute | solution.py:393
  67.0 5.4 %collective-permute-start.13 = (bf16[64,1024]{1,0:T(8,128)(2,1)S(1)}, bf16[64,1024]{1,0:T(8,128)(2,1)S(1)}, u32[]{:S(2)}, u32[]{:S(2)}) collective-permute-start(bf16[64,1024]{1,0:T(8,128)(2,1)S(1)} %collective-permute-done.12.refs_10_), channel_id=1, source_target_pairs={{0,224},{32,0},{64,32},{96,64},{128,96},{160,128},{192,160},{224,1... | collective-permute-start | bytes 393224 | tf_op jit(solution)/shard_map/ppermute | solution.py:395
  73.4 9.0 %collective-permute-start.15 = (bf16[16,224,128]{2,1,0:T(8,128)(2,1)S(1)}, bf16[16,224,128]{2,1,0:T(8,128)(2,1)S(1)}, u32[]{:S(2)}, u32[]{:S(2)}) collective-permute-start(bf16[16,224,128]{2,1,0:T(8,128)(2,1)S(1)} %all-to-all-done.2.refs_2_), channel_id=1, source_target_pairs={{0,1},{1,0},{2,3},{3,2},{4,5},{5,4},{6,7},{7,6},{8,9},{9,8},{10,11... | collective-permute-start | bytes 2752520 | tf_op jit(solution)/shard_map/ppermute | solution.py:437
  80.3 6.7 %collective-permute-start.14 = (bf16[64,1024]{1,0:T(8,128)(2,1)S(1)}, bf16[64,1024]{1,0:T(8,128)(2,1)S(1)}, u32[]{:S(2)}, u32[]{:S(2)}) collective-permute-start(bf16[64,1024]{1,0:T(8,128)(2,1)S(1)} %collective-permute-done.11.refs_7_), channel_id=1, source_target_pairs={{0,32},{32,64},{64,96},{96,128},{128,160},{160,192},{192,224},{224... | collective-permute-start | bytes 393224 | tf_op jit(solution)/shard_map/ppermute | solution.py:393
